TPU v7x, 32 devices: a whole 2x2x4 slice. The times are simulated.
32 devices in a mesh: row: 8 (over z, x), col: 4 (over y, core).
Axes of the slice: x: 2, y: 2, z: 4, core: 2. Of those that a mesh axis runs over, the one named last changes fastest.
Arguments:
- window: float32 [4096, 16384], P('row', 'col'), may hold values from -6 to 6
- leaf_vecs: float32 [2, 4096, 128], P(None, ('row', 'col')), may hold values from -0.25 to 0.25
- leaf_t: float32 [2, 1024, 128], P(None, 'row'), may hold values from -0.25 to 0.25
- node_vecs: float32 [2, 1024, 128], P(None, 'row'), may hold values from -0.5 to 0.5
- node_t: float32 [2, 1024, 128], P(None, 'row'), may hold values from -0.25 to 0.25
Outputs:
- updated: float32 [4096, 16384], P('row', 'col')
All inputs are finite; a program needn't handle non-finite values.
Results may differ from a plain program's by a relative error of at most 0.0002.
Values sent between devices are 32-bit elements; how exact they have to be, the bound alone decides.
No kernel may reach another device: no remote copies, remote signals or barrier semaphores. Data moves between devices by JAX's collectives and lax.ppermute only.
A program may use at most 64 MiB of HBM per device.

v0:
```python
import jax
import jax.numpy as jnp
from jax import lax
from jax.sharding import PartitionSpec as P


def partner(shard, axis, stride):
    return lax.ppermute(shard, axis, [(i, i ^ 1 << stride) for i in range(lax.axis_size(axis))])


def matmul(left, right):
    return jnp.dot(left, right, precision=lax.Precision.HIGHEST, preferred_element_type=jnp.float32)


def tree_pair(top_a, top_b, vfac, sfac):
    weight = matmul(sfac.T, top_a + matmul(vfac.T, top_b))
    return (top_a - weight, top_b - matmul(vfac, weight))


def local(window, leaf_vecs, leaf_t, node_vecs, node_t):
    width = leaf_t.shape[-1]
    panels = leaf_t.shape[0]
    levels = lax.axis_size("row").bit_length() - 1
    myself = lax.axis_index("row")
    work = window
    all_rows = lax.all_gather(leaf_vecs, "col", axis=1, tiled=True)
    for panel in range(panels):
        vecs = all_rows[panel]
        inner = matmul(leaf_t[panel].T, matmul(vecs.T, work))
        work = work - matmul(vecs, inner)
        top = work[:width]
        vfac = node_vecs[panel]
        sfac = node_t[panel]
        for level in range(levels):
            lower = myself // (1 << level) % 2 == 0
            got, got_v, got_s = partner((top, vfac, sfac), "row", level)
            part_a = jnp.where(lower, top, got)
            part_b = jnp.where(lower, got, top)
            use_v = jnp.where(lower, got_v, vfac)
            use_s = jnp.where(lower, got_s, sfac)
            new_a, new_b = tree_pair(part_a, part_b, use_v, use_s)
            top = jnp.where(lower, new_a, new_b)
        inner = matmul(sfac.T, matmul(vfac.T, top))
        top = jnp.where(myself == 0, top - matmul(vfac, inner), top)
        work = jnp.concatenate([top, work[width:]], axis=0)
    return work


def solution(mesh):
    placed = (
        P("row", "col"),
        P(None, ("row", "col"), None),
        P(None, "row", None),
        P(None, "row", None),
        P(None, "row", None),
    )
    return jax.shard_map(
        local, mesh=mesh, in_specs=placed, out_specs=P("row", "col"), check_vma=False
    )
```

profile of v0, /device:TPU:8, one launch (start us, length us, event | category | flops | bytes accessed | tf_op | source)
XLA Modules:
  0.0 508.0 jit_solution(11000862439724194769)
XLA Ops:
  0.0 7.5 %all_gather.3 = f32[2,512,128]{2,1,0:T(8,128)S(1)} all-gather(f32[2,128,128]{2,1,0:T(8,128)} %param.6), channel_id=1, replica_groups=mesh['row'=8,'col'=4] {'col'}, dimensions={1}, use_global_device_ids=true | all-gather | bytes 655360 | tf_op jit(solution)/shard_map/all_gather | solution.py:26
  7.5 7.5 %fusion.5 = f32[128,4096]{1,0:T(8,128)S(1)} fusion(f32[512,4096]{1,0:T(8,128)} %param.5, f32[2,512,128]{2,1,0:T(8,128)S(1)} %all_gather.3), kind=kOutput, calls=%fused_computation.43 | convolution fusion | flops 3221225472 | bytes 10747904 | tf_op jit(solution)/shard_map/dot_general | solution.py:12
  15.1 3.4 fusion.8
  18.6 7.0 %bitcast_subtract_fusion.1 = f32[512,4096]{1,0:T(8,128)S(1)} fusion(f32[512,4096]{1,0:T(8,128)S(1)} %bitcast.122, f32[4096,128]{1,0:T(8,128)S(1)} %fusion.8, f32[2,512,128]{2,1,0:T(8,128)S(1)} %all_gather.3), kind=kOutput, calls=%fused_computation.3 | convolution fusion | flops 3223322624 | bytes 19136512 | tf_op jit(solution)/shard_map/dot_general | solution.py:12
  25.6 0.0 copy-start
  25.6 3.4 copy-done
  29.0 1.5 slice.49
  30.5 1.5 collective-permute-start
  32.1 0.6 collective-permute-start.2
  32.7 1.6 collective-permute-start.1
  34.2 46.4 %collective-permute-done.2 = f32[128,128]{1,0:T(8,128)S(1)} collective-permute-done((f32[128,128]{1,0:T(8,128)S(1)}, f32[128,128]{1,0:T(8,128)S(1)}, u32[]{:S(2)}, u32[]{:S(2)}) %collective-permute-start.2) | collective-permute-done | bytes 65568 | tf_op jit(solution)/shard_map/ppermute | solution.py:8
  80.6 5.3 %convolution_add_fusion.5 = f32[128,4096]{1,0:T(8,128)S(1)} fusion(f32[128,4096]{1,0:T(8,128)S(1)} %collective-permute-done, pred[]{:T(512)S(6)} %eq.26, f32[128,128]{1,0:T(8,128)S(1)} %collective-permute-done.2, f32[2,128,128]{2,1,0:T(8,128)S(1)} %copy-done.4, f32[512,4096]{1,0:T(8,128)} %copy-done), kind=kOutput, calls=%fused_computation.22 | convolution fusion | flops 806895616 | bytes 10618368 | tf_op jit(solution)/shard_map/dot_general | solution.py:12
  85.9 2.0 fusion.21
  87.9 4.0 subtract_select_fusion.5
  91.9 0.5 collective-permute-start.3
  92.4 1.6 collective-permute-start.5
  94.0 0.4 collective-permute-start.4
  94.5 46.1 %collective-permute-done.5 = f32[128,128]{1,0:T(8,128)S(1)} collective-permute-done((f32[128,128]{1,0:T(8,128)S(1)}, f32[128,128]{1,0:T(8,128)S(1)}, u32[]{:S(2)}, u32[]{:S(2)}) %collective-permute-start.5) | collective-permute-done | bytes 65568 | tf_op jit(solution)/shard_map/ppermute | solution.py:8
  140.6 3.7 convolution_add_fusion.4
  144.3 1.9 fusion.19
  146.3 4.0 subtract_select_fusion.4
  150.3 2.7 collective-permute-start.6
  153.0 0.3 collective-permute-start.8
  153.3 2.6 collective-permute-start.7
  155.9 6.3 %slice.50 = f32[384,4096]{1,0:T(8,128)} slice(f32[512,4096]{1,0:T(8,128)} %copy-done), slice={[128:512], [0:4096]} | slice | bytes 12582912 | tf_op jit(solution)/shard_map/slice | solution.py:45
  162.2 83.1 %collective-permute-done.8 = f32[128,128]{1,0:T(8,128)S(1)} collective-permute-done((f32[128,128]{1,0:T(8,128)S(1)}, f32[128,128]{1,0:T(8,128)S(1)}, u32[]{:S(2)}, u32[]{:S(2)}) %collective-permute-start.8) | collective-permute-done | bytes 65568 | tf_op jit(solution)/shard_map/ppermute | solution.py:8
  245.3 4.3 convolution_add_fusion.3
  249.7 1.9 fusion.17
  251.6 4.0 subtract_select_fusion.3
  255.7 3.5 fusion.33
  259.2 1.9 fusion.31
  261.1 2.6 fusion.4
  263.7 14.3 %fusion = f32[4096,128]{1,0:T(8,128)S(1)} fusion(f32[384,4096]{1,0:T(8,128)S(1)} %bitcast.124, f32[128,4096]{1,0:T(8,128)S(1)} %fusion.4, f32[2,512,128]{2,1,0:T(8,128)S(1)} %all_gather.3), kind=kOutput, calls=%fused_computation.4 | convolution fusion | flops 3223322624 | bytes 10747904 | tf_op jit(solution)/shard_map/dot_general | solution.py:12
  278.0 1.8 fusion.6
  279.8 7.0 %bitcast_subtract_fusion = f32[512,4096]{1,0:T(8,128)S(1)} fusion(f32[384,4096]{1,0:T(8,128)S(1)} %bitcast.124, f32[128,4096]{1,0:T(8,128)S(1)} %fusion.4, f32[4096,128]{1,0:T(8,128)S(1)} %fusion.6, f32[2,512,128]{2,1,0:T(8,128)S(1)} %all_gather.3), kind=kOutput, calls=%fused_computation.2 | convolution fusion | flops 3225419776 | bytes 19136512 | tf_op jit(solution)/shard_map/dot_general | solution.py:12
  286.8 0.0 copy-start.1
  286.8 0.1 slice.52
  287.0 1.8 collective-permute-start.9
  288.8 0.5 collective-permute-start.11
  289.3 1.5 collective-permute-start.10
  290.8 45.0 %collective-permute-done.11 = f32[128,128]{1,0:T(8,128)S(1)} collective-permute-done((f32[128,128]{1,0:T(8,128)S(1)}, f32[128,128]{1,0:T(8,128)S(1)}, u32[]{:S(2)}, u32[]{:S(2)}) %collective-permute-start.11) | collective-permute-done | bytes 65568 | tf_op jit(solution)/shard_map/ppermute | solution.py:8
  335.8 2.2 convolution_add_fusion.2
  338.0 1.9 fusion.14
  340.0 2.4 subtract_select_fusion.2
  342.4 1.9 collective-permute-start.12
  344.3 0.2 collective-permute-start.14
  344.5 1.9 collective-permute-start.13
  346.3 43.2 %collective-permute-done.14 = f32[128,128]{1,0:T(8,128)S(1)} collective-permute-done((f32[128,128]{1,0:T(8,128)S(1)}, f32[128,128]{1,0:T(8,128)S(1)}, u32[]{:S(2)}, u32[]{:S(2)}) %collective-permute-start.14) | collective-permute-done | bytes 65568 | tf_op jit(solution)/shard_map/ppermute | solution.py:8
  389.6 2.2 convolution_add_fusion.1
  391.8 1.9 fusion.12
  393.7 2.8 subtract_select_fusion.1
  396.6 2.5 collective-permute-start.15
  399.1 0.4 collective-permute-start.17
  399.5 2.5 collective-permute-start.16
  402.0 87.0 %collective-permute-done.17 = f32[128,128]{1,0:T(8,128)S(1)} collective-permute-done((f32[128,128]{1,0:T(8,128)S(1)}, f32[128,128]{1,0:T(8,128)S(1)}, u32[]{:S(2)}, u32[]{:S(2)}) %collective-permute-start.17) | collective-permute-done | bytes 65568 | tf_op jit(solution)/shard_map/ppermute | solution.py:8
  489.0 2.2 convolution_add_fusion
  491.2 1.9 fusion.10
  493.2 2.5 subtract_select_fusion
  495.7 3.5 fusion.34
  499.2 1.8 fusion.32
  501.0 0.0 slice-start
  501.1 2.3 fusion.2
  503.4 0.4 slice-done
  503.8 3.9 pad_maximum_fusion.1
  (39 shorter events, 0.1 us)
Async XLA Ops:
  0.0 18.5 %slice-start.1 = ((s8[8388608]{0:T(1024)(128)(4,1)}), s8[4194304]{0:T(1024)(128)(4,1)S(1)}, s32[]{:S(2)}) async-start(s8[8388608]{0:T(1024)(128)(4,1)} %bitcast.121), calls=%async_computation.1 | async-start | bytes 8388608
  7.5 7.6 %copy-start.8 = (f32[2,128,128]{2,1,0:T(8,128)S(1)}, f32[2,128,128]{2,1,0:T(8,128)}, u32[]{:S(2)}) copy-start(f32[2,128,128]{2,1,0:T(8,128)} %param.7) | copy-start | bytes 393220
  7.5 11.0 %slice-start.2 = ((s8[8388608]{0:T(1024)(128)(4,1)}), s8[4194304]{0:T(1024)(128)(4,1)S(1)}, s32[]{:S(2)}) async-start(s8[8388608]{0:T(1024)(128)(4,1)} %bitcast.121), calls=%async_computation.2 | async-start | bytes 8388608
  25.6 3.4 copy-start
  29.0 3.0 copy-start.4
  29.0 3.6 copy-start.7
  30.5 50.1 %collective-permute-start = (f32[128,4096]{1,0:T(8,128)}, f32[128,4096]{1,0:T(8,128)S(1)}, u32[]{:S(2)}, u32[]{:S(2)}) collective-permute-start(f32[128,4096]{1,0:T(8,128)} %slice.49), channel_id=1, source_target_pairs={{0,4},{4,0},{8,12},{12,8},{16,20},{20,16},{24,28},{28,24},{1,5},{5... | collective-permute-start | bytes 6291464 | tf_op jit(solution)/shard_map/ppermute | solution.py:8
  32.1 48.6 %collective-permute-start.2 = (f32[128,128]{1,0:T(8,128)S(1)}, f32[128,128]{1,0:T(8,128)S(1)}, u32[]{:S(2)}, u32[]{:S(2)}) collective-permute-start(f32[128,128]{1,0:T(8,128)S(1)} %get-tuple-element.8), channel_id=1, source_target_pairs={{0,4},{4,0},{8,12},{12,8},{16,20},{20,16},{24,28},{28,24},{1,5},{5... | collective-permute-start | bytes 196616 | tf_op jit(solution)/shard_map/ppermute | solution.py:8
  32.7 53.2 %collective-permute-start.1 = (f32[128,128]{1,0:T(8,128)S(1)}, f32[128,128]{1,0:T(8,128)S(1)}, u32[]{:S(2)}, u32[]{:S(2)}) collective-permute-start(f32[128,128]{1,0:T(8,128)S(1)} %get-tuple-element.6), channel_id=1, source_target_pairs={{0,4},{4,0},{8,12},{12,8},{16,20},{20,16},{24,28},{28,24},{1,5},{5... | collective-permute-start | bytes 196616 | tf_op jit(solution)/shard_map/ppermute | solution.py:8
  80.6 5.3 %copy-start.5 = (f32[128,4096]{1,0:T(8,128)}, f32[128,4096]{1,0:T(8,128)S(1)}, u32[]{:S(2)}) copy-start(f32[128,4096]{1,0:T(8,128)S(1)} %collective-permute-done) | copy-start | bytes 6291460
  85.9 2.0 copy-start.6
  91.9 52.4 %copy-start.2 = (f32[128,4096]{1,0:T(8,128)}, f32[128,4096]{1,0:T(8,128)S(1)}, u32[]{:S(2)}) copy-start(f32[128,4096]{1,0:T(8,128)S(1)} %subtract_select_fusion.5) | copy-start | bytes 6291460
  91.9 48.7 %collective-permute-start.3 = (f32[128,4096]{1,0:T(8,128)S(1)}, f32[128,4096]{1,0:T(8,128)}, u32[]{:S(2)}, u32[]{:S(2)}) collective-permute-start(f32[128,4096]{1,0:T(8,128)S(1)} %subtract_select_fusion.5), channel_id=1, source_target_pairs={{0,8},{4,12},{8,0},{12,4},{16,24},{20,28},{24,16},{28,20},{1,9},{5... | collective-permute-start | bytes 6291464 | tf_op jit(solution)/shard_map/ppermute | solution.py:8
  92.4 48.2 %collective-permute-start.5 = (f32[128,128]{1,0:T(8,128)S(1)}, f32[128,128]{1,0:T(8,128)S(1)}, u32[]{:S(2)}, u32[]{:S(2)}) collective-permute-start(f32[128,128]{1,0:T(8,128)S(1)} %get-tuple-element.8), channel_id=1, source_target_pairs={{0,8},{4,12},{8,0},{12,4},{16,24},{20,28},{24,16},{28,20},{1,9},{5... | collective-permute-start | bytes 196616 | tf_op jit(solution)/shard_map/ppermute | solution.py:8
  94.0 50.3 %collective-permute-start.4 = (f32[128,128]{1,0:T(8,128)S(1)}, f32[128,128]{1,0:T(8,128)S(1)}, u32[]{:S(2)}, u32[]{:S(2)}) collective-permute-start(f32[128,128]{1,0:T(8,128)S(1)} %get-tuple-element.6), channel_id=1, source_target_pairs={{0,8},{4,12},{8,0},{12,4},{16,24},{20,28},{24,16},{28,20},{1,9},{5... | collective-permute-start | bytes 196616 | tf_op jit(solution)/shard_map/ppermute | solution.py:8
  144.3 2.0 copy-start.3
  150.3 95.0 %collective-permute-start.6 = (f32[128,4096]{1,0:T(8,128)S(1)}, f32[128,4096]{1,0:T(8,128)}, u32[]{:S(2)}, u32[]{:S(2)}) collective-permute-start(f32[128,4096]{1,0:T(8,128)S(1)} %subtract_select_fusion.4), channel_id=1, source_target_pairs={{0,16},{4,20},{8,24},{12,28},{16,0},{20,4},{24,8},{28,12},{1,17},{... | collective-permute-start | bytes 6291464 | tf_op jit(solution)/shard_map/ppermute | solution.py:8
  153.0 92.3 %collective-permute-start.8 = (f32[128,128]{1,0:T(8,128)S(1)}, f32[128,128]{1,0:T(8,128)S(1)}, u32[]{:S(2)}, u32[]{:S(2)}) collective-permute-start(f32[128,128]{1,0:T(8,128)S(1)} %get-tuple-element.8), channel_id=1, source_target_pairs={{0,16},{4,20},{8,24},{12,28},{16,0},{20,4},{24,8},{28,12},{1,17},{... | collective-permute-start | bytes 196616 | tf_op jit(solution)/shard_map/ppermute | solution.py:8
  153.3 96.3 %collective-permute-start.7 = (f32[128,128]{1,0:T(8,128)S(1)}, f32[128,128]{1,0:T(8,128)S(1)}, u32[]{:S(2)}, u32[]{:S(2)}) collective-permute-start(f32[128,128]{1,0:T(8,128)S(1)} %get-tuple-element.6), channel_id=1, source_target_pairs={{0,16},{4,20},{8,24},{12,28},{16,0},{20,4},{24,8},{28,12},{1,17},{... | collective-permute-start | bytes 196616 | tf_op jit(solution)/shard_map/ppermute | solution.py:8
  255.6 8.0 %slice-start.3 = ((s8[6291456]{0:T(1024)(128)(4,1)}), s8[4194304]{0:T(1024)(128)(4,1)S(1)}, s32[]{:S(2)}) async-start(s8[6291456]{0:T(1024)(128)(4,1)} %bitcast.123), calls=%async_computation.3 | async-start | bytes 8388608
  259.2 4.5 slice-start.4
  286.8 115.2 %copy-start.1 = (f32[512,4096]{1,0:T(8,128)}, f32[512,4096]{1,0:T(8,128)S(1)}, u32[]{:S(2)}) copy-start(f32[512,4096]{1,0:T(8,128)S(1)} %bitcast_subtract_fusion) | copy-start | bytes 25165828
  287.0 48.8 %collective-permute-start.9 = (f32[128,4096]{1,0:T(8,128)S(1)}, f32[128,4096]{1,0:T(8,128)S(1)}, u32[]{:S(2)}, u32[]{:S(2)}) collective-permute-start(f32[128,4096]{1,0:T(8,128)S(1)} %slice.52), channel_id=1, source_target_pairs={{0,4},{4,0},{8,12},{12,8},{16,20},{20,16},{24,28},{28,24},{1,5},{5... | collective-permute-start | bytes 6291464 | tf_op jit(solution)/shard_map/ppermute | solution.py:8
  288.8 47.0 %collective-permute-start.11 = (f32[128,128]{1,0:T(8,128)S(1)}, f32[128,128]{1,0:T(8,128)S(1)}, u32[]{:S(2)}, u32[]{:S(2)}) collective-permute-start(f32[128,128]{1,0:T(8,128)S(1)} %get-tuple-element.7), channel_id=1, source_target_pairs={{0,4},{4,0},{8,12},{12,8},{16,20},{20,16},{24,28},{28,24},{1,5},{5... | collective-permute-start | bytes 196616 | tf_op jit(solution)/shard_map/ppermute | solution.py:8
  289.3 48.7 %collective-permute-start.10 = (f32[128,128]{1,0:T(8,128)S(1)}, f32[128,128]{1,0:T(8,128)S(1)}, u32[]{:S(2)}, u32[]{:S(2)}) collective-permute-start(f32[128,128]{1,0:T(8,128)S(1)} %get-tuple-element.5), channel_id=1, source_target_pairs={{0,4},{4,0},{8,12},{12,8},{16,20},{20,16},{24,28},{28,24},{1,5},{5... | collective-permute-start | bytes 196616 | tf_op jit(solution)/shard_map/ppermute | solution.py:8
  342.4 47.2 %collective-permute-start.12 = (f32[128,4096]{1,0:T(8,128)S(1)}, f32[128,4096]{1,0:T(8,128)S(1)}, u32[]{:S(2)}, u32[]{:S(2)}) collective-permute-start(f32[128,4096]{1,0:T(8,128)S(1)} %subtract_select_fusion.2), channel_id=1, source_target_pairs={{0,8},{4,12},{8,0},{12,4},{16,24},{20,28},{24,16},{28,20},{1,9},{5... | collective-permute-start | bytes 6291464 | tf_op jit(solution)/shard_map/ppermute | solution.py:8
  344.3 45.3 %collective-permute-start.14 = (f32[128,128]{1,0:T(8,128)S(1)}, f32[128,128]{1,0:T(8,128)S(1)}, u32[]{:S(2)}, u32[]{:S(2)}) collective-permute-start(f32[128,128]{1,0:T(8,128)S(1)} %get-tuple-element.7), channel_id=1, source_target_pairs={{0,8},{4,12},{8,0},{12,4},{16,24},{20,28},{24,16},{28,20},{1,9},{5... | collective-permute-start | bytes 196616 | tf_op jit(solution)/shard_map/ppermute | solution.py:8
  344.5 47.3 %collective-permute-start.13 = (f32[128,128]{1,0:T(8,128)S(1)}, f32[128,128]{1,0:T(8,128)S(1)}, u32[]{:S(2)}, u32[]{:S(2)}) collective-permute-start(f32[128,128]{1,0:T(8,128)S(1)} %get-tuple-element.5), channel_id=1, source_target_pairs={{0,8},{4,12},{8,0},{12,4},{16,24},{20,28},{24,16},{28,20},{1,9},{5... | collective-permute-start | bytes 196616 | tf_op jit(solution)/shard_map/ppermute | solution.py:8
  396.6 92.5 %collective-permute-start.15 = (f32[128,4096]{1,0:T(8,128)S(1)}, f32[128,4096]{1,0:T(8,128)S(1)}, u32[]{:S(2)}, u32[]{:S(2)}) collective-permute-start(f32[128,4096]{1,0:T(8,128)S(1)} %subtract_select_fusion.1), channel_id=1, source_target_pairs={{0,16},{4,20},{8,24},{12,28},{16,0},{20,4},{24,8},{28,12},{1,17},{... | collective-permute-start | bytes 6291464 | tf_op jit(solution)/shard_map/ppermute | solution.py:8
  399.1 89.9 %collective-permute-start.17 = (f32[128,128]{1,0:T(8,128)S(1)}, f32[128,128]{1,0:T(8,128)S(1)}, u32[]{:S(2)}, u32[]{:S(2)}) collective-permute-start(f32[128,128]{1,0:T(8,128)S(1)} %get-tuple-element.7), channel_id=1, source_target_pairs={{0,16},{4,20},{8,24},{12,28},{16,0},{20,4},{24,8},{28,12},{1,17},{... | collective-permute-start | bytes 196616 | tf_op jit(solution)/shard_map/ppermute | solution.py:8
  399.5 91.7 %collective-permute-start.16 = (f32[128,128]{1,0:T(8,128)S(1)}, f32[128,128]{1,0:T(8,128)S(1)}, u32[]{:S(2)}, u32[]{:S(2)}) collective-permute-start(f32[128,128]{1,0:T(8,128)S(1)} %get-tuple-element.5), channel_id=1, source_target_pairs={{0,16},{4,20},{8,24},{12,28},{16,0},{20,4},{24,8},{28,12},{1,17},{... | collective-permute-start | bytes 196616 | tf_op jit(solution)/shard_map/ppermute | solution.py:8
  501.0 2.8 slice-start
where the time goes:
time: 514 us; the launch traced here: 508 us
  waiting for transfers between devices  351 us (68%)
  matrix products  108 us (21%)
  starting transfers between devices  25 us (5%)
  local copies, waits for them, and re-layouts  11.9 us (2%)
  blocking collectives  7.53 us (1%)
    ppermute x18, waiting for transfers between devices, partner(): lax.ppermute(shard, axis, [(i, i ^ 1 << stride) for i in range(lax.axis_s...  351 us
    dot_general x30, matrix products, matmul(): jnp.dot(left, right, precision=lax.Precision.HIGHEST, preferred_element_t...  108 us
    ppermute x18, starting transfers between devices, partner(): lax.ppermute(shard, axis, [(i, i ^ 1 << stride) for i in range(lax.axis_s...  25 us
  transfers between devices with their start and end apart: 18, of which 6 were waited for; matrix products, arithmetic and copies ran while one was open for 5% of the time, Pallas kernels for 0%

commit v1 on v0

v1 whole, which is shorter than its diff:
```python
import functools

import jax
import jax.numpy as jnp
from jax import lax
from jax.experimental import pallas as pl
from jax.experimental.pallas import tpu as pltpu
from jax.sharding import PartitionSpec as P

VMEM_LIMIT = 24 * 1024 * 1024
F32 = jnp.float32
BF16 = jnp.bfloat16


def mm(left, right):
    return jnp.dot(left, right, precision=lax.Precision.HIGHEST, preferred_element_type=F32)


def halves(value):
    high = value.astype(BF16)
    return high, (value - high.astype(F32)).astype(BF16)


def mm3(left, right):
    high, low = halves(right)

    def dot(a, b):
        return jnp.dot(a, b, preferred_element_type=F32)

    return dot(left[0], high) + (dot(left[0], low) + dot(left[1], high))


def params():
    return pltpu.CompilerParams(vmem_limit_bytes=VMEM_LIMIT)


def cost(flops, nbytes):
    return pl.CostEstimate(flops=int(flops), bytes_accessed=int(nbytes), transcendentals=0)


def prep_kernel(vecs_ref, leaf_ref, rows_ref, send_ref, rest_ref, dmat_ref):
    width = leaf_ref.shape[-1]

    def put(ref, place, value):
        high, low = halves(value)
        ref[(0, *place)] = high
        ref[(1, *place)] = low

    one, two = vecs_ref[0], vecs_ref[1]
    one_top, one_rest = one[:width], one[width:]
    two_top, two_rest = two[:width], two[width:]
    first, second = leaf_ref[0].T, leaf_ref[1].T
    two_rest_t, two_top_t = two_rest.T, two_top.T
    zero = jnp.zeros((width, width), F32)
    left, right, both = slice(0, width), slice(width, 2 * width), slice(None)
    cross = mm(two_rest_t, one_rest)
    lower = -mm(second, mm(cross, first))
    top_l, rest_l = mm(two_top, second), mm(two_rest, second)
    put(rows_ref, (left, both), one.T)
    put(rows_ref, (right, left), zero)
    put(rows_ref, (right, slice(width, None)), two_rest_t)
    put(send_ref, (left, left), -mm(one_top, first))
    put(send_ref, (left, right), zero)
    put(send_ref, (right, left), mm(two_top, lower))
    put(send_ref, (right, right), top_l)
    put(rest_ref, (both, left), mm(one_rest, first) + mm(two_rest, lower))
    put(rest_ref, (both, right), rest_l)
    put(rest_ref, (both, slice(2 * width, None)), mm(rest_l, two_top_t))
    shape = (width, width)
    eye = lax.broadcasted_iota(jnp.int32, shape, 0) == lax.broadcasted_iota(jnp.int32, shape, 1)
    dmat_ref[...] = eye.astype(F32) - mm(top_l, two_top_t)


def pack_kernel(place_ref, vecs_ref, t_ref, dmat_ref, after_ref, out_ref):
    share = out_ref.shape[1]
    part = pl.ds(pl.multiple_of(place_ref[1] * share, share), share)
    for panel in range(vecs_ref.shape[0]):
        out_ref[2 * panel] = vecs_ref[panel, part, :]
        out_ref[2 * panel + 1] = t_ref[panel, part, :]
    out_ref[2 * vecs_ref.shape[0]] = dmat_ref[part, :]


def leaf_kernel(place_ref, window_ref, rows_ref, send_ref, after_ref, inner_ref, *pieces):
    width = send_ref.shape[1] // 2
    inner = mm3((rows_ref[0], rows_ref[1]), window_ref[...])
    inner_ref[0] = inner
    message = mm3((send_ref[0], send_ref[1]), inner)
    top = message[:width] + window_ref[:width, :]
    for i, piece in enumerate(pieces):

        @pl.when(pl.program_id(0) == i)
        def _(piece=piece):
            piece[:width, :] = top
            piece[width:, :] = message[width:]


def nodes_kernel(place_ref, pack_ref, pair_ref, dmat_ref):
    width, cols = pack_ref.shape[-1], pack_ref.shape[1]
    col = place_ref[1]

    def whole(i):
        return jnp.concatenate([pack_ref[0, c ^ col, i] for c in range(cols)], axis=0)

    def put(panel, rows, columns, value):
        high, low = halves(value)
        pair_ref[0, panel, 0, rows, columns] = high
        pair_ref[1, panel, 0, rows, columns] = low

    top, low = slice(0, width), slice(width, 2 * width)
    panels = pair_ref.shape[1]
    for panel in range(panels):
        vfac = whole(2 * panel)
        sfac_t = whole(2 * panel + 1).T
        right = mm(sfac_t, vfac.T)
        put(panel, top, top, sfac_t)
        put(panel, top, low, right)
        put(panel, low, top, mm(vfac, sfac_t))
        put(panel, low, low, mm(vfac, right))
    dmat_ref[0, 0], dmat_ref[1, 0] = halves(whole(2 * panels))


def tree_kernel(rows, order, place_ref, pair_ref, dmat_ref, *refs):
    pieces, outs = [None] * rows, [None] * rows
    for i, k in enumerate(order):
        pieces[k] = refs[i]
        outs[k] = refs[rows + i]
    first, second = refs[2 * rows :]
    width = first.shape[1]
    me = place_ref[0]
    levels = rows.bit_length() - 1
    for k in range(rows):
        first[me ^ k] = pieces[k][:width, :]
        second[me ^ k] = pieces[k][width:, :]

    def each(count, body):
        if rows <= 8:
            for j in range(count):
                body(j, 0)
        else:
            lax.fori_loop(0, count, body, 0)

    def sweep(panel, tops):
        for level in range(levels):
            stride = 1 << level

            def pair(j, carry, level=level, stride=stride):
                a = (j >> level << (level + 1)) + (j & (stride - 1))
                b = a + stride
                top_a, top_b = tops[a], tops[b]
                both = jnp.concatenate([top_a, top_b], axis=0)
                change = mm3((pair_ref[0, panel, b], pair_ref[1, panel, b]), both)
                tops[a] = top_a - change[:width]
                tops[b] = top_b - change[width:]
                return carry

            each(rows // 2, pair)
        root = tops[0]
        low = slice(width, 2 * width)
        tops[0] = root - mm3((pair_ref[0, panel, 0, low, low], pair_ref[1, panel, 0, low, low]), root)

    def leaf(r, carry):
        second[r] = mm3((dmat_ref[0, r], dmat_ref[1, r]), first[r]) - second[r]
        return carry

    sweep(0, first)
    each(rows, leaf)
    sweep(1, second)
    for k in range(rows):
        outs[k][:width, :] = first[me ^ k]
        outs[k][width:, :] = second[me ^ k]


def last_kernel(count, place_ref, window_ref, inner_ref, rest_ref, *refs):
    pieces = refs[:count]
    out_ref, both = refs[-2], refs[-1]
    width = inner_ref.shape[1] // 2
    both[: 2 * width, :] = inner_ref[0]
    for i, piece in enumerate(pieces):

        @pl.when(pl.program_id(0) == i)
        def _(piece=piece):
            both[2 * width :, :] = piece[:width, :]
            out_ref[:width, :] = piece[width:, :]

    out_ref[width:, :] = window_ref[width:, :] - mm3((rest_ref[0], rest_ref[1]), both[...])


def vmem():
    return pl.BlockSpec(memory_space=pltpu.VMEM)


def anywhere():
    return pl.BlockSpec(memory_space=pl.ANY)


def smem():
    return pl.BlockSpec(memory_space=pltpu.SMEM)


def held(shape):
    return pl.BlockSpec(shape, lambda i, place: (0,) * len(shape))


def swap(value, axis, k):
    return lax.ppermute(value, axis, [(i, i ^ k) for i in range(lax.axis_size(axis))])


def local(window, leaf_vecs, leaf_t, node_vecs, node_t):
    rows, cols = lax.axis_size("row"), lax.axis_size("col")
    width = leaf_t.shape[-1]
    panels = leaf_t.shape[0]
    height, ncols = window.shape
    chunks = 2 if ncols % (2 * rows * 128) == 0 else 1
    span = ncols // chunks
    n = span // rows
    aligned = n % 128 == 0
    me = lax.axis_index("row").astype(jnp.int32)
    col = lax.axis_index("col").astype(jnp.int32)
    place = jnp.stack([me, col])

    vecs = lax.all_gather(leaf_vecs, "col", axis=1, tiled=True)
    rows_m, send_m, rest_m, dmat = pl.pallas_call(
        prep_kernel,
        out_shape=(
            jax.ShapeDtypeStruct((2, 2 * width, height), BF16),
            jax.ShapeDtypeStruct((2, 2 * width, 2 * width), BF16),
            jax.ShapeDtypeStruct((2, height - width, 3 * width), BF16),
            jax.ShapeDtypeStruct((width, width), F32),
        ),
        in_specs=[vmem(), vmem()],
        out_specs=(vmem(),) * 4,
        compiler_params=params(),
        cost_estimate=cost(40 * width**3 * 6, 2**21),
        name="prep",
    )(vecs, leaf_t)

    if aligned:
        source = window

        def columns(chunk, k0):
            return pl.BlockSpec((height, n), lambda i, place: (0, chunk * rows + (place[0] ^ (k0 + i))))

        out_shape = jax.ShapeDtypeStruct(window.shape, F32)
    else:
        source = jnp.stack([lax.dynamic_slice_in_dim(window, (me ^ k) * n, n, axis=1) for k in range(rows)])

        def columns(chunk, k0):
            return pl.BlockSpec((None, height, n), lambda i, place: (k0 + i, 0, 0))

        out_shape = jax.ShapeDtypeStruct(source.shape, F32)

    def leaf(chunk, k0, count, after):
        out = pl.pallas_call(
            leaf_kernel,
            grid_spec=pltpu.PrefetchScalarGridSpec(
                num_scalar_prefetch=1,
                grid=(count,),
                in_specs=[columns(chunk, k0), held(rows_m.shape), held(send_m.shape), anywhere()],
                out_specs=(pl.BlockSpec((1, 2 * width, n), lambda i, place: (i, 0, 0)),)
                + (held((2 * width, n)),) * count,
            ),
            out_shape=(jax.ShapeDtypeStruct((count, 2 * width, n), F32),)
            + (jax.ShapeDtypeStruct((2 * width, n), F32),) * count,
            compiler_params=params(),
            cost_estimate=cost(
                2 * 2 * width * (height + 2 * width) * n * count * 3, 4 * n * count * (height + 4 * width)
            ),
            name="leaf",
        )(place, source, rows_m, send_m, after)
        return out[0], list(out[1:])

    def tree(pieces):
        out = pl.pallas_call(
            functools.partial(tree_kernel, rows, order),
            out_shape=(jax.ShapeDtypeStruct((2 * width, n), F32),) * rows,
            in_specs=[smem()] + [vmem()] * (2 + rows),
            out_specs=(vmem(),) * rows,
            scratch_shapes=[pltpu.VMEM((rows, width, n), F32)] * 2,
            compiler_params=params(),
            cost_estimate=cost(rows * 8 * 4 * width * width * n * 3, 2**23),
            name="tree",
        )(place, pairs, dmats, *[pieces[k] for k in order])
        return [out[order.index(k)] for k in range(rows)]

    def last(chunk, k0, inner, pieces, out):
        count = len(pieces)
        in_specs = [
            columns(chunk, k0),
            pl.BlockSpec((1, 2 * width, n), lambda i, place: (i, 0, 0)),
            held(rest_m.shape),
        ] + [held((2 * width, n))] * count
        operands = [place, source, inner, rest_m, *pieces]
        aliases = {}
        if out is not None:
            in_specs.append(pl.BlockSpec(memory_space=pl.ANY))
            aliases = {len(operands): 0}
            operands.append(out)
        return pl.pallas_call(
            functools.partial(last_kernel, count),
            grid_spec=pltpu.PrefetchScalarGridSpec(
                num_scalar_prefetch=1,
                grid=(count,),
                in_specs=in_specs,
                out_specs=columns(chunk, k0),
                scratch_shapes=[pltpu.VMEM((3 * width, n), F32)],
            ),
            out_shape=out_shape,
            input_output_aliases=aliases,
            compiler_params=params(),
            cost_estimate=cost(
                2 * 3 * width * (height - width) * n * count * 3, 4 * n * count * (2 * height + 4 * width)
            ),
            name="last",
        )(*operands)

    half = rows // 2
    groups = [(half, rows - half), (0, half)]
    inners, sent, after = {}, [], send_m
    for chunk in range(chunks):
        made = [None] * rows
        for k0, count in groups:
            after, made[k0 : k0 + count] = leaf(chunk, k0, count, after)
            inners[chunk, k0] = after
        sent.append(made)
    order = [half + 0, half + 1]
    for k in range(1, half):
        order += [k] + ([half + 1 + k] if half + 1 + k < rows else [])
    order = order[:] + [0]

    def trade(pieces):
        got = list(pieces)
        for k in order[:-1]:
            got[k] = swap(pieces[k], "row", k)
        return got

    arrived = [trade(pieces) for pieces in sent]
    share = width // cols
    pack = pl.pallas_call(
        pack_kernel,
        out_shape=jax.ShapeDtypeStruct((2 * panels + 1, share, width), F32),
        in_specs=[smem(), vmem(), vmem(), vmem(), anywhere()],
        out_specs=vmem(),
        compiler_params=params(),
        cost_estimate=cost(0, 2**20),
        name="pack",
    )(place, node_vecs, node_t, dmat, arrived[0][order[0]])
    pack = pack[None]
    for k in [1 << bit for bit in reversed(range(rows.bit_length() - 1))]:
        pack = jnp.stack([pack, swap(pack, "row", k)], axis=1)
        pack = pack.reshape(-1, *pack.shape[2:])
    pack = pack[:, None]
    for k in [1 << bit for bit in reversed(range(cols.bit_length() - 1))]:
        pack = jnp.stack([pack, swap(pack, "col", k)], axis=2)
        pack = pack.reshape(rows, -1, *pack.shape[3:])
    pairs, dmats = pl.pallas_call(
        nodes_kernel,
        grid_spec=pltpu.PrefetchScalarGridSpec(
            num_scalar_prefetch=1,
            grid=(rows,),
            in_specs=[
                pl.BlockSpec((1, *pack.shape[1:]), lambda r, place: (r ^ place[0], 0, 0, 0, 0)),
            ],
            out_specs=(
                pl.BlockSpec((2, panels, 1, 2 * width, 2 * width), lambda r, place: (0, 0, r, 0, 0)),
                pl.BlockSpec((2, 1, width, width), lambda r, place: (0, r, 0, 0)),
            ),
        ),
        out_shape=(
            jax.ShapeDtypeStruct((2, panels, rows, 2 * width, 2 * width), BF16),
            jax.ShapeDtypeStruct((2, rows, width, width), BF16),
        ),
        compiler_params=params(),
        cost_estimate=cost(rows * 12 * width**3 * 6, 2**23),
        name="nodes",
    )(place, pack)

    returned = [trade(tree(pieces)) for pieces in arrived]
    out = None
    for chunk in range(chunks):
        for k0, count in reversed(groups):
            out = last(chunk, k0, inners[chunk, k0], returned[chunk][k0 : k0 + count], out)
    if aligned:
        return out
    result = jnp.zeros(window.shape, F32)
    for k in range(rows):
        result = lax.dynamic_update_slice_in_dim(result, out[k], (me ^ k) * n, axis=1)
    return result


def solution(mesh):
    placed = (
        P("row", "col"),
        P(None, ("row", "col"), None),
        P(None, "row", None),
        P(None, "row", None),
        P(None, "row", None),
    )
    return jax.shard_map(
        local, mesh=mesh, in_specs=placed, out_specs=P("row", "col"), check_vma=False
    )
```

time: 514 us -> 257 us (0.50); the launches traced: 508 us -> 257 us
  waiting for transfers between devices: 351 us -> 131 us
  matrix products: 108 us -> 0 us
  Pallas kernels: 0 us -> 50.9 us
  starting transfers between devices: 25 us -> 61.4 us
  local copies, waits for them, and re-layouts: 11.9 us -> 4.71 us
    ppermute x18 -> x33, waiting for transfers between devices: 351 us -> 131 us  [swap(): lax.ppermute(value, axis, [(i, i ^ k) for i in range(lax.axis_size(axis))])]
    dot_general x30 -> x0, matrix products: 108 us -> none  [matmul(): jnp.dot(left, right, precision=lax.Precision.HIGHEST, preferred_element_t...]
    pallas_call x0 -> x13, Pallas kernels: none -> 50.9 us  [the longest x4 16 us: leaf(): pl.pallas_call(leaf_kernel, grid_spec=pltpu.PrefetchScalarGridSpec(num_sc...]
    ppermute x18 -> x33, starting transfers between devices: 25 us -> 61.4 us  [swap(): lax.ppermute(value, axis, [(i, i ^ k) for i in range(lax.axis_size(axis))])]
    slice x5 -> x0, local copies, waits for them, and re-layouts: 8.42 us -> none  [the longest x3 6.77 us: local(): work = jnp.concatenate([top, work[width:]], axis=0)]
  transfers between devices with their start and end apart: 18 -> 33, of which waited for: 6 -> 19; matrix products, arithmetic and copies ran while one was open for 5% -> 0% of each run, Pallas kernels for 0% -> 16%
where the time goes in v1:
time: 257 us
  waiting for transfers between devices  131 us (51%)
  starting transfers between devices  61.4 us (24%)
  Pallas kernels  50.9 us (20%)
  blocking collectives  7.4 us (3%)
  local copies, waits for them, and re-layouts  4.71 us (2%)
    ppermute x33, waiting for transfers between devices, swap(): lax.ppermute(value, axis, [(i, i ^ k) for i in range(lax.axis_size(axis))])  131 us
    ppermute x33, starting transfers between devices, swap(): lax.ppermute(value, axis, [(i, i ^ k) for i in range(lax.axis_size(axis))])  61.4 us
    pallas_call x4, Pallas kernels, leaf(): pl.pallas_call(leaf_kernel, grid_spec=pltpu.PrefetchScalarGridSpec(num_sc...  16 us
    pallas_call x4, Pallas kernels, last(): pl.pallas_call(functools.partial(last_kernel, count), grid_spec=pltpu.Pre...  15.3 us
    pallas_call x2, Pallas kernels, tree(): pl.pallas_call(functools.partial(tree_kernel, rows, order), out_shape=(ja...  9.4 us
    pallas_call x1, Pallas kernels, local(): pl.pallas_call(nodes_kernel, grid_spec=pltpu.PrefetchScalarGridSpec(num_s...  7.82 us
    all_gather x1, blocking collectives, local(): vecs = lax.all_gather(leaf_vecs, 'col', axis=1, tiled=True)  7.4 us
  transfers between devices with their start and end apart: 33, of which 19 were waited for; matrix products, arithmetic and copies ran while one was open for 0% of the time, Pallas kernels for 16%

profile of v1, /device:TPU:8, one launch (start us, length us, event | category | flops | bytes accessed | tf_op | source)
XLA Modules:
  0.0 256.7 jit_solution(734802654794684838)
XLA Ops:
  0.0 7.4 %all_gather.3.vecs_ref = f32[2,512,128]{2,1,0:T(8,128)S(1)} all-gather(f32[2,128,128]{2,1,0:T(8,128)} %param.6), channel_id=1, replica_groups=mesh['row'=8,'col'=4] {'col'}, dimensions={1}, use_global_device_ids=true | all-gather | bytes 655360 | tf_op jit(solution)/shard_map/all_gather | solution.py:221
  7.4 0.1 pad_add_fusion.place_ref
  7.5 0.9 copy-done.3
  8.4 1.9 prep.1
  10.3 3.4 %copy-done = f32[512,4096]{1,0:T(8,128)S(1)} copy-done((f32[512,4096]{1,0:T(8,128)S(1)}, f32[512,4096]{1,0:T(8,128)}, u32[]{:S(2)}) %copy-start) | copy-done | bytes 8388632
  13.7 4.0 %leaf.4 = (f32[4,256,256]{2,1,0:T(8,128)S(1)}, f32[256,256]{1,0:T(8,128)S(1)}, f32[256,256]{1,0:T(8,128)S(1)}, f32[256,256]{1,0:T(8,128)S(1)}, f32[256,256]{1,0:T(8,128)S(1)}) custom-call(s32[2]{0:T(128)S(1)} %pad_add_fusion.place_ref, f32[512,4096]{1,0:T(8,128)S(1)} %copy-done, bf16[2,256,512]{2,1,0:T(8,128)(2,1)S(1)} %get-tuple-element.47.rows_ref, ...), custom_call_target="tpu_custom_call" | custom-call | flops 1207959552 | bytes 4194304 | tf_op jit(solution)/shard_map/leaf/pallas_call | solution.py:253
  17.7 2.7 %collective-permute-start = (f32[256,256]{1,0:T(8,128)S(1)}, f32[256,256]{1,0:T(8,128)S(1)}, u32[]{:S(2)}, u32[]{:S(2)}) collective-permute-start(f32[256,256]{1,0:T(8,128)S(1)} %get-tuple-element.54), channel_id=1, source_target_pairs={{0,16},{4,20},{8,24},{12,28},{16,0},{20,4},{24,8},{28,12},{1,17},{... | collective-permute-start | bytes 786440 | tf_op jit(solution)/shard_map/ppermute | solution.py:205
  20.3 11.6 %collective-permute-done.after_ref.refs_0_ = f32[256,256]{1,0:T(8,128)S(1)} collective-permute-done((f32[256,256]{1,0:T(8,128)S(1)}, f32[256,256]{1,0:T(8,128)S(1)}, u32[]{:S(2)}, u32[]{:S(2)}) %collective-permute-start) | collective-permute-done | bytes 262176 | tf_op jit(solution)/shard_map/ppermute | solution.py:205
  31.9 0.6 pack.1
  32.5 3.4 %collective-permute-start.1 = (f32[1,5,32,128]{3,2,1,0:T(8,128)S(1)}, f32[1,5,32,128]{3,2,1,0:T(8,128)S(1)}, u32[]{:S(2)}, u32[]{:S(2)}) collective-permute-start(f32[1,5,32,128]{3,2,1,0:T(8,128)S(1)} %bitcast.25), channel_id=1, source_target_pairs={{0,16},{4,20},{8,24},{12,28},{16,0},{20,4},{24,8},{28,12},{1,17},{... | collective-permute-start | bytes 245768 | tf_op jit(solution)/shard_map/ppermute | solution.py:205
  35.9 2.8 %collective-permute-done.1 = f32[1,5,32,128]{3,2,1,0:T(8,128)S(1)} collective-permute-done((f32[1,5,32,128]{3,2,1,0:T(8,128)S(1)}, f32[1,5,32,128]{3,2,1,0:T(8,128)S(1)}, u32[]{:S(2)}, u32[]{:S(2)}) %collective-permute-start.1) | collective-permute-done | bytes 81952 | tf_op jit(solution)/shard_map/ppermute | solution.py:205
  38.7 2.3 collective-permute-start.2
  41.0 3.3 %collective-permute-done.2 = f32[2,5,32,128]{3,2,1,0:T(8,128)S(1)} collective-permute-done((f32[2,5,32,128]{3,2,1,0:T(8,128)S(1)}, f32[2,5,32,128]{3,2,1,0:T(8,128)S(1)}, u32[]{:S(2)}, u32[]{:S(2)}) %collective-permute-start.2) | collective-permute-done | bytes 163872 | tf_op jit(solution)/shard_map/ppermute | solution.py:205
  44.4 1.6 collective-permute-start.3
  45.9 6.2 %collective-permute-done.3 = f32[4,5,32,128]{3,2,1,0:T(8,128)S(1)} collective-permute-done((f32[4,5,32,128]{3,2,1,0:T(8,128)S(1)}, f32[4,5,32,128]{3,2,1,0:T(8,128)S(1)}, u32[]{:S(2)}, u32[]{:S(2)}) %collective-permute-start.3) | collective-permute-done | bytes 327712 | tf_op jit(solution)/shard_map/ppermute | solution.py:205
  52.2 1.2 collective-permute-start.4
  53.4 12.7 %collective-permute-done.4 = f32[8,1,5,32,128]{4,3,2,0,1:T(8,128)S(1)} collective-permute-done((f32[8,1,5,32,128]{4,3,2,0,1:T(8,128)S(1)}, f32[8,1,5,32,128]{4,3,2,0,1:T(8,128)S(1)}, u32[]{:S(2)}, u32[]{:S(2)}) %collective-permute-start.4) | collective-permute-done | bytes 655392 | tf_op jit(solution)/shard_map/ppermute | solution.py:205
  66.1 0.3 fusion.1
  66.4 0.1 collective-permute-start.5
  66.5 2.7 %collective-permute-start.20 = (f32[256,256]{1,0:T(8,128)S(1)}, f32[256,256]{1,0:T(8,128)S(1)}, u32[]{:S(2)}, u32[]{:S(2)}) collective-permute-start(f32[256,256]{1,0:T(8,128)S(1)} %get-tuple-element.74), channel_id=1, source_target_pairs={{0,20},{4,16},{8,28},{12,24},{16,4},{20,0},{24,12},{28,8},{1,21},{... | collective-permute-start | bytes 786440 | tf_op jit(solution)/shard_map/ppermute | solution.py:205
  69.2 2.0 collective-permute-start.24
  71.2 4.0 %leaf.5 = (f32[4,256,256]{2,1,0:T(8,128)S(1)}, f32[256,256]{1,0:T(8,128)S(1)}, f32[256,256]{1,0:T(8,128)S(1)}, f32[256,256]{1,0:T(8,128)S(1)}, f32[256,256]{1,0:T(8,128)S(1)}) custom-call(s32[2]{0:T(128)S(1)} %pad_add_fusion.place_ref, f32[512,4096]{1,0:T(8,128)S(1)} %copy-done, bf16[2,256,512]{2,1,0:T(8,128)(2,1)S(1)} %get-tuple-element.47.rows_ref, ...), custom_call_target="tpu_custom_call" | custom-call | flops 1207959552 | bytes 4194304 | tf_op jit(solution)/shard_map/leaf/pallas_call | solution.py:253
  75.2 1.6 collective-permute-start.21
  76.8 4.0 %leaf.6 = (f32[4,256,256]{2,1,0:T(8,128)S(1)}, f32[256,256]{1,0:T(8,128)S(1)}, f32[256,256]{1,0:T(8,128)S(1)}, f32[256,256]{1,0:T(8,128)S(1)}, f32[256,256]{1,0:T(8,128)S(1)}) custom-call(s32[2]{0:T(128)S(1)} %pad_add_fusion.place_ref, f32[512,4096]{1,0:T(8,128)S(1)} %copy-done, bf16[2,256,512]{2,1,0:T(8,128)(2,1)S(1)} %get-tuple-element.47.rows_ref, ...), custom_call_target="tpu_custom_call" | custom-call | flops 1207959552 | bytes 4194304 | tf_op jit(solution)/shard_map/leaf/pallas_call | solution.py:253
  80.8 4.0 %leaf.7 = (f32[4,256,256]{2,1,0:T(8,128)S(1)}, f32[256,256]{1,0:T(8,128)S(1)}, f32[256,256]{1,0:T(8,128)S(1)}, f32[256,256]{1,0:T(8,128)S(1)}, f32[256,256]{1,0:T(8,128)S(1)}) custom-call(s32[2]{0:T(128)S(1)} %pad_add_fusion.place_ref, f32[512,4096]{1,0:T(8,128)S(1)} %copy-done, bf16[2,256,512]{2,1,0:T(8,128)(2,1)S(1)} %get-tuple-element.47.rows_ref, ...), custom_call_target="tpu_custom_call" | custom-call | flops 1207959552 | bytes 4194304 | tf_op jit(solution)/shard_map/leaf/pallas_call | solution.py:253
  84.8 7.6 %collective-permute-done.20.refs_1_ = f32[256,256]{1,0:T(8,128)S(1)} collective-permute-done((f32[256,256]{1,0:T(8,128)S(1)}, f32[256,256]{1,0:T(8,128)S(1)}, u32[]{:S(2)}, u32[]{:S(2)}) %collective-permute-start.20) | collective-permute-done | bytes 262176 | tf_op jit(solution)/shard_map/ppermute | solution.py:205
  92.4 1.5 collective-permute-start.23
  93.9 4.1 %collective-permute-done.22.refs_3_ = f32[256,256]{1,0:T(8,128)S(1)} collective-permute-done((f32[256,256]{1,0:T(8,128)S(1)}, f32[256,256]{1,0:T(8,128)S(1)}, u32[]{:S(2)}, u32[]{:S(2)}) %collective-permute-start.22) | collective-permute-done | bytes 262176 | tf_op jit(solution)/shard_map/ppermute | solution.py:205
  98.0 7.5 %collective-permute-done.24.refs_5_ = f32[256,256]{1,0:T(8,128)S(1)} collective-permute-done((f32[256,256]{1,0:T(8,128)S(1)}, f32[256,256]{1,0:T(8,128)S(1)}, u32[]{:S(2)}, u32[]{:S(2)}) %collective-permute-start.24) | collective-permute-done | bytes 262176 | tf_op jit(solution)/shard_map/ppermute | solution.py:205
  105.5 4.1 %collective-permute-start.7 = (f32[256,256]{1,0:T(8,128)S(1)}, f32[256,256]{1,0:T(8,128)S(1)}, u32[]{:S(2)}, u32[]{:S(2)}) collective-permute-start(f32[256,256]{1,0:T(8,128)S(1)} %get-tuple-element.58), channel_id=1, source_target_pairs={{0,20},{4,16},{8,28},{12,24},{16,4},{20,0},{24,12},{28,8},{1,21},{... | collective-permute-start | bytes 786440 | tf_op jit(solution)/shard_map/ppermute | solution.py:205
  109.6 0.3 pad_maximum_fusion
  109.9 0.3 copy.17
  110.2 7.8 %nodes.1 = (bf16[2,2,8,256,256]{4,3,2,1,0:T(8,128)(2,1)S(1)}, bf16[2,8,128,128]{3,2,1,0:T(8,128)(2,1)S(1)}) custom-call(s32[2]{0:T(128)S(1)} %pad_add_fusion.place_ref, f32[8,4,5,32,128]{4,3,2,1,0:T(8,128)S(1)} %bitcast.24), custom_call_target="tpu_custom_call" | custom-call | flops 1207959552 | bytes 8388608 | tf_op jit(solution)/shard_map/nodes/pallas_call | solution.py:355
  118.1 3.3 %collective-permute-start.9 = (f32[256,256]{1,0:T(8,128)S(1)}, f32[256,256]{1,0:T(8,128)S(1)}, u32[]{:S(2)}, u32[]{:S(2)}) collective-permute-start(f32[256,256]{1,0:T(8,128)S(1)} %get-tuple-element.60), channel_id=1, source_target_pairs={{0,24},{4,28},{8,16},{12,20},{16,8},{20,12},{24,0},{28,4},{1,25},{... | collective-permute-start | bytes 786440 | tf_op jit(solution)/shard_map/ppermute | solution.py:205
  121.4 1.5 collective-permute-start.8
  123.0 11.8 %collective-permute-done.6.refs_0_ = f32[256,256]{1,0:T(8,128)S(1)} collective-permute-done((f32[256,256]{1,0:T(8,128)S(1)}, f32[256,256]{1,0:T(8,128)S(1)}, u32[]{:S(2)}, u32[]{:S(2)}) %collective-permute-start.6) | collective-permute-done | bytes 262176 | tf_op jit(solution)/shard_map/ppermute | solution.py:205
  134.7 4.5 %collective-permute-start.10 = (f32[256,256]{1,0:T(8,128)S(1)}, f32[256,256]{1,0:T(8,128)S(1)}, u32[]{:S(2)}, u32[]{:S(2)}) collective-permute-start(f32[256,256]{1,0:T(8,128)S(1)} %get-tuple-element.61), channel_id=1, source_target_pairs={{0,8},{4,12},{8,0},{12,4},{16,24},{20,28},{24,16},{28,20},{1,9},{5... | collective-permute-start | bytes 786440 | tf_op jit(solution)/shard_map/ppermute | solution.py:205
  139.2 1.2 collective-permute-done.7.refs_1_
  140.4 5.3 %collective-permute-start.12 = (f32[256,256]{1,0:T(8,128)S(1)}, f32[256,256]{1,0:T(8,128)S(1)}, u32[]{:S(2)}, u32[]{:S(2)}) collective-permute-start(f32[256,256]{1,0:T(8,128)S(1)} %get-tuple-element.63), channel_id=1, source_target_pairs={{0,12},{4,8},{8,4},{12,0},{16,28},{20,24},{24,20},{28,16},{1,13},{... | collective-permute-start | bytes 786440 | tf_op jit(solution)/shard_map/ppermute | solution.py:205
  145.7 4.7 %tree.3 = (f32[256,256]{1,0:T(8,128)S(1)}, f32[256,256]{1,0:T(8,128)S(1)}, f32[256,256]{1,0:T(8,128)S(1)}, f32[256,256]{1,0:T(8,128)S(1)}, f32[256,256]{1,0:T(8,...) custom-call(s32[2]{0:T(128)S(1)} %pad_add_fusion.place_ref, ...), custom_call_target="tpu_custom_call" | custom-call | flops 3221225472 | bytes 8388608 | tf_op jit(solution)/shard_map/tree/pallas_call | solution.py:273
  150.5 0.1 collective-permute-start.26
  150.5 12.4 %collective-permute-done.11.refs_5_ = f32[256,256]{1,0:T(8,128)S(1)} collective-permute-done((f32[256,256]{1,0:T(8,128)S(1)}, f32[256,256]{1,0:T(8,128)S(1)}, u32[]{:S(2)}, u32[]{:S(2)}) %collective-permute-start.11) | collective-permute-done | bytes 262176 | tf_op jit(solution)/shard_map/ppermute | solution.py:205
  162.9 1.6 collective-permute-start.29
  164.5 1.9 collective-permute-start.30
  166.4 4.7 %tree.2 = (f32[256,256]{1,0:T(8,128)S(1)}, f32[256,256]{1,0:T(8,128)S(1)}, f32[256,256]{1,0:T(8,128)S(1)}, f32[256,256]{1,0:T(8,128)S(1)}, f32[256,256]{1,0:T(8,...) custom-call(s32[2]{0:T(128)S(1)} %pad_add_fusion.place_ref, ...), custom_call_target="tpu_custom_call" | custom-call | flops 3221225472 | bytes 8388608 | tf_op jit(solution)/shard_map/tree/pallas_call | solution.py:273
  171.1 10.4 %collective-permute-done.26.refs_0_ = f32[256,256]{1,0:T(8,128)S(1)} collective-permute-done((f32[256,256]{1,0:T(8,128)S(1)}, f32[256,256]{1,0:T(8,128)S(1)}, u32[]{:S(2)}, u32[]{:S(2)}) %collective-permute-start.26) | collective-permute-done | bytes 262176 | tf_op jit(solution)/shard_map/ppermute | solution.py:205
  181.5 4.0 %collective-permute-start.31 = (f32[256,256]{1,0:T(8,128)S(1)}, f32[256,256]{1,0:T(8,128)S(1)}, u32[]{:S(2)}, u32[]{:S(2)}) collective-permute-start(f32[256,256]{1,0:T(8,128)S(1)} %get-tuple-element.87), channel_id=1, source_target_pairs={{0,8},{4,12},{8,0},{12,4},{16,24},{20,28},{24,16},{28,20},{1,9},{5... | collective-permute-start | bytes 786440 | tf_op jit(solution)/shard_map/ppermute | solution.py:205
  185.5 1.7 collective-permute-done.27.refs_1_
  187.2 4.9 %collective-permute-start.32 = (f32[256,256]{1,0:T(8,128)S(1)}, f32[256,256]{1,0:T(8,128)S(1)}, u32[]{:S(2)}, u32[]{:S(2)}) collective-permute-start(f32[256,256]{1,0:T(8,128)S(1)} %get-tuple-element.88), channel_id=1, source_target_pairs={{0,12},{4,8},{8,4},{12,0},{16,28},{20,24},{24,20},{28,16},{1,13},{... | collective-permute-start | bytes 786440 | tf_op jit(solution)/shard_map/ppermute | solution.py:205
  192.1 3.3 %collective-permute-done.28.refs_2_ = f32[256,256]{1,0:T(8,128)S(1)} collective-permute-done((f32[256,256]{1,0:T(8,128)S(1)}, f32[256,256]{1,0:T(8,128)S(1)}, u32[]{:S(2)}, u32[]{:S(2)}) %collective-permute-start.28) | collective-permute-done | bytes 262176 | tf_op jit(solution)/shard_map/ppermute | solution.py:205
  195.3 1.9 collective-permute-start.17
  197.2 6.4 %collective-permute-done.29.refs_3_ = f32[256,256]{1,0:T(8,128)S(1)} collective-permute-done((f32[256,256]{1,0:T(8,128)S(1)}, f32[256,256]{1,0:T(8,128)S(1)}, u32[]{:S(2)}, u32[]{:S(2)}) %collective-permute-start.29) | collective-permute-done | bytes 262176 | tf_op jit(solution)/shard_map/ppermute | solution.py:205
  203.7 3.0 %collective-permute-start.19 = (f32[256,256]{1,0:T(8,128)S(1)}, f32[256,256]{1,0:T(8,128)S(1)}, u32[]{:S(2)}, u32[]{:S(2)}) collective-permute-start(f32[256,256]{1,0:T(8,128)S(1)} %get-tuple-element.73), channel_id=1, source_target_pairs={{0,12},{4,8},{8,4},{12,0},{16,28},{20,24},{24,20},{28,16},{1,13},{... | collective-permute-start | bytes 786440 | tf_op jit(solution)/shard_map/ppermute | solution.py:205
  206.6 2.9 %collective-permute-start.14 = (f32[256,256]{1,0:T(8,128)S(1)}, f32[256,256]{1,0:T(8,128)S(1)}, u32[]{:S(2)}, u32[]{:S(2)}) collective-permute-start(f32[256,256]{1,0:T(8,128)S(1)} %get-tuple-element.66), channel_id=1, source_target_pairs={{0,20},{4,16},{8,28},{12,24},{16,4},{20,0},{24,12},{28,8},{1,21},{... | collective-permute-start | bytes 786440 | tf_op jit(solution)/shard_map/ppermute | solution.py:205
  209.5 0.5 collective-permute-start.15
  210.1 8.0 %collective-permute-done.18.refs_2_ = f32[256,256]{1,0:T(8,128)S(1)} collective-permute-done((f32[256,256]{1,0:T(8,128)S(1)}, f32[256,256]{1,0:T(8,128)S(1)}, u32[]{:S(2)}, u32[]{:S(2)}) %collective-permute-start.18) | collective-permute-done | bytes 262176 | tf_op jit(solution)/shard_map/ppermute | solution.py:205
  218.0 3.0 %collective-permute-start.16 = (f32[256,256]{1,0:T(8,128)S(1)}, f32[256,256]{1,0:T(8,128)S(1)}, u32[]{:S(2)}, u32[]{:S(2)}) collective-permute-start(f32[256,256]{1,0:T(8,128)S(1)} %get-tuple-element.68), channel_id=1, source_target_pairs={{0,28},{4,24},{8,20},{12,16},{16,12},{20,8},{24,4},{28,0},{1,29},{... | collective-permute-start | bytes 786440 | tf_op jit(solution)/shard_map/ppermute | solution.py:205
  221.0 3.8 %last.4.refs_4_ = f32[512,4096]{1,0:T(8,128)} custom-call(s32[2]{0:T(128)S(1)} %pad_add_fusion.place_ref, f32[512,4096]{1,0:T(8,128)S(1)} %bitcast.23, f32[4,256,256]{2,1,0:T(8,128)S(1)} %get-tuple-element.50.after_ref.inner_ref, bf16[2,384,384]{2,1,0:T(8,128)(2,1)S(1)} %get-tuple-element.52.rest_ref, f32[256,256]{1,0:T(8,128)S(1)} %get-tuple-element.85.refs_0_, ...), custom_call_target="tpu_custom_call" | custom-call | flops 905969664 | bytes 6291456 | tf_op jit(solution)/shard_map/last/pallas_call | solution.py:298
  224.9 3.8 %last.5.refs_4_ = f32[512,4096]{1,0:T(8,128)} custom-call(s32[2]{0:T(128)S(1)} %pad_add_fusion.place_ref, f32[512,4096]{1,0:T(8,128)S(1)} %bitcast.23, f32[4,256,256]{2,1,0:T(8,128)S(1)} %get-tuple-element.49.after_ref.inner_ref, bf16[2,384,384]{2,1,0:T(8,128)(2,1)S(1)} %get-tuple-element.52.rest_ref, ...), custom_call_target="tpu_custom_call", output_to_operand_aliasing={{}: (8, {})} | custom-call | flops 905969664 | bytes 6291456 | tf_op jit(solution)/shard_map/last/pallas_call | solution.py:298
  228.7 3.8 %last.6.refs_4_ = f32[512,4096]{1,0:T(8,128)} custom-call(s32[2]{0:T(128)S(1)} %pad_add_fusion.place_ref, f32[512,4096]{1,0:T(8,128)S(1)} %bitcast.23, f32[4,256,256]{2,1,0:T(8,128)S(1)} %get-tuple-element.69.inner_ref, bf16[2,384,384]{2,1,0:T(8,128)(2,1)S(1)} %get-tuple-element.52.rest_ref, ...), custom_call_target="tpu_custom_call", output_to_operand_aliasing={{}: (8, {})} | custom-call | flops 905969664 | bytes 6291456 | tf_op jit(solution)/shard_map/last/pallas_call | solution.py:298
  232.5 9.0 %collective-permute-done.14.refs_1_ = f32[256,256]{1,0:T(8,128)S(1)} collective-permute-done((f32[256,256]{1,0:T(8,128)S(1)}, f32[256,256]{1,0:T(8,128)S(1)}, u32[]{:S(2)}, u32[]{:S(2)}) %collective-permute-start.14) | collective-permute-done | bytes 262176 | tf_op jit(solution)/shard_map/ppermute | solution.py:205
  241.5 7.5 %collective-permute-done.15.refs_2_ = f32[256,256]{1,0:T(8,128)S(1)} collective-permute-done((f32[256,256]{1,0:T(8,128)S(1)}, f32[256,256]{1,0:T(8,128)S(1)}, u32[]{:S(2)}, u32[]{:S(2)}) %collective-permute-start.15) | collective-permute-done | bytes 262176 | tf_op jit(solution)/shard_map/ppermute | solution.py:205
  249.0 3.8 %collective-permute-done.16.refs_3_ = f32[256,256]{1,0:T(8,128)S(1)} collective-permute-done((f32[256,256]{1,0:T(8,128)S(1)}, f32[256,256]{1,0:T(8,128)S(1)}, u32[]{:S(2)}, u32[]{:S(2)}) %collective-permute-start.16) | collective-permute-done | bytes 262176 | tf_op jit(solution)/shard_map/ppermute | solution.py:205
  252.8 3.8 %last.7 = f32[512,4096]{1,0:T(8,128)} custom-call(s32[2]{0:T(128)S(1)} %pad_add_fusion.place_ref, f32[512,4096]{1,0:T(8,128)S(1)} %bitcast.23, f32[4,256,256]{2,1,0:T(8,128)S(1)} %get-tuple-element.51.after_ref.inner_ref, bf16[2,384,384]{2,1,0:T(8,128)(2,1)S(1)} %get-tuple-element.52.rest_ref, ...), custom_call_target="tpu_custom_call", output_to_operand_aliasing={{}: (8, {})} | custom-call | flops 905969664 | bytes 6291456 | tf_op jit(solution)/shard_map/last/pallas_call | solution.py:298
  (38 shorter events, 0.2 us)
Async XLA Ops:
  7.5 0.9 copy-start.3
  10.3 3.4 %copy-start = (f32[512,4096]{1,0:T(8,128)S(1)}, f32[512,4096]{1,0:T(8,128)}, u32[]{:S(2)}) copy-start(f32[512,4096]{1,0:T(8,128)} %window_ref.15) | copy-start | bytes 25165828
  13.7 18.3 %copy-start.1 = (f32[2,128,128]{2,1,0:T(8,128)S(1)}, f32[2,128,128]{2,1,0:T(8,128)}, u32[]{:S(2)}) copy-start(f32[2,128,128]{2,1,0:T(8,128)} %vecs_ref.1) | copy-start | bytes 393220
  13.7 18.3 %copy-start.2 = (f32[2,128,128]{2,1,0:T(8,128)S(1)}, f32[2,128,128]{2,1,0:T(8,128)}, u32[]{:S(2)}) copy-start(f32[2,128,128]{2,1,0:T(8,128)} %t_ref.1) | copy-start | bytes 393220
  17.7 14.3 %collective-permute-start = (f32[256,256]{1,0:T(8,128)S(1)}, f32[256,256]{1,0:T(8,128)S(1)}, u32[]{:S(2)}, u32[]{:S(2)}) collective-permute-start(f32[256,256]{1,0:T(8,128)S(1)} %get-tuple-element.54), channel_id=1, source_target_pairs={{0,16},{4,20},{8,24},{12,28},{16,0},{20,4},{24,8},{28,12},{1,17},{... | collective-permute-start | bytes 786440 | tf_op jit(solution)/shard_map/ppermute | solution.py:205
  32.5 6.2 %collective-permute-start.1 = (f32[1,5,32,128]{3,2,1,0:T(8,128)S(1)}, f32[1,5,32,128]{3,2,1,0:T(8,128)S(1)}, u32[]{:S(2)}, u32[]{:S(2)}) collective-permute-start(f32[1,5,32,128]{3,2,1,0:T(8,128)S(1)} %bitcast.25), channel_id=1, source_target_pairs={{0,16},{4,20},{8,24},{12,28},{16,0},{20,4},{24,8},{28,12},{1,17},{... | collective-permute-start | bytes 245768 | tf_op jit(solution)/shard_map/ppermute | solution.py:205
  38.7 5.6 %collective-permute-start.2 = (f32[2,5,32,128]{3,2,1,0:T(8,128)S(1)}, f32[2,5,32,128]{3,2,1,0:T(8,128)S(1)}, u32[]{:S(2)}, u32[]{:S(2)}) collective-permute-start(f32[2,5,32,128]{3,2,1,0:T(8,128)S(1)} %get-tuple-element.92), channel_id=1, source_target_pairs={{0,8},{4,12},{8,0},{12,4},{16,24},{20,28},{24,16},{28,20},{1,9},{5... | collective-permute-start | bytes 491528 | tf_op jit(solution)/shard_map/ppermute | solution.py:205
  44.4 7.7 %collective-permute-start.3 = (f32[4,5,32,128]{3,2,1,0:T(8,128)S(1)}, f32[4,5,32,128]{3,2,1,0:T(8,128)S(1)}, u32[]{:S(2)}, u32[]{:S(2)}) collective-permute-start(f32[4,5,32,128]{3,2,1,0:T(8,128)S(1)} %bitcast.30), channel_id=1, source_target_pairs={{0,4},{4,0},{8,12},{12,8},{16,20},{20,16},{24,28},{28,24},{1,5},{5... | collective-permute-start | bytes 983048 | tf_op jit(solution)/shard_map/ppermute | solution.py:205
  52.2 13.8 %collective-permute-start.4 = (f32[8,1,5,32,128]{4,3,2,0,1:T(8,128)S(1)}, f32[8,1,5,32,128]{4,3,2,0,1:T(8,128)S(1)}, u32[]{:S(2)}, u32[]{:S(2)}) collective-permute-start(f32[8,1,5,32,128]{4,3,2,0,1:T(8,128)S(1)} %bitcast.27), channel_id=1, source_target_pairs={{0,2},{1,3},{2,0},{3,1},{4,6},{5,7},{6,4},{7,5},{8,10},{9,11},{10,... | collective-permute-start | bytes 1966088 | tf_op jit(solution)/shard_map/ppermute | solution.py:205
  66.4 39.1 %collective-permute-start.5 = (f32[8,2,5,32,128]{4,3,2,0,1:T(8,128)S(1)}, f32[8,2,5,32,128]{4,3,2,0,1:T(8,128)S(1)}, u32[]{:S(2)}, u32[]{:S(2)}) collective-permute-start(f32[8,2,5,32,128]{4,3,2,0,1:T(8,128)S(1)} %get-tuple-element.90), channel_id=1, source_target_pairs={{0,1},{1,0},{2,3},{3,2},{4,5},{5,4},{6,7},{7,6},{8,9},{9,8},{10,11... | collective-permute-start | bytes 3932168 | tf_op jit(solution)/shard_map/ppermute | solution.py:205
  66.5 25.9 %collective-permute-start.20 = (f32[256,256]{1,0:T(8,128)S(1)}, f32[256,256]{1,0:T(8,128)S(1)}, u32[]{:S(2)}, u32[]{:S(2)}) collective-permute-start(f32[256,256]{1,0:T(8,128)S(1)} %get-tuple-element.74), channel_id=1, source_target_pairs={{0,20},{4,16},{8,28},{12,24},{16,4},{20,0},{24,12},{28,8},{1,21},{... | collective-permute-start | bytes 786440 | tf_op jit(solution)/shard_map/ppermute | solution.py:205
  69.2 28.7 %collective-permute-start.22 = (f32[256,256]{1,0:T(8,128)S(1)}, f32[256,256]{1,0:T(8,128)S(1)}, u32[]{:S(2)}, u32[]{:S(2)}) collective-permute-start(f32[256,256]{1,0:T(8,128)S(1)} %get-tuple-element.76), channel_id=1, source_target_pairs={{0,24},{4,28},{8,16},{12,20},{16,8},{20,12},{24,0},{28,4},{1,25},{... | collective-permute-start | bytes 786440 | tf_op jit(solution)/shard_map/ppermute | solution.py:205
  69.2 36.3 %collective-permute-start.24 = (f32[256,256]{1,0:T(8,128)S(1)}, f32[256,256]{1,0:T(8,128)S(1)}, u32[]{:S(2)}, u32[]{:S(2)}) collective-permute-start(f32[256,256]{1,0:T(8,128)S(1)} %get-tuple-element.78), channel_id=1, source_target_pairs={{0,28},{4,24},{8,20},{12,16},{16,12},{20,8},{24,4},{28,0},{1,29},{... | collective-permute-start | bytes 786440 | tf_op jit(solution)/shard_map/ppermute | solution.py:205
  75.2 42.8 %collective-permute-start.21 = (f32[256,256]{1,0:T(8,128)S(1)}, f32[256,256]{1,0:T(8,128)S(1)}, u32[]{:S(2)}, u32[]{:S(2)}) collective-permute-start(f32[256,256]{1,0:T(8,128)S(1)} %get-tuple-element.75), channel_id=1, source_target_pairs={{0,4},{4,0},{8,12},{12,8},{16,20},{20,16},{24,28},{28,24},{1,5},{5... | collective-permute-start | bytes 786440 | tf_op jit(solution)/shard_map/ppermute | solution.py:205
  92.4 29.0 %collective-permute-start.23 = (f32[256,256]{1,0:T(8,128)S(1)}, f32[256,256]{1,0:T(8,128)S(1)}, u32[]{:S(2)}, u32[]{:S(2)}) collective-permute-start(f32[256,256]{1,0:T(8,128)S(1)} %get-tuple-element.77), channel_id=1, source_target_pairs={{0,8},{4,12},{8,0},{12,4},{16,24},{20,28},{24,16},{28,20},{1,9},{5... | collective-permute-start | bytes 786440 | tf_op jit(solution)/shard_map/ppermute | solution.py:205
  98.0 23.4 %collective-permute-start.25 = (f32[256,256]{1,0:T(8,128)S(1)}, f32[256,256]{1,0:T(8,128)S(1)}, u32[]{:S(2)}, u32[]{:S(2)}) collective-permute-start(f32[256,256]{1,0:T(8,128)S(1)} %get-tuple-element.79), channel_id=1, source_target_pairs={{0,12},{4,8},{8,4},{12,0},{16,28},{20,24},{24,20},{28,16},{1,13},{... | collective-permute-start | bytes 786440 | tf_op jit(solution)/shard_map/ppermute | solution.py:205
  105.5 29.2 %collective-permute-start.6 = (f32[256,256]{1,0:T(8,128)S(1)}, f32[256,256]{1,0:T(8,128)S(1)}, u32[]{:S(2)}, u32[]{:S(2)}) collective-permute-start(f32[256,256]{1,0:T(8,128)S(1)} %get-tuple-element.57), channel_id=1, source_target_pairs={{0,16},{4,20},{8,24},{12,28},{16,0},{20,4},{24,8},{28,12},{1,17},{... | collective-permute-start | bytes 786440 | tf_op jit(solution)/shard_map/ppermute | solution.py:205
  105.5 34.9 %collective-permute-start.7 = (f32[256,256]{1,0:T(8,128)S(1)}, f32[256,256]{1,0:T(8,128)S(1)}, u32[]{:S(2)}, u32[]{:S(2)}) collective-permute-start(f32[256,256]{1,0:T(8,128)S(1)} %get-tuple-element.58), channel_id=1, source_target_pairs={{0,20},{4,16},{8,28},{12,24},{16,4},{20,0},{24,12},{28,8},{1,21},{... | collective-permute-start | bytes 786440 | tf_op jit(solution)/shard_map/ppermute | solution.py:205
  118.1 32.4 %collective-permute-start.9 = (f32[256,256]{1,0:T(8,128)S(1)}, f32[256,256]{1,0:T(8,128)S(1)}, u32[]{:S(2)}, u32[]{:S(2)}) collective-permute-start(f32[256,256]{1,0:T(8,128)S(1)} %get-tuple-element.60), channel_id=1, source_target_pairs={{0,24},{4,28},{8,16},{12,20},{16,8},{20,12},{24,0},{28,4},{1,25},{... | collective-permute-start | bytes 786440 | tf_op jit(solution)/shard_map/ppermute | solution.py:205
  121.4 41.5 %collective-permute-start.11 = (f32[256,256]{1,0:T(8,128)S(1)}, f32[256,256]{1,0:T(8,128)S(1)}, u32[]{:S(2)}, u32[]{:S(2)}) collective-permute-start(f32[256,256]{1,0:T(8,128)S(1)} %get-tuple-element.62), channel_id=1, source_target_pairs={{0,28},{4,24},{8,20},{12,16},{16,12},{20,8},{24,4},{28,0},{1,29},{... | collective-permute-start | bytes 786440 | tf_op jit(solution)/shard_map/ppermute | solution.py:205
  121.4 41.5 %collective-permute-start.8 = (f32[256,256]{1,0:T(8,128)S(1)}, f32[256,256]{1,0:T(8,128)S(1)}, u32[]{:S(2)}, u32[]{:S(2)}) collective-permute-start(f32[256,256]{1,0:T(8,128)S(1)} %get-tuple-element.59), channel_id=1, source_target_pairs={{0,4},{4,0},{8,12},{12,8},{16,20},{20,16},{24,28},{28,24},{1,5},{5... | collective-permute-start | bytes 786440 | tf_op jit(solution)/shard_map/ppermute | solution.py:205
  134.7 28.2 %collective-permute-start.10 = (f32[256,256]{1,0:T(8,128)S(1)}, f32[256,256]{1,0:T(8,128)S(1)}, u32[]{:S(2)}, u32[]{:S(2)}) collective-permute-start(f32[256,256]{1,0:T(8,128)S(1)} %get-tuple-element.61), channel_id=1, source_target_pairs={{0,8},{4,12},{8,0},{12,4},{16,24},{20,28},{24,16},{28,20},{1,9},{5... | collective-permute-start | bytes 786440 | tf_op jit(solution)/shard_map/ppermute | solution.py:205
  140.4 24.1 %collective-permute-start.12 = (f32[256,256]{1,0:T(8,128)S(1)}, f32[256,256]{1,0:T(8,128)S(1)}, u32[]{:S(2)}, u32[]{:S(2)}) collective-permute-start(f32[256,256]{1,0:T(8,128)S(1)} %get-tuple-element.63), channel_id=1, source_target_pairs={{0,12},{4,8},{8,4},{12,0},{16,28},{20,24},{24,20},{28,16},{1,13},{... | collective-permute-start | bytes 786440 | tf_op jit(solution)/shard_map/ppermute | solution.py:205
  145.7 75.3 %slice-start = ((s8[8388608]{0:T(1024)(128)(4,1)}), s8[4194304]{0:T(1024)(128)(4,1)S(1)}, s32[]{:S(2)}) async-start(s8[8388608]{0:T(1024)(128)(4,1)} %bitcast.22), calls=%async_computation | async-start | bytes 8388608
  150.5 31.0 %collective-permute-start.26 = (f32[256,256]{1,0:T(8,128)S(1)}, f32[256,256]{1,0:T(8,128)S(1)}, u32[]{:S(2)}, u32[]{:S(2)}) collective-permute-start(f32[256,256]{1,0:T(8,128)S(1)} %get-tuple-element.81), channel_id=1, source_target_pairs={{0,16},{4,20},{8,24},{12,28},{16,0},{20,4},{24,8},{28,12},{1,17},{... | collective-permute-start | bytes 786440 | tf_op jit(solution)/shard_map/ppermute | solution.py:205
  162.9 24.3 %collective-permute-start.27 = (f32[256,256]{1,0:T(8,128)S(1)}, f32[256,256]{1,0:T(8,128)S(1)}, u32[]{:S(2)}, u32[]{:S(2)}) collective-permute-start(f32[256,256]{1,0:T(8,128)S(1)} %get-tuple-element.82), channel_id=1, source_target_pairs={{0,20},{4,16},{8,28},{12,24},{16,4},{20,0},{24,12},{28,8},{1,21},{... | collective-permute-start | bytes 786440 | tf_op jit(solution)/shard_map/ppermute | solution.py:205
  162.9 32.4 %collective-permute-start.28 = (f32[256,256]{1,0:T(8,128)S(1)}, f32[256,256]{1,0:T(8,128)S(1)}, u32[]{:S(2)}, u32[]{:S(2)}) collective-permute-start(f32[256,256]{1,0:T(8,128)S(1)} %get-tuple-element.83), channel_id=1, source_target_pairs={{0,24},{4,28},{8,16},{12,20},{16,8},{20,12},{24,0},{28,4},{1,25},{... | collective-permute-start | bytes 786440 | tf_op jit(solution)/shard_map/ppermute | solution.py:205
  162.9 40.7 %collective-permute-start.29 = (f32[256,256]{1,0:T(8,128)S(1)}, f32[256,256]{1,0:T(8,128)S(1)}, u32[]{:S(2)}, u32[]{:S(2)}) collective-permute-start(f32[256,256]{1,0:T(8,128)S(1)} %get-tuple-element.84), channel_id=1, source_target_pairs={{0,28},{4,24},{8,20},{12,16},{16,12},{20,8},{24,4},{28,0},{1,29},{... | collective-permute-start | bytes 786440 | tf_op jit(solution)/shard_map/ppermute | solution.py:205
  164.5 39.2 %collective-permute-start.30 = (f32[256,256]{1,0:T(8,128)S(1)}, f32[256,256]{1,0:T(8,128)S(1)}, u32[]{:S(2)}, u32[]{:S(2)}) collective-permute-start(f32[256,256]{1,0:T(8,128)S(1)} %get-tuple-element.86), channel_id=1, source_target_pairs={{0,4},{4,0},{8,12},{12,8},{16,20},{20,16},{24,28},{28,24},{1,5},{5... | collective-permute-start | bytes 786440 | tf_op jit(solution)/shard_map/ppermute | solution.py:205
  166.4 54.6 %slice-start.1 = ((s8[8388608]{0:T(1024)(128)(4,1)}), s8[4194304]{0:T(1024)(128)(4,1)S(1)}, s32[]{:S(2)}) async-start(s8[8388608]{0:T(1024)(128)(4,1)} %bitcast.22), calls=%async_computation.1 | async-start | bytes 8388608
  181.5 25.1 %collective-permute-start.31 = (f32[256,256]{1,0:T(8,128)S(1)}, f32[256,256]{1,0:T(8,128)S(1)}, u32[]{:S(2)}, u32[]{:S(2)}) collective-permute-start(f32[256,256]{1,0:T(8,128)S(1)} %get-tuple-element.87), channel_id=1, source_target_pairs={{0,8},{4,12},{8,0},{12,4},{16,24},{20,28},{24,16},{28,20},{1,9},{5... | collective-permute-start | bytes 786440 | tf_op jit(solution)/shard_map/ppermute | solution.py:205
  187.2 19.5 %collective-permute-start.32 = (f32[256,256]{1,0:T(8,128)S(1)}, f32[256,256]{1,0:T(8,128)S(1)}, u32[]{:S(2)}, u32[]{:S(2)}) collective-permute-start(f32[256,256]{1,0:T(8,128)S(1)} %get-tuple-element.88), channel_id=1, source_target_pairs={{0,12},{4,8},{8,4},{12,0},{16,28},{20,24},{24,20},{28,16},{1,13},{... | collective-permute-start | bytes 786440 | tf_op jit(solution)/shard_map/ppermute | solution.py:205
  195.3 14.2 %collective-permute-start.17 = (f32[256,256]{1,0:T(8,128)S(1)}, f32[256,256]{1,0:T(8,128)S(1)}, u32[]{:S(2)}, u32[]{:S(2)}) collective-permute-start(f32[256,256]{1,0:T(8,128)S(1)} %get-tuple-element.71), channel_id=1, source_target_pairs={{0,4},{4,0},{8,12},{12,8},{16,20},{20,16},{24,28},{28,24},{1,5},{5... | collective-permute-start | bytes 786440 | tf_op jit(solution)/shard_map/ppermute | solution.py:205
  203.7 14.4 %collective-permute-start.18 = (f32[256,256]{1,0:T(8,128)S(1)}, f32[256,256]{1,0:T(8,128)S(1)}, u32[]{:S(2)}, u32[]{:S(2)}) collective-permute-start(f32[256,256]{1,0:T(8,128)S(1)} %get-tuple-element.72), channel_id=1, source_target_pairs={{0,8},{4,12},{8,0},{12,4},{16,24},{20,28},{24,16},{28,20},{1,9},{5... | collective-permute-start | bytes 786440 | tf_op jit(solution)/shard_map/ppermute | solution.py:205
  203.7 25.0 %collective-permute-start.19 = (f32[256,256]{1,0:T(8,128)S(1)}, f32[256,256]{1,0:T(8,128)S(1)}, u32[]{:S(2)}, u32[]{:S(2)}) collective-permute-start(f32[256,256]{1,0:T(8,128)S(1)} %get-tuple-element.73), channel_id=1, source_target_pairs={{0,12},{4,8},{8,4},{12,0},{16,28},{20,24},{24,20},{28,16},{1,13},{... | collective-permute-start | bytes 786440 | tf_op jit(solution)/shard_map/ppermute | solution.py:205
  206.6 25.9 %collective-permute-start.13 = (f32[256,256]{1,0:T(8,128)S(1)}, f32[256,256]{1,0:T(8,128)S(1)}, u32[]{:S(2)}, u32[]{:S(2)}) collective-permute-start(f32[256,256]{1,0:T(8,128)S(1)} %get-tuple-element.65), channel_id=1, source_target_pairs={{0,16},{4,20},{8,24},{12,28},{16,0},{20,4},{24,8},{28,12},{1,17},{... | collective-permute-start | bytes 786440 | tf_op jit(solution)/shard_map/ppermute | solution.py:205
  206.6 34.8 %collective-permute-start.14 = (f32[256,256]{1,0:T(8,128)S(1)}, f32[256,256]{1,0:T(8,128)S(1)}, u32[]{:S(2)}, u32[]{:S(2)}) collective-permute-start(f32[256,256]{1,0:T(8,128)S(1)} %get-tuple-element.66), channel_id=1, source_target_pairs={{0,20},{4,16},{8,28},{12,24},{16,4},{20,0},{24,12},{28,8},{1,21},{... | collective-permute-start | bytes 786440 | tf_op jit(solution)/shard_map/ppermute | solution.py:205
  209.5 39.5 %collective-permute-start.15 = (f32[256,256]{1,0:T(8,128)S(1)}, f32[256,256]{1,0:T(8,128)S(1)}, u32[]{:S(2)}, u32[]{:S(2)}) collective-permute-start(f32[256,256]{1,0:T(8,128)S(1)} %get-tuple-element.67), channel_id=1, source_target_pairs={{0,24},{4,28},{8,16},{12,20},{16,8},{20,12},{24,0},{28,4},{1,25},{... | collective-permute-start | bytes 786440 | tf_op jit(solution)/shard_map/ppermute | solution.py:205
  218.0 34.8 %collective-permute-start.16 = (f32[256,256]{1,0:T(8,128)S(1)}, f32[256,256]{1,0:T(8,128)S(1)}, u32[]{:S(2)}, u32[]{:S(2)}) collective-permute-start(f32[256,256]{1,0:T(8,128)S(1)} %get-tuple-element.68), channel_id=1, source_target_pairs={{0,28},{4,24},{8,20},{12,16},{16,12},{20,8},{24,4},{28,0},{1,29},{... | collective-permute-start | bytes 786440 | tf_op jit(solution)/shard_map/ppermute | solution.py:205

commit v2 on v1

v2 whole, which is shorter than its diff:
```python
import functools

import jax
import jax.numpy as jnp
from jax import lax
from jax.experimental import pallas as pl
from jax.experimental.pallas import tpu as pltpu
from jax.sharding import PartitionSpec as P

VMEM_LIMIT = 16 * 1024 * 1024
LARGE_LIMIT = 56 * 1024 * 1024
F32 = jnp.float32
BF16 = jnp.bfloat16
FLIGHT = 3
STRICT = False
RIDE = 0
PACE = (0, 2, 4)
CHUNKS = 2


def mm(left, right):
    return jnp.dot(left, right, precision=lax.Precision.HIGHEST, preferred_element_type=F32)


def halves(value):
    high = value.astype(BF16)
    return high, (value - high.astype(F32)).astype(BF16)


def mm3(left, right):
    high, low = halves(right)

    def dot(a, b):
        return jnp.dot(a, b, preferred_element_type=F32)

    return dot(left[0], high) + (dot(left[0], low) + dot(left[1], high))


def params(limit=VMEM_LIMIT):
    return pltpu.CompilerParams(vmem_limit_bytes=limit)


def cost(flops, nbytes):
    return pl.CostEstimate(flops=int(flops), bytes_accessed=int(nbytes), transcendentals=0)


def prep_kernel(vecs_ref, leaf_ref, after_ref, rows_ref, send_ref, rest_ref, dmat_ref):
    width = leaf_ref.shape[-1]

    def put(ref, place, value):
        high, low = halves(value)
        ref[(0, *place)] = high
        ref[(1, *place)] = low

    one, two = vecs_ref[0], vecs_ref[1]
    one_top, one_rest = one[:width], one[width:]
    two_top, two_rest = two[:width], two[width:]
    first, second = leaf_ref[0].T, leaf_ref[1].T
    two_rest_t, two_top_t = two_rest.T, two_top.T
    zero = jnp.zeros((width, width), F32)
    left, right, both = slice(0, width), slice(width, 2 * width), slice(None)
    cross = mm(two_rest_t, one_rest)
    lower = -mm(second, mm(cross, first))
    top_l, rest_l = mm(two_top, second), mm(two_rest, second)
    put(rows_ref, (left, both), one.T)
    put(rows_ref, (right, left), zero)
    put(rows_ref, (right, slice(width, None)), two_rest_t)
    put(send_ref, (left, left), -mm(one_top, first))
    put(send_ref, (left, right), zero)
    put(send_ref, (right, left), mm(two_top, lower))
    put(send_ref, (right, right), top_l)
    put(rest_ref, (both, left), mm(one_rest, first) + mm(two_rest, lower))
    put(rest_ref, (both, right), rest_l)
    put(rest_ref, (both, slice(2 * width, None)), mm(rest_l, two_top_t))
    shape = (width, width)
    eye = lax.broadcasted_iota(jnp.int32, shape, 0) == lax.broadcasted_iota(jnp.int32, shape, 1)
    dmat_ref[...] = eye.astype(F32) - mm(top_l, two_top_t)


def pack_kernel(place_ref, vecs_ref, t_ref, out_ref):
    panels = vecs_ref.shape[0]
    share = out_ref.shape[1] // (2 * panels)
    part = pl.ds(pl.multiple_of(place_ref[1] * share, share), share)
    for panel in range(panels):
        out_ref[0, pl.ds(2 * panel * share, share), :] = vecs_ref[panel, part, :]
        out_ref[0, pl.ds((2 * panel + 1) * share, share), :] = t_ref[panel, part, :]


def touch_kernel(*refs):
    refs[-1][...] = refs[0][...]


def leaf_kernel(parts, place_ref, window_ref, rows_ref, send_ref, after_ref, inner_ref, *refs):
    pieces, (buffer, sems) = refs[: len(parts)], refs[len(parts) :]
    width = send_ref.shape[1] // 2
    copies = []
    for i, part in enumerate(parts):
        copy = pltpu.make_async_copy(part(place_ref, window_ref), buffer.at[i], sems.at[i])
        copy.start()
        copies.append(copy)
    for i, piece in enumerate(pieces):
        copies[i].wait()
        inner = mm3((rows_ref[0], rows_ref[1]), buffer[i])
        inner_ref[i] = inner
        message = mm3((send_ref[0], send_ref[1]), inner)
        piece[:width, :] = message[:width] + buffer[i, :width, :]
        piece[width:, :] = message[width:]


def nodes_kernel(place_ref, after_ref, pack_ref, pair_ref):
    width = pair_ref.shape[-1] // 2

    def whole(i):
        parts = pack_ref.shape[0]
        share = width // parts
        return jnp.concatenate(
            [pack_ref[c ^ place_ref[1], 0, i * share : (i + 1) * share] for c in range(parts)], axis=0
        )

    def put(panel, rows, columns, value):
        high, low = halves(value)
        pair_ref[0, panel, 0, rows, columns] = high
        pair_ref[1, panel, 0, rows, columns] = low

    top, low = slice(0, width), slice(width, 2 * width)
    panels = pair_ref.shape[1]
    for panel in range(panels):
        vfac = whole(2 * panel)
        sfac_t = whole(2 * panel + 1).T
        right = mm(sfac_t, vfac.T)
        put(panel, top, top, sfac_t)
        put(panel, top, low, right)
        put(panel, low, top, mm(vfac, sfac_t))
        put(panel, low, low, mm(vfac, right))


def tree_kernel(rows, order, place_ref, pair_ref, dmat_ref, *refs):
    pieces, outs = [None] * rows, [None] * rows
    for i, k in enumerate(order):
        pieces[k] = refs[i]
        outs[k] = refs[rows + i]
    first, second = refs[2 * rows :]
    width = first.shape[1]
    me = place_ref[0]
    levels = rows.bit_length() - 1
    for k in range(rows):
        first[me ^ k] = pieces[k][:width, :]
        second[me ^ k] = pieces[k][width:, :]

    def each(count, body):
        if rows <= 8:
            for j in range(count):
                body(j, 0)
        else:
            lax.fori_loop(0, count, body, 0)

    def sweep(panel, tops):
        for level in range(levels):
            stride = 1 << level

            def pair(j, carry, level=level, stride=stride):
                a = (j >> level << (level + 1)) + (j & (stride - 1))
                b = a + stride
                top_a, top_b = tops[a], tops[b]
                both = jnp.concatenate([top_a, top_b], axis=0)
                change = mm3((pair_ref[0, panel, b], pair_ref[1, panel, b]), both)
                tops[a] = top_a - change[:width]
                tops[b] = top_b - change[width:]
                return carry

            each(rows // 2, pair)
        root = tops[0]
        low = slice(width, 2 * width)
        tops[0] = root - mm3((pair_ref[0, panel, 0, low, low], pair_ref[1, panel, 0, low, low]), root)

    def leaf(r, carry):
        dmat = jnp.concatenate([dmat_ref[c ^ place_ref[1], me ^ r] for c in range(dmat_ref.shape[0])], axis=0)
        second[r] = mm3(halves(dmat), first[r]) - second[r]
        return carry

    sweep(0, first)
    each(rows, leaf)
    sweep(1, second)
    for k in range(rows):
        outs[k][:width, :] = first[me ^ k]
        outs[k][width:, :] = second[me ^ k]


def last_kernel(parts, begin, place_ref, window_ref, inner_ref, rest_ref, *refs):
    count = len(parts)
    pieces, (out_ref, buffer, both, sems) = refs[:count], refs[-4:]
    width = inner_ref.shape[1] // 2
    loads, stores = [], []
    for i, part in enumerate(parts):
        source = part(place_ref, window_ref).at[pl.ds(width, window_ref.shape[-2] - width)]
        loads.append(pltpu.make_async_copy(source, buffer.at[i, pl.ds(width, source.shape[0])], sems.at[0, i]))
        stores.append(pltpu.make_async_copy(buffer.at[i], part(place_ref, out_ref), sems.at[1, i]))
    for load in loads:
        load.start()
    for i, piece in enumerate(pieces):
        both[: 2 * width, :] = inner_ref[begin + i]
        both[2 * width :, :] = piece[:width, :]
        change = mm3((rest_ref[0], rest_ref[1]), both[...])
        buffer[i, :width, :] = piece[width:, :]
        loads[i].wait()
        buffer[i, width:, :] = buffer[i, width:, :] - change
        stores[i].start()
    for store in stores:
        store.wait()


def vmem():
    return pl.BlockSpec(memory_space=pltpu.VMEM)


def anywhere():
    return pl.BlockSpec(memory_space=pl.ANY)


def smem():
    return pl.BlockSpec(memory_space=pltpu.SMEM)


def hbm():
    return pl.BlockSpec(memory_space=pltpu.HBM)


def swap(value, axis, k):
    return lax.ppermute(value, axis, [(i, i ^ k) for i in range(lax.axis_size(axis))])


def butterfly(window, leaf_vecs, leaf_t, node_vecs, node_t):
    width, panels = leaf_t.shape[-1], leaf_t.shape[0]
    rows = lax.axis_size("row")
    me = lax.axis_index("row")
    work = window
    all_rows = lax.all_gather(leaf_vecs, "col", axis=1, tiled=True)
    for panel in range(panels):
        vecs = all_rows[panel]
        work = work - mm(vecs, mm(leaf_t[panel].T, mm(vecs.T, work)))
        top, vfac, sfac = work[:width], node_vecs[panel], node_t[panel]
        for level in range(rows.bit_length() - 1):
            lower = me // (1 << level) % 2 == 0
            got, got_v, got_s = (swap(value, "row", 1 << level) for value in (top, vfac, sfac))
            top_a, top_b = jnp.where(lower, top, got), jnp.where(lower, got, top)
            use_v, use_s = jnp.where(lower, got_v, vfac), jnp.where(lower, got_s, sfac)
            weight = mm(use_s.T, top_a + mm(use_v.T, top_b))
            top = jnp.where(lower, top_a - weight, top_b - mm(use_v, weight))
        root = top - mm(vfac, mm(sfac.T, mm(vfac.T, top)))
        work = jnp.concatenate([jnp.where(me == 0, root, top), work[width:]], axis=0)
    return work


def local(window, leaf_vecs, leaf_t, node_vecs, node_t):
    rows, cols = lax.axis_size("row"), lax.axis_size("col")
    width = leaf_t.shape[-1]
    panels = leaf_t.shape[0]
    height, ncols = window.shape
    chunks = CHUNKS if ncols % (CHUNKS * rows * 128) == 0 else 1
    span = ncols // chunks
    n = span // rows
    if n % 128 or panels != 2 or rows < 4:
        return butterfly(window, leaf_vecs, leaf_t, node_vecs, node_t)
    me = lax.axis_index("row").astype(jnp.int32)
    col = lax.axis_index("col").astype(jnp.int32)
    parts = 2 if cols % 2 == 0 else 1
    core = col % parts
    place = jnp.stack([me, core])

    vecs = lax.all_gather(leaf_vecs, "col", axis=1, tiled=True)
    share = width // parts
    pack = pl.pallas_call(
        pack_kernel,
        out_shape=jax.ShapeDtypeStruct((1, 2 * panels * share, width), F32),
        in_specs=[smem(), vmem(), vmem()],
        out_specs=vmem(),
        compiler_params=params(),
        cost_estimate=cost(0, 2**20),
        name="pack",
    )(place, node_vecs, node_t)
    steps = []
    for k in [1 << bit for bit in reversed(range(rows.bit_length() - 1))]:
        steps.append(swap(pack, "row", k))
        pack = jnp.stack([pack, steps[-1]], axis=1).reshape(-1, *pack.shape[1:])

    rows_m, send_m, rest_m, dmat = pl.pallas_call(
        prep_kernel,
        out_shape=(
            jax.ShapeDtypeStruct((2, 2 * width, height), BF16),
            jax.ShapeDtypeStruct((2, 2 * width, 2 * width), BF16),
            jax.ShapeDtypeStruct((2, height - width, 3 * width), BF16),
            jax.ShapeDtypeStruct((width, width), F32),
        ),
        in_specs=[vmem(), vmem(), vmem()],
        out_specs=(vmem(),) * 4,
        compiler_params=params(),
        cost_estimate=cost(40 * width**3 * 6, 2**21),
        name="prep",
    )(vecs, leaf_t, steps[0])

    def part(chunk, k):
        return lambda place, ref: ref.at[:, pl.ds(pl.multiple_of((chunk * rows + (place[0] ^ k)) * n, n), n)]

    def touch(value, after):
        if not after:
            return value
        return pl.pallas_call(
            touch_kernel,
            out_shape=jax.ShapeDtypeStruct(value.shape, value.dtype),
            in_specs=[vmem()] * (1 + len(after)),
            out_specs=vmem(),
            input_output_aliases={0: 0},
            compiler_params=params(),
            cost_estimate=cost(0, 0),
            name="touch",
        )(value, *after)

    def leaf(chunk, ks, after):
        count = len(ks)
        out = pl.pallas_call(
            functools.partial(leaf_kernel, [part(chunk, k) for k in ks]),
            in_specs=[smem(), hbm(), vmem(), vmem(), vmem()],
            out_specs=(vmem(),) * (1 + count),
            scratch_shapes=[pltpu.VMEM((count, height, n), F32), pltpu.SemaphoreType.DMA((count,))],
            out_shape=(jax.ShapeDtypeStruct((count, 2 * width, n), F32),)
            + (jax.ShapeDtypeStruct((2 * width, n), F32),) * count,
            compiler_params=params(LARGE_LIMIT if chunk == 0 and ks[0] == far[0] else VMEM_LIMIT),
            cost_estimate=cost(
                2 * 2 * width * (height + 2 * width) * n * count * 3, 4 * n * count * (height + 4 * width)
            ),
            name="leaf",
        )(place, window, rows_m, send_m, after)
        return out[0], list(out[1:])

    def nodes(pack, after):
        return pl.pallas_call(
            nodes_kernel,
            grid_spec=pltpu.PrefetchScalarGridSpec(
                num_scalar_prefetch=1,
                grid=(rows,),
                in_specs=[
                    pl.BlockSpec(after.shape, lambda r, place: (0, 0)),
                    pl.BlockSpec((parts, 1, *pack.shape[2:]), lambda r, place: (0, r ^ place[0], 0, 0)),
                ],
                out_specs=pl.BlockSpec((2, panels, 1, 2 * width, 2 * width), lambda r, place: (0, 0, r, 0, 0)),
            ),
            out_shape=jax.ShapeDtypeStruct((2, panels, rows, 2 * width, 2 * width), BF16),
            compiler_params=params(),
            cost_estimate=cost(rows * 12 * width**3 * 6, 2**23),
            name="nodes",
        )(place, after, pack)

    def tree(pairs, dmats, pieces):
        out = pl.pallas_call(
            functools.partial(tree_kernel, rows, order),
            out_shape=(jax.ShapeDtypeStruct((2 * width, n), F32),) * rows,
            in_specs=[smem()] + [vmem()] * (2 + rows),
            out_specs=(vmem(),) * rows,
            scratch_shapes=[pltpu.VMEM((rows, width, n), F32)] * 2,
            compiler_params=params(),
            cost_estimate=cost(rows * 8 * 4 * width * width * n * 3, 2**23),
            name="tree",
        )(place, pairs, dmats, *[pieces[k] for k in order])
        return [out[order.index(k)] for k in range(rows)]

    def last(chunk, ks, inner, begin, pieces, out):
        count = len(ks)
        operands = [place, window, inner, rest_m, *pieces]
        in_specs = [smem(), hbm()] + [vmem()] * (2 + count)
        aliases = {}
        if out is not None:
            in_specs.append(hbm())
            aliases = {len(operands): 0}
            operands.append(out)
        return pl.pallas_call(
            functools.partial(last_kernel, [part(chunk, k) for k in ks], begin),
            in_specs=in_specs,
            out_specs=hbm(),
            scratch_shapes=[
                pltpu.VMEM((count, height, n), F32),
                pltpu.VMEM((3 * width, n), F32),
                pltpu.SemaphoreType.DMA((2, count)),
            ],
            out_shape=jax.ShapeDtypeStruct(window.shape, F32),
            input_output_aliases=aliases,
            compiler_params=params(),
            cost_estimate=cost(
                2 * 3 * width * (height - width) * n * count * 3, 4 * n * count * (2 * height + 4 * width)
            ),
            name="last",
        )(*operands)

    half = rows // 2
    far, near = list(range(half, rows)), list(range(1, half))
    order = far + near + [0]
    cut = max(1, half // 2)

    inners, sent = {}, [[None] * rows for _ in range(chunks)]

    def leaves(chunk, ks, after):
        inner, made = leaf(chunk, ks, after)
        for i, k in enumerate(ks):
            inners[chunk, k] = inner, i
            sent[chunk][k] = made[i]
        return inner

    ride = far[RIDE]
    flat = share
    groups = max(1, n // width)
    extra = flat * width // n

    def fold(pack):
        return jnp.concatenate([pack[g * extra : (g + 1) * extra] for g in range(groups)], axis=1)

    def unfold(rider):
        return jnp.concatenate([rider[:, g * width : (g + 1) * width] for g in range(groups)], axis=0)

    fars, nears, queue = [], [], []

    def far_swap(value, k):
        needs = fars[len(fars) - FLIGHT :][:1] if len(fars) >= FLIGHT else []
        if STRICT:
            needs += nears[:-1]
            del nears[:-1]
        fars.append(swap(touch(value, needs), "row", k))
        return fars[-1]

    def near_trades(got, pieces):
        def run(k):
            got[k] = swap(pieces[k], "row", k)
            nears.append(got[k])

        return [functools.partial(run, k) for k in near]

    arrived = [[None] * rows for _ in range(chunks)]
    own = other = None
    for chunk in range(chunks):
        if chunk == 0:
            after = leaves(0, far[:cut], send_m)
            leaves(0, far[cut:], steps[min(1, len(steps) - 1)])
        else:
            leaves(chunk, far, fars[0])
            leaves(chunk, [0] + near, fars[0])
            arrived[chunk][0] = sent[chunk][0]
            for k in near:
                arrived[chunk][k] = swap(sent[chunk][k], "row", k)
        for k in far:
            if (chunk, k) == (0, ride):
                own = fold(lax.dynamic_slice_in_dim(dmat, core * share, share, axis=0))
                got = far_swap(jnp.concatenate([sent[0][k], own]), k)
                arrived[0][k], other = got[: 2 * width], got[2 * width :]
                leaves(0, [0] + near, fars[0])
                arrived[0][0] = sent[0][0]
                for j in near:
                    sent[0][j] = jnp.concatenate([sent[0][j], own, other])
                queue += near_trades(arrived[0], sent[0])
            else:
                arrived[chunk][k] = far_swap(sent[chunk][k], k)
            if queue:
                queue.pop(0)()

    while any(got is None for got in arrived[0]):
        queue.pop(0)()
    shares = {0: own, ride: other}
    for k in near:
        got = arrived[0][k]
        arrived[0][k] = got[: 2 * width]
        shares[k], shares[k ^ ride] = got[2 * width : 2 * width + extra], got[2 * width + extra :]
    shares = jnp.stack([unfold(shares[k]) for k in range(rows)])
    def join(value, after):
        if parts == 1:
            return value[None]
        return jnp.stack([value, swap(touch(value, after), "col", 1)])

    pace = [fars[min(i, len(fars) - 1)] for i in PACE]
    dmats = join(shares, [pace[2]])
    pack = join(pack, [pace[0]])

    pairs = None
    returned = []
    for chunk in range(chunks):
        while any(got is None for got in arrived[chunk]):
            queue.pop(0)()
        if chunk == 0:
            pairs = nodes(pack, pace[1])
        made = tree(pairs, dmats, arrived[chunk])
        returned.append([made[0]] + [None] * (rows - 1))
        queue += near_trades(returned[chunk], made)
        for k in far:
            if queue:
                queue.pop(0)()
            returned[chunk][k] = far_swap(made[k], k)
    while queue:
        queue.pop(0)()

    out = None
    for chunk in range(chunks):
        groups = [[0] + near, far]
        if chunk == chunks - 1:
            groups = [[0] + near, far[:cut]] + [[k] for k in far[cut:]]
        for ks in groups:
            ks = [k for k in ks if k < rows]
            if not ks:
                continue
            held = {}
            for k in ks:
                held.setdefault(id(inners[chunk, k][0]), []).append(k)
            for some in held.values():
                inner, begin = inners[chunk, some[0]]
                out = last(chunk, some, inner, begin, [returned[chunk][k] for k in some], out)
    return out


def solution(mesh):
    placed = (
        P("row", "col"),
        P(None, ("row", "col"), None),
        P(None, "row", None),
        P(None, "row", None),
        P(None, "row", None),
    )
    return jax.shard_map(
        local, mesh=mesh, in_specs=placed, out_specs=P("row", "col"), check_vma=False
    )
```

time: 257 us -> 235 us (0.914)
  waiting for transfers between devices: 131 us -> 95.5 us
  Pallas kernels: 50.9 us -> 63.2 us
  starting transfers between devices: 61.4 us -> 55.9 us
  local copies, waits for them, and re-layouts: 4.71 us -> 8.51 us
    ppermute x33, waiting for transfers between devices: 131 us -> 95.5 us  [swap(): lax.ppermute(value, axis, [(i, i ^ k) for i in range(lax.axis_size(axis))])]
    pallas_call x10 -> x29, Pallas kernels: 39.7 us -> 52.2 us  [the longest x7 22.4 us: last(): pl.pallas_call(functools.partial(last_kernel, [part(chunk, k) for k in ks...]
    ppermute x33, starting transfers between devices: 61.4 us -> 55.9 us  [swap(): lax.ppermute(value, axis, [(i, i ^ k) for i in range(lax.axis_size(axis))])]
    unnamed x12 -> x31, local copies, waits for them, and re-layouts: 4.3 us -> 8.3 us
  transfers between devices with their start and end apart: 33 -> 33, of which waited for: 19 -> 13; matrix products, arithmetic and copies ran while one was open for 0% -> 1% of each run, Pallas kernels for 16% -> 26%
where the time goes in v2:
time: 235 us; the launch traced here: 233 us
  waiting for transfers between devices  95.5 us (41%)
  Pallas kernels  63.2 us (27%)
  starting transfers between devices  55.9 us (24%)
  local copies, waits for them, and re-layouts  8.51 us (4%)
  blocking collectives  7.4 us (3%)
    ppermute x33, waiting for transfers between devices, swap(): lax.ppermute(value, axis, [(i, i ^ k) for i in range(lax.axis_size(axis))])  95.5 us
    ppermute x33, starting transfers between devices, swap(): lax.ppermute(value, axis, [(i, i ^ k) for i in range(lax.axis_size(axis))])  55.9 us
    pallas_call x7, Pallas kernels, last(): pl.pallas_call(functools.partial(last_kernel, [part(chunk, k) for k in ks...  22.4 us
    pallas_call x5, Pallas kernels, leaf(): pl.pallas_call(functools.partial(leaf_kernel, [part(chunk, k) for k in ks...  20.8 us
    pallas_call x2, Pallas kernels, tree(): pl.pallas_call(functools.partial(tree_kernel, rows, order), out_shape=(ja...  9.11 us
    unnamed x31, local copies, waits for them, and re-layouts  8.3 us
    pallas_call x1, Pallas kernels, nodes(): pl.pallas_call(nodes_kernel, grid_spec=pltpu.PrefetchScalarGridSpec(num_s...  7.82 us
    all_gather x1, blocking collectives, local(): vecs = lax.all_gather(leaf_vecs, 'col', axis=1, tiled=True)  7.4 us
  transfers between devices with their start and end apart: 33, of which 13 were waited for; matrix products, arithmetic and copies ran while one was open for 1% of the time, Pallas kernels for 26%

profile of v2, /device:TPU:8, one launch (start us, length us, event | category | flops | bytes accessed | tf_op | source)
XLA Modules:
  0.0 232.8 jit_solution(17794506868991302250)
XLA Ops:
  0.1 0.9 copy-done.6
  1.0 0.9 copy-done.7
  1.9 0.6 pack.1
  2.4 2.7 %collective-permute-start = (f32[1,256,128]{2,1,0:T(8,128)S(1)}, f32[1,256,128]{2,1,0:T(8,128)S(1)}, u32[]{:S(2)}, u32[]{:S(2)}) collective-permute-start(f32[1,256,128]{2,1,0:T(8,128)S(1)} %pack.1), channel_id=1, source_target_pairs={{0,16},{4,20},{8,24},{12,28},{16,0},{20,4},{24,8},{28,12},{1,17},{... | collective-permute-start | bytes 393224 | tf_op jit(solution)/shard_map/ppermute | solution.py:229
  5.1 7.4 %all_gather.3.vecs_ref = f32[2,512,128]{2,1,0:T(8,128)S(1)} all-gather(f32[2,128,128]{2,1,0:T(8,128)} %param.6), channel_id=1, replica_groups=mesh['row'=8,'col'=4] {'col'}, dimensions={1}, use_global_device_ids=true | all-gather | bytes 655360 | tf_op jit(solution)/shard_map/all_gather | solution.py:270
  12.5 0.5 collective-permute-start.2
  13.1 0.9 copy-done.11
  14.0 1.9 prep.1
  15.9 0.8 copy-done.1
  16.7 0.7 copy-done.3
  17.4 4.8 %leaf.5 = (f32[2,256,256]{2,1,0:T(8,128)}, f32[256,256]{1,0:T(8,128)}, f32[256,256]{1,0:T(8,128)}) custom-call(s32[2]{0:T(128)} %copy-done.8, f32[512,4096]{1,0:T(8,128)} %window_ref.23, bf16[2,256,512]{2,1,0:T(8,128)(2,1)} %copy-done.1, bf16[2,256,256]{2,1,0:T(8,128)(2,1)} %copy-done.3, bf16[2,256,256]{2,1,0:T(8,128)(2,1)} %copy-done.3), custom_call_target="tpu_custom_call" | custom-call | flops 603979776 | bytes 2097152 | tf_op jit(solution)/shard_map/leaf/pallas_call | solution.py:320
  22.2 2.0 collective-permute-start.9
  24.2 1.0 maximum_maximum_fusion
  25.1 2.0 collective-permute-start.1
  27.2 0.6 collective-permute-start.4
  27.8 3.4 %copy-done = f32[512,4096]{1,0:T(8,128)S(1)} copy-done((f32[512,4096]{1,0:T(8,128)S(1)}, f32[512,4096]{1,0:T(8,128)}, u32[]{:S(2)}) %copy-start) | copy-done | bytes 8388632
  31.2 0.6 copy-done.9
  31.8 2.6 %leaf.7 = (f32[2,256,256]{2,1,0:T(8,128)S(1)}, f32[256,256]{1,0:T(8,128)S(1)}, f32[256,256]{1,0:T(8,128)S(1)}) custom-call(s32[2]{0:T(128)S(1)} %copy-done.9, f32[512,4096]{1,0:T(8,128)S(1)} %copy-done, bf16[2,256,512]{2,1,0:T(8,128)(2,1)S(1)} %copy-done.2, bf16[2,256,256]{2,1,0:T(8,128)(2,1)S(1)} %copy-done.4, ...), custom_call_target="tpu_custom_call" | custom-call | flops 603979776 | bytes 2097152 | tf_op jit(solution)/shard_map/leaf/pallas_call | solution.py:320
  34.5 1.6 collective-permute-start.3
  36.1 18.9 %collective-permute-done.1.after_ref.refs_1_ = f32[288,256]{1,0:T(8,128)S(1)} collective-permute-done((f32[288,256]{1,0:T(8,128)S(1)}, f32[288,256]{1,0:T(8,128)S(1)}, u32[]{:S(2)}, u32[]{:S(2)}) %collective-permute-start.1) | collective-permute-done | bytes 294944 | tf_op jit(solution)/shard_map/ppermute | solution.py:229
  55.0 1.2 collective-permute-start.13
  56.1 4.4 %leaf.8 = (f32[4,256,256]{2,1,0:T(8,128)S(1)}, f32[256,256]{1,0:T(8,128)S(1)}, f32[256,256]{1,0:T(8,128)S(1)}, f32[256,256]{1,0:T(8,128)S(1)}, f32[256,256]{1,0:T(8,128)S(1)}) custom-call(s32[2]{0:T(128)S(1)} %copy-done.10, f32[512,4096]{1,0:T(8,128)S(1)} %copy-done, bf16[2,256,512]{2,1,0:T(8,128)(2,1)S(1)} %copy-done.2, bf16[2,256,256]{2,1,0:T(8,128)(2,1)S(1)} %copy-done.4, ...), custom_call_target="tpu_custom_call" | custom-call | flops 1207959552 | bytes 4194304 | tf_op jit(solution)/shard_map/leaf/pallas_call | solution.py:320
  60.6 1.6 collective-permute-start.6
  62.2 4.4 %leaf.6 = (f32[4,256,256]{2,1,0:T(8,128)S(1)}, f32[256,256]{1,0:T(8,128)S(1)}, f32[256,256]{1,0:T(8,128)S(1)}, f32[256,256]{1,0:T(8,128)S(1)}, f32[256,256]{1,0:T(8,128)S(1)}) custom-call(s32[2]{0:T(128)S(1)} %copy-done.10, f32[512,4096]{1,0:T(8,128)S(1)} %copy-done, bf16[2,256,512]{2,1,0:T(8,128)(2,1)S(1)} %copy-done.2, bf16[2,256,256]{2,1,0:T(8,128)(2,1)S(1)} %copy-done.4, ...), custom_call_target="tpu_custom_call" | custom-call | flops 1207959552 | bytes 4194304 | tf_op jit(solution)/shard_map/leaf/pallas_call | solution.py:320
  66.6 3.8 %collective-permute-start.8 = (f32[320,256]{1,0:T(8,128)S(1)}, f32[320,256]{1,0:T(8,128)S(1)}, u32[]{:S(2)}, u32[]{:S(2)}) collective-permute-start(f32[320,256]{1,0:T(8,128)S(1)} %get-tuple-element.103), channel_id=1, source_target_pairs={{0,12},{4,8},{8,4},{12,0},{16,28},{20,24},{24,20},{28,16},{1,13},{... | collective-permute-start | bytes 983048 | tf_op jit(solution)/shard_map/ppermute | solution.py:229
  70.4 12.2 %collective-permute-done.6 = f32[320,256]{1,0:T(8,128)S(1)} collective-permute-done((f32[320,256]{1,0:T(8,128)S(1)}, f32[320,256]{1,0:T(8,128)S(1)}, u32[]{:S(2)}, u32[]{:S(2)}) %collective-permute-start.6) | collective-permute-done | bytes 327712 | tf_op jit(solution)/shard_map/ppermute | solution.py:229
  82.6 0.5 collective-permute-start.7
  83.1 1.4 collective-permute-start.10
  84.5 11.4 %collective-permute-done.7 = f32[320,256]{1,0:T(8,128)S(1)} collective-permute-done((f32[320,256]{1,0:T(8,128)S(1)}, f32[320,256]{1,0:T(8,128)S(1)}, u32[]{:S(2)}, u32[]{:S(2)}) %collective-permute-start.7) | collective-permute-done | bytes 327712 | tf_op jit(solution)/shard_map/ppermute | solution.py:229
  96.5 0.5 collective-permute-start.11
  97.3 3.4 %collective-permute-start.14 = (f32[256,256]{1,0:T(8,128)S(1)}, f32[256,256]{1,0:T(8,128)S(1)}, u32[]{:S(2)}, u32[]{:S(2)}) collective-permute-start(f32[256,256]{1,0:T(8,128)S(1)} %touch.20), channel_id=1, source_target_pairs={{0,24},{4,28},{8,16},{12,20},{16,8},{20,12},{24,0},{28,4},{1,25},{... | collective-permute-start | bytes 786440 | tf_op jit(solution)/shard_map/ppermute | solution.py:229
  100.7 1.5 collective-permute-start.15
  102.6 7.8 %nodes.1.pair_ref = bf16[2,2,8,256,256]{4,3,2,1,0:T(8,128)(2,1)S(1)} custom-call(s32[2]{0:T(128)S(1)} %copy-done.10, f32[256,256]{1,0:T(8,128)S(1)} %collective-permute-done.3.after_ref.refs_1_.refs_2_, f32[2,8,256,128]{3,2,1,0:T(8,128)S(1)} %pad_maximum_fusion.pack_ref), custom_call_target="tpu_custom_call" | custom-call | flops 1207959552 | bytes 8388608 | tf_op jit(solution)/shard_map/nodes/pallas_call | solution.py:336
  110.4 4.6 %tree.3 = (f32[256,256]{1,0:T(8,128)S(1)}, f32[256,256]{1,0:T(8,128)S(1)}, f32[256,256]{1,0:T(8,128)S(1)}, f32[256,256]{1,0:T(8,128)S(1)}, f32[256,256]{1,0:T(8,...) custom-call(s32[2]{0:T(128)S(1)} %copy-done.10, ...), custom_call_target="tpu_custom_call" | custom-call | flops 3221225472 | bytes 8388608 | tf_op jit(solution)/shard_map/tree/pallas_call | solution.py:354
  115.0 5.7 %collective-permute-done.12.refs_1_ = f32[256,256]{1,0:T(8,128)S(1)} collective-permute-done((f32[256,256]{1,0:T(8,128)S(1)}, f32[256,256]{1,0:T(8,128)S(1)}, u32[]{:S(2)}, u32[]{:S(2)}) %collective-permute-start.12) | collective-permute-done | bytes 262176 | tf_op jit(solution)/shard_map/ppermute | solution.py:229
  120.7 4.5 %collective-permute-start.22 = (f32[256,256]{1,0:T(8,128)S(1)}, f32[256,256]{1,0:T(8,128)S(1)}, u32[]{:S(2)}, u32[]{:S(2)}) collective-permute-start(f32[256,256]{1,0:T(8,128)S(1)} %touch.25), channel_id=1, source_target_pairs={{0,16},{4,20},{8,24},{12,28},{16,0},{20,4},{24,8},{28,12},{1,17},{... | collective-permute-start | bytes 786440 | tf_op jit(solution)/shard_map/ppermute | solution.py:229
  125.3 4.6 %leaf.9 = (f32[4,256,256]{2,1,0:T(8,128)S(1)}, f32[256,256]{1,0:T(8,128)S(1)}, f32[256,256]{1,0:T(8,128)S(1)}, f32[256,256]{1,0:T(8,128)S(1)}, f32[256,256]{1,0:T(8,128)S(1)}) custom-call(s32[2]{0:T(128)S(1)} %copy-done.10, f32[512,4096]{1,0:T(8,128)S(1)} %bitcast.48, bf16[2,256,512]{2,1,0:T(8,128)(2,1)S(1)} %copy-done.2, ...), custom_call_target="tpu_custom_call" | custom-call | flops 1207959552 | bytes 4194304 | tf_op jit(solution)/shard_map/leaf/pallas_call | solution.py:320
  129.9 0.4 collective-permute-start.16
  130.3 0.2 collective-permute-start.17
  130.5 2.5 %collective-permute-done.14.refs_2_.refs_1_ = f32[256,256]{1,0:T(8,128)S(1)} collective-permute-done((f32[256,256]{1,0:T(8,128)S(1)}, f32[256,256]{1,0:T(8,128)S(1)}, u32[]{:S(2)}, u32[]{:S(2)}) %collective-permute-start.14) | collective-permute-done | bytes 262176 | tf_op jit(solution)/shard_map/ppermute | solution.py:229
  133.0 0.4 collective-permute-start.18
  133.5 11.3 %collective-permute-done.15.refs_3_.refs_1_ = f32[256,256]{1,0:T(8,128)S(1)} collective-permute-done((f32[256,256]{1,0:T(8,128)S(1)}, f32[256,256]{1,0:T(8,128)S(1)}, u32[]{:S(2)}, u32[]{:S(2)}) %collective-permute-start.15) | collective-permute-done | bytes 262176 | tf_op jit(solution)/shard_map/ppermute | solution.py:229
  145.0 8.6 %collective-permute-done.16.refs_4_ = f32[256,256]{1,0:T(8,128)S(1)} collective-permute-done((f32[256,256]{1,0:T(8,128)S(1)}, f32[256,256]{1,0:T(8,128)S(1)}, u32[]{:S(2)}, u32[]{:S(2)}) %collective-permute-start.16) | collective-permute-done | bytes 262176 | tf_op jit(solution)/shard_map/ppermute | solution.py:229
  153.6 3.6 %collective-permute-start.31 = (f32[256,256]{1,0:T(8,128)S(1)}, f32[256,256]{1,0:T(8,128)S(1)}, u32[]{:S(2)}, u32[]{:S(2)}) collective-permute-start(f32[256,256]{1,0:T(8,128)S(1)} %get-tuple-element.85), channel_id=1, source_target_pairs={{0,8},{4,12},{8,0},{12,4},{16,24},{20,28},{24,16},{28,20},{1,9},{5... | collective-permute-start | bytes 786440 | tf_op jit(solution)/shard_map/ppermute | solution.py:229
  157.2 1.5 collective-permute-start.23
  158.7 4.5 %tree.2 = (f32[256,256]{1,0:T(8,128)S(1)}, f32[256,256]{1,0:T(8,128)S(1)}, f32[256,256]{1,0:T(8,128)S(1)}, f32[256,256]{1,0:T(8,128)S(1)}, f32[256,256]{1,0:T(8,...) custom-call(s32[2]{0:T(128)S(1)} %copy-done.10, ...), custom_call_target="tpu_custom_call" | custom-call | flops 3221225472 | bytes 8388608 | tf_op jit(solution)/shard_map/tree/pallas_call | solution.py:354
  163.3 2.7 %collective-permute-start.20 = (f32[256,256]{1,0:T(8,128)S(1)}, f32[256,256]{1,0:T(8,128)S(1)}, u32[]{:S(2)}, u32[]{:S(2)}) collective-permute-start(f32[256,256]{1,0:T(8,128)S(1)} %touch.23), channel_id=1, source_target_pairs={{0,16},{4,20},{8,24},{12,28},{16,0},{20,4},{24,8},{28,12},{1,17},{... | collective-permute-start | bytes 786440 | tf_op jit(solution)/shard_map/ppermute | solution.py:229
  166.0 0.8 collective-permute-start.32
  166.8 10.3 %collective-permute-start.27 = (f32[256,256]{1,0:T(8,128)S(1)}, f32[256,256]{1,0:T(8,128)S(1)}, u32[]{:S(2)}, u32[]{:S(2)}) collective-permute-start(f32[256,256]{1,0:T(8,128)S(1)} %get-tuple-element.77), channel_id=1, source_target_pairs={{0,4},{4,0},{8,12},{12,8},{16,20},{20,16},{24,28},{28,24},{1,5},{5... | collective-permute-start | bytes 786440 | tf_op jit(solution)/shard_map/ppermute | solution.py:229
  177.1 6.2 %collective-permute-done.25.refs_1_.refs_0_ = f32[256,256]{1,0:T(8,128)S(1)} collective-permute-done((f32[256,256]{1,0:T(8,128)S(1)}, f32[256,256]{1,0:T(8,128)S(1)}, u32[]{:S(2)}, u32[]{:S(2)}) %collective-permute-start.25) | collective-permute-done | bytes 262176 | tf_op jit(solution)/shard_map/ppermute | solution.py:229
  183.3 8.1 %collective-permute-done.23.refs_1_ = f32[256,256]{1,0:T(8,128)S(1)} collective-permute-done((f32[256,256]{1,0:T(8,128)S(1)}, f32[256,256]{1,0:T(8,128)S(1)}, u32[]{:S(2)}, u32[]{:S(2)}) %collective-permute-start.23) | collective-permute-done | bytes 262176 | tf_op jit(solution)/shard_map/ppermute | solution.py:229
  191.5 1.3 collective-permute-done.20.refs_1_.refs_0_
  192.8 3.5 %collective-permute-start.26 = (f32[256,256]{1,0:T(8,128)S(1)}, f32[256,256]{1,0:T(8,128)S(1)}, u32[]{:S(2)}, u32[]{:S(2)}) collective-permute-start(f32[256,256]{1,0:T(8,128)S(1)} %touch.29), channel_id=1, source_target_pairs={{0,20},{4,16},{8,28},{12,24},{16,4},{20,0},{24,12},{28,8},{1,21},{... | collective-permute-start | bytes 786440 | tf_op jit(solution)/shard_map/ppermute | solution.py:229
  196.4 4.5 %collective-permute-start.24 = (f32[256,256]{1,0:T(8,128)S(1)}, f32[256,256]{1,0:T(8,128)S(1)}, u32[]{:S(2)}, u32[]{:S(2)}) collective-permute-start(f32[256,256]{1,0:T(8,128)S(1)} %touch.27), channel_id=1, source_target_pairs={{0,24},{4,28},{8,16},{12,20},{16,8},{20,12},{24,0},{28,4},{1,25},{... | collective-permute-start | bytes 786440 | tf_op jit(solution)/shard_map/ppermute | solution.py:229
  200.9 3.5 %collective-permute-done.27.refs_1_ = f32[256,256]{1,0:T(8,128)S(1)} collective-permute-done((f32[256,256]{1,0:T(8,128)S(1)}, f32[256,256]{1,0:T(8,128)S(1)}, u32[]{:S(2)}, u32[]{:S(2)}) %collective-permute-start.27) | collective-permute-done | bytes 262176 | tf_op jit(solution)/shard_map/ppermute | solution.py:229
  204.3 4.7 %last.7.refs_2_ = f32[512,4096]{1,0:T(8,128)} custom-call(s32[2]{0:T(128)S(1)} %copy-done.10, f32[512,4096]{1,0:T(8,128)S(1)} %bitcast.48, f32[4,256,256]{2,1,0:T(8,128)S(1)} %get-tuple-element.82.inner_ref, bf16[2,384,384]{2,1,0:T(8,128)(2,1)S(1)} %get-tuple-element.51.rest_ref, f32[256,256]{1,0:T(8,128)S(1)} %get-tuple-element.83.refs_0_, ...), custom_call_target="tpu_custom_call" | custom-call | flops 905969664 | bytes 6291456 | tf_op jit(solution)/shard_map/last/pallas_call | solution.py:375
  209.0 3.1 %last.8.refs_2_ = f32[512,4096]{1,0:T(8,128)} custom-call(s32[2]{0:T(128)S(1)} %copy-done.10, f32[512,4096]{1,0:T(8,128)S(1)} %bitcast.48, f32[2,256,256]{2,1,0:T(8,128)S(1)} %copy-done.5, bf16[2,384,384]{2,1,0:T(8,128)(2,1)S(1)} %get-tuple-element.51.rest_ref, ...), custom_call_target="tpu_custom_call", output_to_operand_aliasing={{}: (6, {})} | custom-call | flops 452984832 | bytes 3145728 | tf_op jit(solution)/shard_map/last/pallas_call | solution.py:375
  212.1 3.1 %last.9.refs_4_ = f32[512,4096]{1,0:T(8,128)} custom-call(s32[2]{0:T(128)S(1)} %copy-done.10, f32[512,4096]{1,0:T(8,128)S(1)} %bitcast.48, f32[2,256,256]{2,1,0:T(8,128)S(1)} %get-tuple-element.80.inner_ref, bf16[2,384,384]{2,1,0:T(8,128)(2,1)S(1)} %get-tuple-element.51.rest_ref, ...), custom_call_target="tpu_custom_call", output_to_operand_aliasing={{}: (6, {})} | custom-call | flops 452984832 | bytes 3145728 | tf_op jit(solution)/shard_map/last/pallas_call | solution.py:375
  215.2 4.7 %last.10.refs_2_ = f32[512,4096]{1,0:T(8,128)} custom-call(s32[2]{0:T(128)S(1)} %copy-done.10, f32[512,4096]{1,0:T(8,128)S(1)} %bitcast.48, f32[4,256,256]{2,1,0:T(8,128)S(1)} %get-tuple-element.75.inner_ref, bf16[2,384,384]{2,1,0:T(8,128)(2,1)S(1)} %get-tuple-element.51.rest_ref, ...), custom_call_target="tpu_custom_call", output_to_operand_aliasing={{}: (8, {})} | custom-call | flops 905969664 | bytes 6291456 | tf_op jit(solution)/shard_map/last/pallas_call | solution.py:375
  220.0 3.1 %last.11.refs_1_ = f32[512,4096]{1,0:T(8,128)} custom-call(s32[2]{0:T(128)S(1)} %copy-done.10, f32[512,4096]{1,0:T(8,128)S(1)} %bitcast.48, f32[4,256,256]{2,1,0:T(8,128)S(1)} %get-tuple-element.50.inner_ref, bf16[2,384,384]{2,1,0:T(8,128)(2,1)S(1)} %get-tuple-element.51.rest_ref, ...), custom_call_target="tpu_custom_call", output_to_operand_aliasing={{}: (6, {})} | custom-call | flops 452984832 | bytes 3145728 | tf_op jit(solution)/shard_map/last/pallas_call | solution.py:375
  223.0 4.1 %collective-permute-done.24.refs_0_ = f32[256,256]{1,0:T(8,128)S(1)} collective-permute-done((f32[256,256]{1,0:T(8,128)S(1)}, f32[256,256]{1,0:T(8,128)S(1)}, u32[]{:S(2)}, u32[]{:S(2)}) %collective-permute-start.24) | collective-permute-done | bytes 262176 | tf_op jit(solution)/shard_map/ppermute | solution.py:229
  227.1 1.9 last.12.refs_1_
  229.0 1.7 collective-permute-done.21.refs_0_
  230.7 1.9 last.13
  (94 shorter events, 1.9 us)
Async XLA Ops:
  0.1 0.9 copy-start.6
  1.0 0.9 copy-start.7
  1.9 15.5 %copy-start.8 = (s32[2]{0:T(128)}, s32[2]{0:T(128)S(1)}, u32[]{:S(2)}) copy-start(s32[2]{0:T(128)S(1)} %pad_add_fusion.place_ref) | copy-start | bytes 28
  2.4 10.1 %collective-permute-start = (f32[1,256,128]{2,1,0:T(8,128)S(1)}, f32[1,256,128]{2,1,0:T(8,128)S(1)}, u32[]{:S(2)}, u32[]{:S(2)}) collective-permute-start(f32[1,256,128]{2,1,0:T(8,128)S(1)} %pack.1), channel_id=1, source_target_pairs={{0,16},{4,20},{8,24},{12,28},{16,0},{20,4},{24,8},{28,12},{1,17},{... | collective-permute-start | bytes 393224 | tf_op jit(solution)/shard_map/ppermute | solution.py:229
  12.5 14.6 %collective-permute-start.2 = (f32[2,256,128]{2,1,0:T(8,128)S(1)}, f32[2,256,128]{2,1,0:T(8,128)S(1)}, u32[]{:S(2)}, u32[]{:S(2)}) collective-permute-start(f32[2,256,128]{2,1,0:T(8,128)S(1)} %get-tuple-element.102), channel_id=1, source_target_pairs={{0,8},{4,12},{8,0},{12,4},{16,24},{20,28},{24,16},{28,20},{1,9},{5... | collective-permute-start | bytes 786440 | tf_op jit(solution)/shard_map/ppermute | solution.py:229
  13.1 0.9 copy-start.11
  15.9 0.8 copy-start.1
  16.7 0.7 copy-start.3
  17.4 10.5 %copy-start.2 = (bf16[2,256,512]{2,1,0:T(8,128)(2,1)S(1)}, bf16[2,256,512]{2,1,0:T(8,128)(2,1)}, u32[]{:S(2)}) copy-start(bf16[2,256,512]{2,1,0:T(8,128)(2,1)} %copy-done.1) | copy-start | bytes 1572868
  17.4 10.5 %copy-start.4 = (bf16[2,256,256]{2,1,0:T(8,128)(2,1)S(1)}, bf16[2,256,256]{2,1,0:T(8,128)(2,1)}, u32[]{:S(2)}) copy-start(bf16[2,256,256]{2,1,0:T(8,128)(2,1)} %copy-done.3) | copy-start | bytes 786436
  22.2 34.0 %copy-start.10 = (s32[2]{0:T(128)S(1)}, s32[2]{0:T(128)}, u32[]{:S(2)}) copy-start(s32[2]{0:T(128)} %copy-done.8) | copy-start | bytes 28
  22.2 44.4 %collective-permute-start.9 = (f32[256,256]{1,0:T(8,128)}, f32[256,256]{1,0:T(8,128)S(1)}, u32[]{:S(2)}, u32[]{:S(2)}) collective-permute-start(f32[256,256]{1,0:T(8,128)} %get-tuple-element.57), channel_id=1, source_target_pairs={{0,20},{4,16},{8,28},{12,24},{16,4},{20,0},{24,12},{28,8},{1,21},{... | collective-permute-start | bytes 786440 | tf_op jit(solution)/shard_map/ppermute | solution.py:229
  25.1 29.8 %collective-permute-start.1 = (f32[288,256]{1,0:T(8,128)S(1)}, f32[288,256]{1,0:T(8,128)S(1)}, u32[]{:S(2)}, u32[]{:S(2)}) collective-permute-start(f32[288,256]{1,0:T(8,128)S(1)} %maximum_maximum_fusion), channel_id=1, source_target_pairs={{0,16},{4,20},{8,24},{12,28},{16,0},{20,4},{24,8},{28,12},{1,17},{... | collective-permute-start | bytes 884744 | tf_op jit(solution)/shard_map/ppermute | solution.py:229
  27.2 68.7 %collective-permute-start.4 = (f32[4,256,128]{2,1,0:T(8,128)S(1)}, f32[4,256,128]{2,1,0:T(8,128)S(1)}, u32[]{:S(2)}, u32[]{:S(2)}) collective-permute-start(f32[4,256,128]{2,1,0:T(8,128)S(1)} %bitcast.54), channel_id=1, source_target_pairs={{0,4},{4,0},{8,12},{12,8},{16,20},{20,16},{24,28},{28,24},{1,5},{5... | collective-permute-start | bytes 1572872 | tf_op jit(solution)/shard_map/ppermute | solution.py:229
  27.8 3.4 %copy-start = (f32[512,4096]{1,0:T(8,128)S(1)}, f32[512,4096]{1,0:T(8,128)}, u32[]{:S(2)}) copy-start(f32[512,4096]{1,0:T(8,128)} %window_ref.23) | copy-start | bytes 25165828
  31.2 0.6 copy-start.9
  34.5 62.6 %collective-permute-start.3 = (f32[256,256]{1,0:T(8,128)S(1)}, f32[256,256]{1,0:T(8,128)S(1)}, u32[]{:S(2)}, u32[]{:S(2)}) collective-permute-start(f32[256,256]{1,0:T(8,128)S(1)} %get-tuple-element.52), channel_id=1, source_target_pairs={{0,24},{4,28},{8,16},{12,20},{16,8},{20,12},{24,0},{28,4},{1,25},{... | collective-permute-start | bytes 786440 | tf_op jit(solution)/shard_map/ppermute | solution.py:229
  55.0 42.2 %collective-permute-start.13 = (f32[256,256]{1,0:T(8,128)S(1)}, f32[256,256]{1,0:T(8,128)S(1)}, u32[]{:S(2)}, u32[]{:S(2)}) collective-permute-start(f32[256,256]{1,0:T(8,128)S(1)} %touch.19), channel_id=1, source_target_pairs={{0,28},{4,24},{8,20},{12,16},{16,12},{20,8},{24,4},{28,0},{1,29},{... | collective-permute-start | bytes 786440 | tf_op jit(solution)/shard_map/ppermute | solution.py:229
  60.6 22.0 %collective-permute-start.6 = (f32[320,256]{1,0:T(8,128)S(1)}, f32[320,256]{1,0:T(8,128)S(1)}, u32[]{:S(2)}, u32[]{:S(2)}) collective-permute-start(f32[320,256]{1,0:T(8,128)S(1)} %get-tuple-element.105), channel_id=1, source_target_pairs={{0,4},{4,0},{8,12},{12,8},{16,20},{20,16},{24,28},{28,24},{1,5},{5... | collective-permute-start | bytes 983048 | tf_op jit(solution)/shard_map/ppermute | solution.py:229
  66.6 16.5 %collective-permute-start.8 = (f32[320,256]{1,0:T(8,128)S(1)}, f32[320,256]{1,0:T(8,128)S(1)}, u32[]{:S(2)}, u32[]{:S(2)}) collective-permute-start(f32[320,256]{1,0:T(8,128)S(1)} %get-tuple-element.103), channel_id=1, source_target_pairs={{0,12},{4,8},{8,4},{12,0},{16,28},{20,24},{24,20},{28,16},{1,13},{... | collective-permute-start | bytes 983048 | tf_op jit(solution)/shard_map/ppermute | solution.py:229
  82.6 13.3 %collective-permute-start.7 = (f32[320,256]{1,0:T(8,128)S(1)}, f32[320,256]{1,0:T(8,128)S(1)}, u32[]{:S(2)}, u32[]{:S(2)}) collective-permute-start(f32[320,256]{1,0:T(8,128)S(1)} %get-tuple-element.104), channel_id=1, source_target_pairs={{0,8},{4,12},{8,0},{12,4},{16,24},{20,28},{24,16},{28,20},{1,9},{5... | collective-permute-start | bytes 983048 | tf_op jit(solution)/shard_map/ppermute | solution.py:229
  83.1 13.4 %collective-permute-start.10 = (f32[256,256]{1,0:T(8,128)S(1)}, f32[256,256]{1,0:T(8,128)S(1)}, u32[]{:S(2)}, u32[]{:S(2)}) collective-permute-start(f32[256,256]{1,0:T(8,128)S(1)} %touch.16), channel_id=1, source_target_pairs={{0,16},{4,20},{8,24},{12,28},{16,0},{20,4},{24,8},{28,12},{1,17},{... | collective-permute-start | bytes 786440 | tf_op jit(solution)/shard_map/ppermute | solution.py:229
  96.3 6.1 %collective-permute-start.5 = (f32[8,256,128]{2,1,0:T(8,128)S(1)}, f32[8,256,128]{2,1,0:T(8,128)S(1)}, u32[]{:S(2)}, u32[]{:S(2)}) collective-permute-start(f32[8,256,128]{2,1,0:T(8,128)S(1)} %touch.15), channel_id=1, source_target_pairs={{0,1},{1,0},{2,3},{3,2},{4,5},{5,4},{6,7},{7,6},{8,9},{9,8},{10,11... | collective-permute-start | bytes 3145736 | tf_op jit(solution)/shard_map/ppermute | solution.py:229
  96.5 5.8 %collective-permute-start.11 = (f32[8,64,128]{2,1,0:T(8,128)S(1)}, f32[8,64,128]{2,1,0:T(8,128)S(1)}, u32[]{:S(2)}, u32[]{:S(2)}) collective-permute-start(f32[8,64,128]{2,1,0:T(8,128)S(1)} %touch.17), channel_id=1, source_target_pairs={{0,1},{1,0},{2,3},{3,2},{4,5},{5,4},{6,7},{7,6},{8,9},{9,8},{10,11... | collective-permute-start | bytes 786440 | tf_op jit(solution)/shard_map/ppermute | solution.py:229
  97.1 23.6 %collective-permute-start.12 = (f32[256,256]{1,0:T(8,128)S(1)}, f32[256,256]{1,0:T(8,128)S(1)}, u32[]{:S(2)}, u32[]{:S(2)}) collective-permute-start(f32[256,256]{1,0:T(8,128)S(1)} %touch.18), channel_id=1, source_target_pairs={{0,20},{4,16},{8,28},{12,24},{16,4},{20,0},{24,12},{28,8},{1,21},{... | collective-permute-start | bytes 786440 | tf_op jit(solution)/shard_map/ppermute | solution.py:229
  97.3 35.8 %collective-permute-start.14 = (f32[256,256]{1,0:T(8,128)S(1)}, f32[256,256]{1,0:T(8,128)S(1)}, u32[]{:S(2)}, u32[]{:S(2)}) collective-permute-start(f32[256,256]{1,0:T(8,128)S(1)} %touch.20), channel_id=1, source_target_pairs={{0,24},{4,28},{8,16},{12,20},{16,8},{20,12},{24,0},{28,4},{1,25},{... | collective-permute-start | bytes 786440 | tf_op jit(solution)/shard_map/ppermute | solution.py:229
  100.7 44.1 %collective-permute-start.15 = (f32[256,256]{1,0:T(8,128)S(1)}, f32[256,256]{1,0:T(8,128)S(1)}, u32[]{:S(2)}, u32[]{:S(2)}) collective-permute-start(f32[256,256]{1,0:T(8,128)S(1)} %touch.21), channel_id=1, source_target_pairs={{0,28},{4,24},{8,20},{12,16},{16,12},{20,8},{24,4},{28,0},{1,29},{... | collective-permute-start | bytes 786440 | tf_op jit(solution)/shard_map/ppermute | solution.py:229
  102.6 22.7 %slice-start = ((s8[8388608]{0:T(1024)(128)(4,1)}), s8[4194304]{0:T(1024)(128)(4,1)S(1)}, s32[]{:S(2)}) async-start(s8[8388608]{0:T(1024)(128)(4,1)} %bitcast.47), calls=%async_computation | async-start | bytes 8388608
  110.4 14.8 %slice-start.1 = ((s8[8388608]{0:T(1024)(128)(4,1)}), s8[4194304]{0:T(1024)(128)(4,1)S(1)}, s32[]{:S(2)}) async-start(s8[8388608]{0:T(1024)(128)(4,1)} %bitcast.47), calls=%async_computation.1 | async-start | bytes 8388608
  120.7 24.1 %collective-permute-start.22 = (f32[256,256]{1,0:T(8,128)S(1)}, f32[256,256]{1,0:T(8,128)S(1)}, u32[]{:S(2)}, u32[]{:S(2)}) collective-permute-start(f32[256,256]{1,0:T(8,128)S(1)} %touch.25), channel_id=1, source_target_pairs={{0,16},{4,20},{8,24},{12,28},{16,0},{20,4},{24,8},{28,12},{1,17},{... | collective-permute-start | bytes 786440 | tf_op jit(solution)/shard_map/ppermute | solution.py:229
  129.9 23.7 %collective-permute-start.16 = (f32[256,256]{1,0:T(8,128)S(1)}, f32[256,256]{1,0:T(8,128)S(1)}, u32[]{:S(2)}, u32[]{:S(2)}) collective-permute-start(f32[256,256]{1,0:T(8,128)S(1)} %get-tuple-element.62), channel_id=1, source_target_pairs={{0,4},{4,0},{8,12},{12,8},{16,20},{20,16},{24,28},{28,24},{1,5},{5... | collective-permute-start | bytes 786440 | tf_op jit(solution)/shard_map/ppermute | solution.py:229
  130.3 26.9 %collective-permute-start.17 = (f32[256,256]{1,0:T(8,128)S(1)}, f32[256,256]{1,0:T(8,128)S(1)}, u32[]{:S(2)}, u32[]{:S(2)}) collective-permute-start(f32[256,256]{1,0:T(8,128)S(1)} %get-tuple-element.63), channel_id=1, source_target_pairs={{0,8},{4,12},{8,0},{12,4},{16,24},{20,28},{24,16},{28,20},{1,9},{5... | collective-permute-start | bytes 786440 | tf_op jit(solution)/shard_map/ppermute | solution.py:229
  133.0 24.2 %collective-permute-start.18 = (f32[256,256]{1,0:T(8,128)S(1)}, f32[256,256]{1,0:T(8,128)S(1)}, u32[]{:S(2)}, u32[]{:S(2)}) collective-permute-start(f32[256,256]{1,0:T(8,128)S(1)} %get-tuple-element.64), channel_id=1, source_target_pairs={{0,12},{4,8},{8,4},{12,0},{16,28},{20,24},{24,20},{28,16},{1,13},{... | collective-permute-start | bytes 786440 | tf_op jit(solution)/shard_map/ppermute | solution.py:229
  144.8 18.5 %collective-permute-start.19 = (f32[256,256]{1,0:T(8,128)S(1)}, f32[256,256]{1,0:T(8,128)S(1)}, u32[]{:S(2)}, u32[]{:S(2)}) collective-permute-start(f32[256,256]{1,0:T(8,128)S(1)} %touch.22), channel_id=1, source_target_pairs={{0,20},{4,16},{8,28},{12,24},{16,4},{20,0},{24,12},{28,8},{1,21},{... | collective-permute-start | bytes 786440 | tf_op jit(solution)/shard_map/ppermute | solution.py:229
  144.9 21.2 %collective-permute-start.30 = (f32[256,256]{1,0:T(8,128)S(1)}, f32[256,256]{1,0:T(8,128)S(1)}, u32[]{:S(2)}, u32[]{:S(2)}) collective-permute-start(f32[256,256]{1,0:T(8,128)S(1)} %get-tuple-element.84), channel_id=1, source_target_pairs={{0,4},{4,0},{8,12},{12,8},{16,20},{20,16},{24,28},{28,24},{1,5},{5... | collective-permute-start | bytes 786440 | tf_op jit(solution)/shard_map/ppermute | solution.py:229
  153.6 13.2 %collective-permute-start.31 = (f32[256,256]{1,0:T(8,128)S(1)}, f32[256,256]{1,0:T(8,128)S(1)}, u32[]{:S(2)}, u32[]{:S(2)}) collective-permute-start(f32[256,256]{1,0:T(8,128)S(1)} %get-tuple-element.85), channel_id=1, source_target_pairs={{0,8},{4,12},{8,0},{12,4},{16,24},{20,28},{24,16},{28,20},{1,9},{5... | collective-permute-start | bytes 786440 | tf_op jit(solution)/shard_map/ppermute | solution.py:229
  157.2 26.1 %collective-permute-start.25 = (f32[256,256]{1,0:T(8,128)S(1)}, f32[256,256]{1,0:T(8,128)S(1)}, u32[]{:S(2)}, u32[]{:S(2)}) collective-permute-start(f32[256,256]{1,0:T(8,128)S(1)} %touch.28), channel_id=1, source_target_pairs={{0,24},{4,28},{8,16},{12,20},{16,8},{20,12},{24,0},{28,4},{1,25},{... | collective-permute-start | bytes 786440 | tf_op jit(solution)/shard_map/ppermute | solution.py:229
  157.2 34.2 %collective-permute-start.23 = (f32[256,256]{1,0:T(8,128)S(1)}, f32[256,256]{1,0:T(8,128)S(1)}, u32[]{:S(2)}, u32[]{:S(2)}) collective-permute-start(f32[256,256]{1,0:T(8,128)S(1)} %touch.26), channel_id=1, source_target_pairs={{0,28},{4,24},{8,20},{12,16},{16,12},{20,8},{24,4},{28,0},{1,29},{... | collective-permute-start | bytes 786440 | tf_op jit(solution)/shard_map/ppermute | solution.py:229
  163.3 29.5 %collective-permute-start.20 = (f32[256,256]{1,0:T(8,128)S(1)}, f32[256,256]{1,0:T(8,128)S(1)}, u32[]{:S(2)}, u32[]{:S(2)}) collective-permute-start(f32[256,256]{1,0:T(8,128)S(1)} %touch.23), channel_id=1, source_target_pairs={{0,16},{4,20},{8,24},{12,28},{16,0},{20,4},{24,8},{28,12},{1,17},{... | collective-permute-start | bytes 786440 | tf_op jit(solution)/shard_map/ppermute | solution.py:229
  166.0 30.3 %collective-permute-start.32 = (f32[256,256]{1,0:T(8,128)S(1)}, f32[256,256]{1,0:T(8,128)S(1)}, u32[]{:S(2)}, u32[]{:S(2)}) collective-permute-start(f32[256,256]{1,0:T(8,128)S(1)} %get-tuple-element.86), channel_id=1, source_target_pairs={{0,12},{4,8},{8,4},{12,0},{16,28},{20,24},{24,20},{28,16},{1,13},{... | collective-permute-start | bytes 786440 | tf_op jit(solution)/shard_map/ppermute | solution.py:229
  166.8 37.5 %collective-permute-start.27 = (f32[256,256]{1,0:T(8,128)S(1)}, f32[256,256]{1,0:T(8,128)S(1)}, u32[]{:S(2)}, u32[]{:S(2)}) collective-permute-start(f32[256,256]{1,0:T(8,128)S(1)} %get-tuple-element.77), channel_id=1, source_target_pairs={{0,4},{4,0},{8,12},{12,8},{16,20},{20,16},{24,28},{28,24},{1,5},{5... | collective-permute-start | bytes 786440 | tf_op jit(solution)/shard_map/ppermute | solution.py:229
  183.3 31.9 %collective-permute-start.28 = (f32[256,256]{1,0:T(8,128)S(1)}, f32[256,256]{1,0:T(8,128)S(1)}, u32[]{:S(2)}, u32[]{:S(2)}) collective-permute-start(f32[256,256]{1,0:T(8,128)S(1)} %get-tuple-element.78), channel_id=1, source_target_pairs={{0,8},{4,12},{8,0},{12,4},{16,24},{20,28},{24,16},{28,20},{1,9},{5... | collective-permute-start | bytes 786440 | tf_op jit(solution)/shard_map/ppermute | solution.py:229
  191.4 23.8 %collective-permute-start.29 = (f32[256,256]{1,0:T(8,128)S(1)}, f32[256,256]{1,0:T(8,128)S(1)}, u32[]{:S(2)}, u32[]{:S(2)}) collective-permute-start(f32[256,256]{1,0:T(8,128)S(1)} %get-tuple-element.79), channel_id=1, source_target_pairs={{0,12},{4,8},{8,4},{12,0},{16,28},{20,24},{24,20},{28,16},{1,13},{... | collective-permute-start | bytes 786440 | tf_op jit(solution)/shard_map/ppermute | solution.py:229
  192.8 27.2 %collective-permute-start.26 = (f32[256,256]{1,0:T(8,128)S(1)}, f32[256,256]{1,0:T(8,128)S(1)}, u32[]{:S(2)}, u32[]{:S(2)}) collective-permute-start(f32[256,256]{1,0:T(8,128)S(1)} %touch.29), channel_id=1, source_target_pairs={{0,20},{4,16},{8,28},{12,24},{16,4},{20,0},{24,12},{28,8},{1,21},{... | collective-permute-start | bytes 786440 | tf_op jit(solution)/shard_map/ppermute | solution.py:229
  196.4 30.7 %collective-permute-start.24 = (f32[256,256]{1,0:T(8,128)S(1)}, f32[256,256]{1,0:T(8,128)S(1)}, u32[]{:S(2)}, u32[]{:S(2)}) collective-permute-start(f32[256,256]{1,0:T(8,128)S(1)} %touch.27), channel_id=1, source_target_pairs={{0,24},{4,28},{8,16},{12,20},{16,8},{20,12},{24,0},{28,4},{1,25},{... | collective-permute-start | bytes 786440 | tf_op jit(solution)/shard_map/ppermute | solution.py:229
  204.3 26.4 %collective-permute-start.21 = (f32[256,256]{1,0:T(8,128)S(1)}, f32[256,256]{1,0:T(8,128)S(1)}, u32[]{:S(2)}, u32[]{:S(2)}) collective-permute-start(f32[256,256]{1,0:T(8,128)S(1)} %touch.24), channel_id=1, source_target_pairs={{0,28},{4,24},{8,20},{12,16},{16,12},{20,8},{24,4},{28,0},{1,29},{... | collective-permute-start | bytes 786440 | tf_op jit(solution)/shard_map/ppermute | solution.py:229
  204.3 4.7 %copy-start.5 = (f32[2,256,256]{2,1,0:T(8,128)S(1)}, f32[2,256,256]{2,1,0:T(8,128)}, u32[]{:S(2)}) copy-start(f32[2,256,256]{2,1,0:T(8,128)} %get-tuple-element.81.inner_ref) | copy-start | bytes 1572868

commit v3 on v2

--- a/solution.py
+++ b/solution.py
@@ -12,7 +12,7 @@
 F32 = jnp.float32
 BF16 = jnp.bfloat16
 FLIGHT = 3
-STRICT = False
+NEEDS = {3: ["leaf"], 5: [(0, 0)], 6: [(0, 1)], 7: [(0, 2), (1, 0)], 8: [(1, 1)], 9: [(1, 2)], 12: [(2, 0)], 13: [(2, 1)], 14: [(2, 2)], 15: [(3, 0), (3, 1)]}
 RIDE = 0
 PACE = (0, 2, 4)
 CHUNKS = 2
@@ -225,6 +225,10 @@
     return pl.BlockSpec(memory_space=pltpu.HBM)
 
 
+def corner(value):
+    return value[(0,) * (value.ndim - 2)][:8, :128]
+
+
 def swap(value, axis, k):
     return lax.ppermute(value, axis, [(i, i ^ k) for i in range(lax.axis_size(axis))])
 
@@ -304,6 +308,7 @@
     def touch(value, after):
         if not after:
             return value
+        after = [corner(array) for array in after]
         return pl.pallas_call(
             touch_kernel,
             out_shape=jax.ShapeDtypeStruct(value.shape, value.dtype),
@@ -329,7 +334,7 @@
                 2 * 2 * width * (height + 2 * width) * n * count * 3, 4 * n * count * (height + 4 * width)
             ),
             name="leaf",
-        )(place, window, rows_m, send_m, after)
+        )(place, window, rows_m, send_m, corner(after))
         return out[0], list(out[1:])
 
     def nodes(pack, after):
@@ -415,52 +420,42 @@
     def unfold(rider):
         return jnp.concatenate([rider[:, g * width : (g + 1) * width] for g in range(groups)], axis=0)
 
-    fars, nears, queue = [], [], []
+    fars, nears = [], {}
 
     def far_swap(value, k):
-        needs = fars[len(fars) - FLIGHT :][:1] if len(fars) >= FLIGHT else []
-        if STRICT:
-            needs += nears[:-1]
-            del nears[:-1]
-        fars.append(swap(touch(value, needs), "row", k))
+        after = fars[len(fars) - FLIGHT :][:1] if len(fars) >= FLIGHT else []
+        after += [nears[key] for key in NEEDS.get(len(fars), ()) if key in nears]
+        fars.append(swap(touch(value, after), "row", k))
         return fars[-1]
 
-    def near_trades(got, pieces):
-        def run(k):
-            got[k] = swap(pieces[k], "row", k)
-            nears.append(got[k])
-
-        return [functools.partial(run, k) for k in near]
+    def near_trades(stage, got, pieces):
+        for i, k in enumerate(near):
+            got[k] = nears[stage, i] = swap(pieces[k], "row", k)
 
     arrived = [[None] * rows for _ in range(chunks)]
     own = other = None
     for chunk in range(chunks):
         if chunk == 0:
-            after = leaves(0, far[:cut], send_m)
-            leaves(0, far[cut:], steps[min(1, len(steps) - 1)])
+            after = leaves(0, far[:1], send_m)
+            leaves(0, far[1:], steps[min(1, len(steps) - 1)])
         else:
-            leaves(chunk, far, fars[0])
-            leaves(chunk, [0] + near, fars[0])
+            leaves(chunk, far, fars[1])
+            leaves(chunk, [0] + near, nears[0, len(near) - 1])
             arrived[chunk][0] = sent[chunk][0]
-            for k in near:
-                arrived[chunk][k] = swap(sent[chunk][k], "row", k)
+            near_trades(chunk, arrived[chunk], sent[chunk])
         for k in far:
             if (chunk, k) == (0, ride):
                 own = fold(lax.dynamic_slice_in_dim(dmat, core * share, share, axis=0))
                 got = far_swap(jnp.concatenate([sent[0][k], own]), k)
                 arrived[0][k], other = got[: 2 * width], got[2 * width :]
-                leaves(0, [0] + near, fars[0])
+                nears["leaf"] = leaves(0, [0] + near, steps[-1])
                 arrived[0][0] = sent[0][0]
                 for j in near:
                     sent[0][j] = jnp.concatenate([sent[0][j], own, other])
-                queue += near_trades(arrived[0], sent[0])
+                near_trades(0, arrived[0], sent[0])
             else:
                 arrived[chunk][k] = far_swap(sent[chunk][k], k)
-            if queue:
-                queue.pop(0)()
-
-    while any(got is None for got in arrived[0]):
-        queue.pop(0)()
+
     shares = {0: own, ride: other}
     for k in near:
         got = arrived[0][k]
@@ -479,19 +474,13 @@
     pairs = None
     returned = []
     for chunk in range(chunks):
-        while any(got is None for got in arrived[chunk]):
-            queue.pop(0)()
         if chunk == 0:
-            pairs = nodes(pack, pace[1])
+            pairs = nodes(pack, corner(pace[1]))
         made = tree(pairs, dmats, arrived[chunk])
         returned.append([made[0]] + [None] * (rows - 1))
-        queue += near_trades(returned[chunk], made)
+        near_trades(chunks + chunk, returned[chunk], made)
         for k in far:
-            if queue:
-                queue.pop(0)()
             returned[chunk][k] = far_swap(made[k], k)
-    while queue:
-        queue.pop(0)()
 
     out = None
     for chunk in range(chunks):

time: 235 us -> 228 us (0.970)
  starting transfers between devices: 55.9 us -> 51.9 us
  waiting for transfers between devices: 95.5 us -> 92 us
    ppermute x33, starting transfers between devices: 55.9 us -> 51.9 us  [swap(): lax.ppermute(value, axis, [(i, i ^ k) for i in range(lax.axis_size(axis))])]
    ppermute x33, waiting for transfers between devices: 95.5 us -> 92 us  [swap(): lax.ppermute(value, axis, [(i, i ^ k) for i in range(lax.axis_size(axis))])]
    unnamed x31 -> x33, local copies, waits for them, and re-layouts: 8.3 us -> 8.74 us
  transfers between devices with their start and end apart: 33 -> 33, of which waited for: 13 -> 18; matrix products, arithmetic and copies ran while one was open for 1% -> 1% of each run, Pallas kernels for 26% -> 27%
where the time goes in v3:
time: 228 us; the launch traced here: 226 us
  waiting for transfers between devices  92 us (40%)
  Pallas kernels  62.8 us (28%)
  starting transfers between devices  51.9 us (23%)
  local copies, waits for them, and re-layouts  9.62 us (4%)
  blocking collectives  7.4 us (3%)
    ppermute x33, waiting for transfers between devices, swap(): lax.ppermute(value, axis, [(i, i ^ k) for i in range(lax.axis_size(axis))])  92 us
    ppermute x33, starting transfers between devices, swap(): lax.ppermute(value, axis, [(i, i ^ k) for i in range(lax.axis_size(axis))])  51.9 us
    pallas_call x7, Pallas kernels, last(): pl.pallas_call(functools.partial(last_kernel, [part(chunk, k) for k in ks...  22 us
    pallas_call x5, Pallas kernels, leaf(): pl.pallas_call(functools.partial(leaf_kernel, [part(chunk, k) for k in ks...  20.4 us
    pallas_call x2, Pallas kernels, tree(): pl.pallas_call(functools.partial(tree_kernel, rows, order), out_shape=(ja...  9.37 us
    unnamed x33, local copies, waits for them, and re-layouts  8.74 us
    pallas_call x1, Pallas kernels, nodes(): pl.pallas_call(nodes_kernel, grid_spec=pltpu.PrefetchScalarGridSpec(num_s...  8.05 us
    all_gather x1, blocking collectives, local(): vecs = lax.all_gather(leaf_vecs, 'col', axis=1, tiled=True)  7.4 us
  transfers between devices with their start and end apart: 33, of which 18 were waited for; matrix products, arithmetic and copies ran while one was open for 1% of the time, Pallas kernels for 27%

profile of v3, /device:TPU:8, one launch (start us, length us, event | category | flops | bytes accessed | tf_op | source)
XLA Modules:
  0.0 226.1 jit_solution(17218761305672919931)
XLA Ops:
  0.1 0.9 copy-done.7
  1.0 0.9 copy-done.8
  1.9 0.6 pack.1
  2.4 2.7 %collective-permute-start = (f32[1,256,128]{2,1,0:T(8,128)S(1)}, f32[1,256,128]{2,1,0:T(8,128)S(1)}, u32[]{:S(2)}, u32[]{:S(2)}) collective-permute-start(f32[1,256,128]{2,1,0:T(8,128)S(1)} %pack.1), channel_id=1, source_target_pairs={{0,16},{4,20},{8,24},{12,28},{16,0},{20,4},{24,8},{28,12},{1,17},{... | collective-permute-start | bytes 393224 | tf_op jit(solution)/shard_map/ppermute | solution.py:233
  5.1 7.4 %all_gather.3.vecs_ref = f32[2,512,128]{2,1,0:T(8,128)S(1)} all-gather(f32[2,128,128]{2,1,0:T(8,128)} %param.6), channel_id=1, replica_groups=mesh['row'=8,'col'=4] {'col'}, dimensions={1}, use_global_device_ids=true | all-gather | bytes 655360 | tf_op jit(solution)/shard_map/all_gather | solution.py:274
  12.5 0.5 collective-permute-start.1
  13.1 0.9 copy-done.12
  14.0 1.9 prep.1
  15.9 0.8 copy-done.1
  16.7 0.6 slice.245.after_ref
  17.4 3.7 %leaf.7 = (f32[1,256,256]{2,1,0:T(8,128)}, f32[256,256]{1,0:T(8,128)}) custom-call(s32[2]{0:T(128)} %copy-done.9, f32[512,4096]{1,0:T(8,128)} %window_ref.23, bf16[2,256,512]{2,1,0:T(8,128)(2,1)} %copy-done.1, bf16[2,256,256]{2,1,0:T(8,128)(2,1)} %copy-done.3, bf16[8,128]{1,0:T(8,128)(2,1)} %slice.245.after_ref), custom_call_target="tpu_custom_call" | custom-call | flops 301989888 | bytes 1048576 | tf_op jit(solution)/shard_map/leaf/pallas_call | solution.py:325
  21.1 1.0 maximum_maximum_fusion
  22.0 1.1 collective-permute-start.5
  23.2 1.6 collective-permute-start.4
  24.7 3.4 %copy-done = f32[512,4096]{1,0:T(8,128)S(1)} copy-done((f32[512,4096]{1,0:T(8,128)S(1)}, f32[512,4096]{1,0:T(8,128)}, u32[]{:S(2)}) %copy-start) | copy-done | bytes 8388632
  28.1 0.9 copy-done.4
  29.1 0.7 copy-done.10
  29.8 3.5 %leaf.5 = (f32[3,256,256]{2,1,0:T(8,128)S(1)}, f32[256,256]{1,0:T(8,128)S(1)}, f32[256,256]{1,0:T(8,128)S(1)}, f32[256,256]{1,0:T(8,128)S(1)}) custom-call(s32[2]{0:T(128)S(1)} %copy-done.10, f32[512,4096]{1,0:T(8,128)S(1)} %copy-done, bf16[2,256,512]{2,1,0:T(8,128)(2,1)S(1)} %copy-done.2, bf16[2,256,256]{2,1,0:T(8,128)(2,1)S(1)} %copy-done.4, ...), custom_call_target="tpu_custom_call" | custom-call | flops 905969664 | bytes 3145728 | tf_op jit(solution)/shard_map/leaf/pallas_call | solution.py:325
  33.3 2.0 collective-permute-start.2
  35.2 1.5 collective-permute-start.3
  36.8 11.3 %collective-permute-done.5 = f32[288,256]{1,0:T(8,128)S(1)} collective-permute-done((f32[288,256]{1,0:T(8,128)S(1)}, f32[288,256]{1,0:T(8,128)S(1)}, u32[]{:S(2)}, u32[]{:S(2)}) %collective-permute-start.5) | collective-permute-done | bytes 294944 | tf_op jit(solution)/shard_map/ppermute | solution.py:233
  48.1 5.6 %collective-permute-done.2.refs_1_ = f32[256,256]{1,0:T(8,128)S(1)} collective-permute-done((f32[256,256]{1,0:T(8,128)S(1)}, f32[256,256]{1,0:T(8,128)S(1)}, u32[]{:S(2)}, u32[]{:S(2)}) %collective-permute-start.2) | collective-permute-done | bytes 262176 | tf_op jit(solution)/shard_map/ppermute | solution.py:233
  53.7 4.4 %leaf.6 = (f32[4,256,256]{2,1,0:T(8,128)S(1)}, f32[256,256]{1,0:T(8,128)S(1)}, f32[256,256]{1,0:T(8,128)S(1)}, f32[256,256]{1,0:T(8,128)S(1)}, f32[256,256]{1,0:T(8,128)S(1)}) custom-call(s32[2]{0:T(128)S(1)} %copy-done.10, f32[512,4096]{1,0:T(8,128)S(1)} %copy-done, bf16[2,256,512]{2,1,0:T(8,128)(2,1)S(1)} %copy-done.2, bf16[2,256,256]{2,1,0:T(8,128)(2,1)S(1)} %copy-done.4, ...), custom_call_target="tpu_custom_call" | custom-call | flops 1207959552 | bytes 4194304 | tf_op jit(solution)/shard_map/leaf/pallas_call | solution.py:325
  58.1 4.4 %collective-permute-start.10 = (f32[256,256]{1,0:T(8,128)S(1)}, f32[256,256]{1,0:T(8,128)S(1)}, u32[]{:S(2)}, u32[]{:S(2)}) collective-permute-start(f32[256,256]{1,0:T(8,128)S(1)} %touch.16), channel_id=1, source_target_pairs={{0,16},{4,20},{8,24},{12,28},{16,0},{20,4},{24,8},{28,12},{1,17},{... | collective-permute-start | bytes 786440 | tf_op jit(solution)/shard_map/ppermute | solution.py:233
  62.5 4.4 %leaf.8 = (f32[4,256,256]{2,1,0:T(8,128)S(1)}, f32[256,256]{1,0:T(8,128)S(1)}, f32[256,256]{1,0:T(8,128)S(1)}, f32[256,256]{1,0:T(8,128)S(1)}, f32[256,256]{1,0:T(8,128)S(1)}) custom-call(s32[2]{0:T(128)S(1)} %copy-done.11, f32[512,4096]{1,0:T(8,128)S(1)} %copy-done, bf16[2,256,512]{2,1,0:T(8,128)(2,1)S(1)} %copy-done.2, bf16[2,256,256]{2,1,0:T(8,128)(2,1)S(1)} %copy-done.5, ...), custom_call_target="tpu_custom_call" | custom-call | flops 1207959552 | bytes 4194304 | tf_op jit(solution)/shard_map/leaf/pallas_call | solution.py:325
  67.5 5.5 %collective-permute-start.7 = (f32[320,256]{1,0:T(8,128)S(1)}, f32[320,256]{1,0:T(8,128)S(1)}, u32[]{:S(2)}, u32[]{:S(2)}) collective-permute-start(f32[320,256]{1,0:T(8,128)S(1)} %get-tuple-element.105), channel_id=1, source_target_pairs={{0,4},{4,0},{8,12},{12,8},{16,20},{20,16},{24,28},{28,24},{1,5},{5... | collective-permute-start | bytes 983048 | tf_op jit(solution)/shard_map/ppermute | solution.py:233
  73.3 1.5 collective-permute-start.8
  74.8 9.3 %collective-permute-done.9 = f32[320,256]{1,0:T(8,128)S(1)} collective-permute-done((f32[320,256]{1,0:T(8,128)S(1)}, f32[320,256]{1,0:T(8,128)S(1)}, u32[]{:S(2)}, u32[]{:S(2)}) %collective-permute-start.9) | collective-permute-done | bytes 327712 | tf_op jit(solution)/shard_map/ppermute | solution.py:233
  84.1 4.4 %leaf.9 = (f32[4,256,256]{2,1,0:T(8,128)S(1)}, f32[256,256]{1,0:T(8,128)S(1)}, f32[256,256]{1,0:T(8,128)S(1)}, f32[256,256]{1,0:T(8,128)S(1)}, f32[256,256]{1,0:T(8,128)S(1)}) custom-call(s32[2]{0:T(128)S(1)} %copy-done.11, f32[512,4096]{1,0:T(8,128)S(1)} %bitcast.56, bf16[2,256,512]{2,1,0:T(8,128)(2,1)S(1)} %copy-done.2, ...), custom_call_target="tpu_custom_call" | custom-call | flops 1207959552 | bytes 4194304 | tf_op jit(solution)/shard_map/leaf/pallas_call | solution.py:325
  88.6 2.4 %collective-permute-start.15 = (f32[256,256]{1,0:T(8,128)S(1)}, f32[256,256]{1,0:T(8,128)S(1)}, u32[]{:S(2)}, u32[]{:S(2)}) collective-permute-start(f32[256,256]{1,0:T(8,128)S(1)} %get-tuple-element.63), channel_id=1, source_target_pairs={{0,4},{4,0},{8,12},{12,8},{16,20},{20,16},{24,28},{28,24},{1,5},{5... | collective-permute-start | bytes 786440 | tf_op jit(solution)/shard_map/ppermute | solution.py:233
  90.9 2.3 %collective-permute-done.7 = f32[320,256]{1,0:T(8,128)S(1)} collective-permute-done((f32[320,256]{1,0:T(8,128)S(1)}, f32[320,256]{1,0:T(8,128)S(1)}, u32[]{:S(2)}, u32[]{:S(2)}) %collective-permute-start.7) | collective-permute-done | bytes 327712 | tf_op jit(solution)/shard_map/ppermute | solution.py:233
  93.2 3.3 %collective-permute-done.8 = f32[320,256]{1,0:T(8,128)S(1)} collective-permute-done((f32[320,256]{1,0:T(8,128)S(1)}, f32[320,256]{1,0:T(8,128)S(1)}, u32[]{:S(2)}, u32[]{:S(2)}) %collective-permute-start.8) | collective-permute-done | bytes 327712 | tf_op jit(solution)/shard_map/ppermute | solution.py:233
  97.2 2.1 collective-permute-done.15.refs_4_
  99.2 1.2 collective-permute-start.18
  100.5 5.5 %collective-permute-done.17.refs_5_ = f32[256,256]{1,0:T(8,128)S(1)} collective-permute-done((f32[256,256]{1,0:T(8,128)S(1)}, f32[256,256]{1,0:T(8,128)S(1)}, u32[]{:S(2)}, u32[]{:S(2)}) %collective-permute-start.17) | collective-permute-done | bytes 262176 | tf_op jit(solution)/shard_map/ppermute | solution.py:233
  106.0 1.5 collective-permute-start.14
  107.9 7.3 %collective-permute-start.16 = (f32[256,256]{1,0:T(8,128)S(1)}, f32[256,256]{1,0:T(8,128)S(1)}, u32[]{:S(2)}, u32[]{:S(2)}) collective-permute-start(f32[256,256]{1,0:T(8,128)S(1)} %touch.21), channel_id=1, source_target_pairs={{0,28},{4,24},{8,20},{12,16},{16,12},{20,8},{24,4},{28,0},{1,29},{... | collective-permute-start | bytes 786440 | tf_op jit(solution)/shard_map/ppermute | solution.py:233
  115.5 8.0 %nodes.1.pair_ref = bf16[2,2,8,256,256]{4,3,2,1,0:T(8,128)(2,1)S(1)} custom-call(s32[2]{0:T(128)S(1)} %copy-done.11, f32[8,128]{1,0:T(8,128)S(1)} %slice.244.after_ref.refs_1_, f32[2,8,256,128]{3,2,1,0:T(8,128)S(1)} %pad_maximum_fusion.pack_ref), custom_call_target="tpu_custom_call" | custom-call | flops 1207959552 | bytes 8388608 | tf_op jit(solution)/shard_map/nodes/pallas_call | solution.py:341
  123.5 4.7 %tree.3 = (f32[256,256]{1,0:T(8,128)S(1)}, f32[256,256]{1,0:T(8,128)S(1)}, f32[256,256]{1,0:T(8,128)S(1)}, f32[256,256]{1,0:T(8,128)S(1)}, f32[256,256]{1,0:T(8,...) custom-call(s32[2]{0:T(128)S(1)} %copy-done.11, ...), custom_call_target="tpu_custom_call" | custom-call | flops 3221225472 | bytes 8388608 | tf_op jit(solution)/shard_map/tree/pallas_call | solution.py:359
  128.3 0.7 collective-permute-start.25
  129.0 10.8 %collective-permute-done.16.refs_3_ = f32[256,256]{1,0:T(8,128)S(1)} collective-permute-done((f32[256,256]{1,0:T(8,128)S(1)}, f32[256,256]{1,0:T(8,128)S(1)}, u32[]{:S(2)}, u32[]{:S(2)}) %collective-permute-start.16) | collective-permute-done | bytes 262176 | tf_op jit(solution)/shard_map/ppermute | solution.py:233
  139.9 1.0 collective-permute-start.20
  140.9 3.5 %collective-permute-start.27 = (f32[256,256]{1,0:T(8,128)S(1)}, f32[256,256]{1,0:T(8,128)S(1)}, u32[]{:S(2)}, u32[]{:S(2)}) collective-permute-start(f32[256,256]{1,0:T(8,128)S(1)} %get-tuple-element.77), channel_id=1, source_target_pairs={{0,12},{4,8},{8,4},{12,0},{16,28},{20,24},{24,20},{28,16},{1,13},{... | collective-permute-start | bytes 786440 | tf_op jit(solution)/shard_map/ppermute | solution.py:233
  144.4 4.0 %collective-permute-done.25.refs_0_ = f32[256,256]{1,0:T(8,128)S(1)} collective-permute-done((f32[256,256]{1,0:T(8,128)S(1)}, f32[256,256]{1,0:T(8,128)S(1)}, u32[]{:S(2)}, u32[]{:S(2)}) %collective-permute-start.25) | collective-permute-done | bytes 262176 | tf_op jit(solution)/shard_map/ppermute | solution.py:233
  148.4 0.9 collective-permute-start.29
  149.4 4.7 %tree.2 = (f32[256,256]{1,0:T(8,128)S(1)}, f32[256,256]{1,0:T(8,128)S(1)}, f32[256,256]{1,0:T(8,128)S(1)}, f32[256,256]{1,0:T(8,128)S(1)}, f32[256,256]{1,0:T(8,...) custom-call(s32[2]{0:T(128)S(1)} %copy-done.11, ...), custom_call_target="tpu_custom_call" | custom-call | flops 3221225472 | bytes 8388608 | tf_op jit(solution)/shard_map/tree/pallas_call | solution.py:359
  154.8 5.6 %collective-permute-done.20.refs_1_ = f32[256,256]{1,0:T(8,128)S(1)} collective-permute-done((f32[256,256]{1,0:T(8,128)S(1)}, f32[256,256]{1,0:T(8,128)S(1)}, u32[]{:S(2)}, u32[]{:S(2)}) %collective-permute-start.20) | collective-permute-done | bytes 262176 | tf_op jit(solution)/shard_map/ppermute | solution.py:233
  160.4 3.9 %collective-permute-start.26 = (f32[256,256]{1,0:T(8,128)S(1)}, f32[256,256]{1,0:T(8,128)S(1)}, u32[]{:S(2)}, u32[]{:S(2)}) collective-permute-start(f32[256,256]{1,0:T(8,128)S(1)} %touch.26), channel_id=1, source_target_pairs={{0,28},{4,24},{8,20},{12,16},{16,12},{20,8},{24,4},{28,0},{1,29},{... | collective-permute-start | bytes 786440 | tf_op jit(solution)/shard_map/ppermute | solution.py:233
  164.4 4.4 %collective-permute-done.30.refs_2_ = f32[256,256]{1,0:T(8,128)S(1)} collective-permute-done((f32[256,256]{1,0:T(8,128)S(1)}, f32[256,256]{1,0:T(8,128)S(1)}, u32[]{:S(2)}, u32[]{:S(2)}) %collective-permute-start.30) | collective-permute-done | bytes 262176 | tf_op jit(solution)/shard_map/ppermute | solution.py:233
  168.7 4.7 %collective-permute-start.21 = (f32[256,256]{1,0:T(8,128)S(1)}, f32[256,256]{1,0:T(8,128)S(1)}, u32[]{:S(2)}, u32[]{:S(2)}) collective-permute-start(f32[256,256]{1,0:T(8,128)S(1)} %touch.23), channel_id=1, source_target_pairs={{0,16},{4,20},{8,24},{12,28},{16,0},{20,4},{24,8},{28,12},{1,17},{... | collective-permute-start | bytes 786440 | tf_op jit(solution)/shard_map/ppermute | solution.py:233
  173.4 0.6 collective-permute-start.32
  174.1 1.5 collective-permute-start.31
  175.7 3.7 %collective-permute-done.23.refs_2_ = f32[256,256]{1,0:T(8,128)S(1)} collective-permute-done((f32[256,256]{1,0:T(8,128)S(1)}, f32[256,256]{1,0:T(8,128)S(1)}, u32[]{:S(2)}, u32[]{:S(2)}) %collective-permute-start.23) | collective-permute-done | bytes 262176 | tf_op jit(solution)/shard_map/ppermute | solution.py:233
  179.3 5.1 %collective-permute-done.26.refs_2_ = f32[256,256]{1,0:T(8,128)S(1)} collective-permute-done((f32[256,256]{1,0:T(8,128)S(1)}, f32[256,256]{1,0:T(8,128)S(1)}, u32[]{:S(2)}, u32[]{:S(2)}) %collective-permute-start.26) | collective-permute-done | bytes 262176 | tf_op jit(solution)/shard_map/ppermute | solution.py:233
  184.4 1.1 collective-permute-start.28
  185.5 13.9 %collective-permute-done.21.refs_0_ = f32[256,256]{1,0:T(8,128)S(1)} collective-permute-done((f32[256,256]{1,0:T(8,128)S(1)}, f32[256,256]{1,0:T(8,128)S(1)}, u32[]{:S(2)}, u32[]{:S(2)}) %collective-permute-start.21) | collective-permute-done | bytes 262176 | tf_op jit(solution)/shard_map/ppermute | solution.py:233
  199.5 4.7 %last.7.refs_1_ = f32[512,4096]{1,0:T(8,128)} custom-call(s32[2]{0:T(128)S(1)} %copy-done.11, f32[512,4096]{1,0:T(8,128)S(1)} %bitcast.56, f32[4,256,256]{2,1,0:T(8,128)S(1)} %get-tuple-element.61.inner_ref, bf16[2,384,384]{2,1,0:T(8,128)(2,1)S(1)} %get-tuple-element.50.rest_ref, f32[256,256]{1,0:T(8,128)S(1)} %get-tuple-element.86.refs_0_, ...), custom_call_target="tpu_custom_call" | custom-call | flops 905969664 | bytes 6291456 | tf_op jit(solution)/shard_map/last/pallas_call | solution.py:380
  204.2 1.9 last.8.refs_3_
  206.1 3.6 %last.9.refs_4_ = f32[512,4096]{1,0:T(8,128)} custom-call(s32[2]{0:T(128)S(1)} %copy-done.11, f32[512,4096]{1,0:T(8,128)S(1)} %bitcast.56, f32[3,256,256]{2,1,0:T(8,128)S(1)} %get-tuple-element.84.inner_ref, bf16[2,384,384]{2,1,0:T(8,128)(2,1)S(1)} %get-tuple-element.50.rest_ref, ...), custom_call_target="tpu_custom_call", output_to_operand_aliasing={{}: (7, {})} | custom-call | flops 679477248 | bytes 4718592 | tf_op jit(solution)/shard_map/last/pallas_call | solution.py:380
  209.7 4.9 %last.10.refs_2_ = f32[512,4096]{1,0:T(8,128)} custom-call(s32[2]{0:T(128)S(1)} %copy-done.11, f32[512,4096]{1,0:T(8,128)S(1)} %bitcast.56, f32[4,256,256]{2,1,0:T(8,128)S(1)} %get-tuple-element.81.inner_ref, bf16[2,384,384]{2,1,0:T(8,128)(2,1)S(1)} %get-tuple-element.50.rest_ref, ...), custom_call_target="tpu_custom_call", output_to_operand_aliasing={{}: (8, {})} | custom-call | flops 905969664 | bytes 6291456 | tf_op jit(solution)/shard_map/last/pallas_call | solution.py:380
  214.7 3.1 %last.11.refs_1_ = f32[512,4096]{1,0:T(8,128)} custom-call(s32[2]{0:T(128)S(1)} %copy-done.11, f32[512,4096]{1,0:T(8,128)S(1)} %bitcast.56, f32[4,256,256]{2,1,0:T(8,128)S(1)} %get-tuple-element.49.inner_ref, bf16[2,384,384]{2,1,0:T(8,128)(2,1)S(1)} %get-tuple-element.50.rest_ref, ...), custom_call_target="tpu_custom_call", output_to_operand_aliasing={{}: (6, {})} | custom-call | flops 452984832 | bytes 3145728 | tf_op jit(solution)/shard_map/last/pallas_call | solution.py:380
  218.0 1.9 last.12.refs_1_
  219.9 4.1 %collective-permute-done.24.refs_0_ = f32[256,256]{1,0:T(8,128)S(1)} collective-permute-done((f32[256,256]{1,0:T(8,128)S(1)}, f32[256,256]{1,0:T(8,128)S(1)}, u32[]{:S(2)}, u32[]{:S(2)}) %collective-permute-start.24) | collective-permute-done | bytes 262176 | tf_op jit(solution)/shard_map/ppermute | solution.py:233
  224.0 1.9 last.13
  (126 shorter events, 3.7 us)
Async XLA Ops:
  0.1 0.9 copy-start.7
  1.0 0.9 copy-start.8
  1.9 15.4 %copy-start.9 = (s32[2]{0:T(128)}, s32[2]{0:T(128)S(1)}, u32[]{:S(2)}) copy-start(s32[2]{0:T(128)S(1)} %pad_add_fusion.place_ref) | copy-start | bytes 28
  2.4 10.1 %collective-permute-start = (f32[1,256,128]{2,1,0:T(8,128)S(1)}, f32[1,256,128]{2,1,0:T(8,128)S(1)}, u32[]{:S(2)}, u32[]{:S(2)}) collective-permute-start(f32[1,256,128]{2,1,0:T(8,128)S(1)} %pack.1), channel_id=1, source_target_pairs={{0,16},{4,20},{8,24},{12,28},{16,0},{20,4},{24,8},{28,12},{1,17},{... | collective-permute-start | bytes 393224 | tf_op jit(solution)/shard_map/ppermute | solution.py:233
  12.5 10.6 %collective-permute-start.1 = (f32[2,256,128]{2,1,0:T(8,128)S(1)}, f32[2,256,128]{2,1,0:T(8,128)S(1)}, u32[]{:S(2)}, u32[]{:S(2)}) collective-permute-start(f32[2,256,128]{2,1,0:T(8,128)S(1)} %get-tuple-element.102), channel_id=1, source_target_pairs={{0,8},{4,12},{8,0},{12,4},{16,24},{20,28},{24,16},{28,20},{1,9},{5... | collective-permute-start | bytes 786440 | tf_op jit(solution)/shard_map/ppermute | solution.py:233
  13.1 0.9 copy-start.12
  15.9 0.8 copy-start.1
  16.7 0.7 copy-start.3
  16.7 8.1 %copy-start.2 = (bf16[2,256,512]{2,1,0:T(8,128)(2,1)S(1)}, bf16[2,256,512]{2,1,0:T(8,128)(2,1)}, u32[]{:S(2)}) copy-start(bf16[2,256,512]{2,1,0:T(8,128)(2,1)} %copy-done.1) | copy-start | bytes 1572868
  22.0 26.0 %collective-permute-start.5 = (f32[288,256]{1,0:T(8,128)S(1)}, f32[288,256]{1,0:T(8,128)S(1)}, u32[]{:S(2)}, u32[]{:S(2)}) collective-permute-start(f32[288,256]{1,0:T(8,128)S(1)} %maximum_maximum_fusion), channel_id=1, source_target_pairs={{0,16},{4,20},{8,24},{12,28},{16,0},{20,4},{24,8},{28,12},{1,17},{... | collective-permute-start | bytes 884744 | tf_op jit(solution)/shard_map/ppermute | solution.py:233
  23.2 39.3 %collective-permute-start.4 = (f32[4,256,128]{2,1,0:T(8,128)S(1)}, f32[4,256,128]{2,1,0:T(8,128)S(1)}, u32[]{:S(2)}, u32[]{:S(2)}) collective-permute-start(f32[4,256,128]{2,1,0:T(8,128)S(1)} %bitcast.61), channel_id=1, source_target_pairs={{0,4},{4,0},{8,12},{12,8},{16,20},{20,16},{24,28},{28,24},{1,5},{5... | collective-permute-start | bytes 1572872 | tf_op jit(solution)/shard_map/ppermute | solution.py:233
  24.7 3.4 %copy-start = (f32[512,4096]{1,0:T(8,128)S(1)}, f32[512,4096]{1,0:T(8,128)}, u32[]{:S(2)}) copy-start(f32[512,4096]{1,0:T(8,128)} %window_ref.23) | copy-start | bytes 25165828
  28.1 0.9 copy-start.4
  29.1 0.7 copy-start.10
  29.8 32.7 %copy-start.5 = (bf16[2,256,256]{2,1,0:T(8,128)(2,1)S(1)}, bf16[2,256,256]{2,1,0:T(8,128)(2,1)}, u32[]{:S(2)}) copy-start(bf16[2,256,256]{2,1,0:T(8,128)(2,1)} %copy-done.3) | copy-start | bytes 786436
  29.8 32.7 %copy-start.11 = (s32[2]{0:T(128)S(1)}, s32[2]{0:T(128)}, u32[]{:S(2)}) copy-start(s32[2]{0:T(128)} %copy-done.9) | copy-start | bytes 28
  33.3 20.4 %collective-permute-start.2 = (f32[256,256]{1,0:T(8,128)S(1)}, f32[256,256]{1,0:T(8,128)S(1)}, u32[]{:S(2)}, u32[]{:S(2)}) collective-permute-start(f32[256,256]{1,0:T(8,128)S(1)} %get-tuple-element.48), channel_id=1, source_target_pairs={{0,20},{4,16},{8,28},{12,24},{16,4},{20,0},{24,12},{28,8},{1,21},{... | collective-permute-start | bytes 786440 | tf_op jit(solution)/shard_map/ppermute | solution.py:233
  35.2 27.2 %collective-permute-start.3 = (f32[256,256]{1,0:T(8,128)S(1)}, f32[256,256]{1,0:T(8,128)S(1)}, u32[]{:S(2)}, u32[]{:S(2)}) collective-permute-start(f32[256,256]{1,0:T(8,128)S(1)} %get-tuple-element.51), channel_id=1, source_target_pairs={{0,24},{4,28},{8,16},{12,20},{16,8},{20,12},{24,0},{28,4},{1,25},{... | collective-permute-start | bytes 786440 | tf_op jit(solution)/shard_map/ppermute | solution.py:233
  58.1 15.1 %collective-permute-start.10 = (f32[256,256]{1,0:T(8,128)S(1)}, f32[256,256]{1,0:T(8,128)S(1)}, u32[]{:S(2)}, u32[]{:S(2)}) collective-permute-start(f32[256,256]{1,0:T(8,128)S(1)} %touch.16), channel_id=1, source_target_pairs={{0,16},{4,20},{8,24},{12,28},{16,0},{20,4},{24,8},{28,12},{1,17},{... | collective-permute-start | bytes 786440 | tf_op jit(solution)/shard_map/ppermute | solution.py:233
  62.5 21.6 %slice-start = ((s8[8388608]{0:T(1024)(128)(4,1)}), s8[4194304]{0:T(1024)(128)(4,1)S(1)}, s32[]{:S(2)}) async-start(s8[8388608]{0:T(1024)(128)(4,1)} %bitcast.55), calls=%async_computation | async-start | bytes 8388608
  66.9 17.2 %slice-start.1 = ((s8[8388608]{0:T(1024)(128)(4,1)}), s8[4194304]{0:T(1024)(128)(4,1)S(1)}, s32[]{:S(2)}) async-start(s8[8388608]{0:T(1024)(128)(4,1)} %bitcast.55), calls=%async_computation.1 | async-start | bytes 8388608
  67.0 17.1 %collective-permute-start.9 = (f32[320,256]{1,0:T(8,128)S(1)}, f32[320,256]{1,0:T(8,128)S(1)}, u32[]{:S(2)}, u32[]{:S(2)}) collective-permute-start(f32[320,256]{1,0:T(8,128)S(1)} %get-tuple-element.103), channel_id=1, source_target_pairs={{0,12},{4,8},{8,4},{12,0},{16,28},{20,24},{24,20},{28,16},{1,13},{... | collective-permute-start | bytes 983048 | tf_op jit(solution)/shard_map/ppermute | solution.py:233
  67.5 47.8 %collective-permute-start.6 = (f32[8,256,128]{2,1,0:T(8,128)S(1)}, f32[8,256,128]{2,1,0:T(8,128)S(1)}, u32[]{:S(2)}, u32[]{:S(2)}) collective-permute-start(f32[8,256,128]{2,1,0:T(8,128)S(1)} %touch.15), channel_id=1, source_target_pairs={{0,1},{1,0},{2,3},{3,2},{4,5},{5,4},{6,7},{7,6},{8,9},{9,8},{10,11... | collective-permute-start | bytes 3145736 | tf_op jit(solution)/shard_map/ppermute | solution.py:233
  67.5 25.7 %collective-permute-start.7 = (f32[320,256]{1,0:T(8,128)S(1)}, f32[320,256]{1,0:T(8,128)S(1)}, u32[]{:S(2)}, u32[]{:S(2)}) collective-permute-start(f32[320,256]{1,0:T(8,128)S(1)} %get-tuple-element.105), channel_id=1, source_target_pairs={{0,4},{4,0},{8,12},{12,8},{16,20},{20,16},{24,28},{28,24},{1,5},{5... | collective-permute-start | bytes 983048 | tf_op jit(solution)/shard_map/ppermute | solution.py:233
  73.2 23.7 %collective-permute-start.13 = (f32[256,256]{1,0:T(8,128)S(1)}, f32[256,256]{1,0:T(8,128)S(1)}, u32[]{:S(2)}, u32[]{:S(2)}) collective-permute-start(f32[256,256]{1,0:T(8,128)S(1)} %touch.19), channel_id=1, source_target_pairs={{0,28},{4,24},{8,20},{12,16},{16,12},{20,8},{24,4},{28,0},{1,29},{... | collective-permute-start | bytes 786440 | tf_op jit(solution)/shard_map/ppermute | solution.py:233
  73.3 23.3 %collective-permute-start.8 = (f32[320,256]{1,0:T(8,128)S(1)}, f32[320,256]{1,0:T(8,128)S(1)}, u32[]{:S(2)}, u32[]{:S(2)}) collective-permute-start(f32[320,256]{1,0:T(8,128)S(1)} %get-tuple-element.104), channel_id=1, source_target_pairs={{0,8},{4,12},{8,0},{12,4},{16,24},{20,28},{24,16},{28,20},{1,9},{5... | collective-permute-start | bytes 983048 | tf_op jit(solution)/shard_map/ppermute | solution.py:233
  88.6 10.7 %collective-permute-start.15 = (f32[256,256]{1,0:T(8,128)S(1)}, f32[256,256]{1,0:T(8,128)S(1)}, u32[]{:S(2)}, u32[]{:S(2)}) collective-permute-start(f32[256,256]{1,0:T(8,128)S(1)} %get-tuple-element.63), channel_id=1, source_target_pairs={{0,4},{4,0},{8,12},{12,8},{16,20},{20,16},{24,28},{28,24},{1,5},{5... | collective-permute-start | bytes 786440 | tf_op jit(solution)/shard_map/ppermute | solution.py:233
  96.6 9.3 %collective-permute-start.17 = (f32[256,256]{1,0:T(8,128)S(1)}, f32[256,256]{1,0:T(8,128)S(1)}, u32[]{:S(2)}, u32[]{:S(2)}) collective-permute-start(f32[256,256]{1,0:T(8,128)S(1)} %get-tuple-element.64), channel_id=1, source_target_pairs={{0,8},{4,12},{8,0},{12,4},{16,24},{20,28},{24,16},{28,20},{1,9},{5... | collective-permute-start | bytes 786440 | tf_op jit(solution)/shard_map/ppermute | solution.py:233
  96.8 11.1 %collective-permute-start.12 = (f32[256,256]{1,0:T(8,128)S(1)}, f32[256,256]{1,0:T(8,128)S(1)}, u32[]{:S(2)}, u32[]{:S(2)}) collective-permute-start(f32[256,256]{1,0:T(8,128)S(1)} %touch.18), channel_id=1, source_target_pairs={{0,20},{4,16},{8,28},{12,24},{16,4},{20,0},{24,12},{28,8},{1,21},{... | collective-permute-start | bytes 786440 | tf_op jit(solution)/shard_map/ppermute | solution.py:233
  96.9 18.3 %collective-permute-start.11 = (f32[8,64,128]{2,1,0:T(8,128)S(1)}, f32[8,64,128]{2,1,0:T(8,128)S(1)}, u32[]{:S(2)}, u32[]{:S(2)}) collective-permute-start(f32[8,64,128]{2,1,0:T(8,128)S(1)} %touch.17), channel_id=1, source_target_pairs={{0,1},{1,0},{2,3},{3,2},{4,5},{5,4},{6,7},{7,6},{8,9},{9,8},{10,11... | collective-permute-start | bytes 786440 | tf_op jit(solution)/shard_map/ppermute | solution.py:233
  99.2 29.8 %collective-permute-start.18 = (f32[256,256]{1,0:T(8,128)S(1)}, f32[256,256]{1,0:T(8,128)S(1)}, u32[]{:S(2)}, u32[]{:S(2)}) collective-permute-start(f32[256,256]{1,0:T(8,128)S(1)} %get-tuple-element.65), channel_id=1, source_target_pairs={{0,12},{4,8},{8,4},{12,0},{16,28},{20,24},{24,20},{28,16},{1,13},{... | collective-permute-start | bytes 786440 | tf_op jit(solution)/shard_map/ppermute | solution.py:233
  106.0 23.1 %collective-permute-start.14 = (f32[256,256]{1,0:T(8,128)S(1)}, f32[256,256]{1,0:T(8,128)S(1)}, u32[]{:S(2)}, u32[]{:S(2)}) collective-permute-start(f32[256,256]{1,0:T(8,128)S(1)} %touch.20), channel_id=1, source_target_pairs={{0,24},{4,28},{8,16},{12,20},{16,8},{20,12},{24,0},{28,4},{1,25},{... | collective-permute-start | bytes 786440 | tf_op jit(solution)/shard_map/ppermute | solution.py:233
  107.9 31.9 %collective-permute-start.16 = (f32[256,256]{1,0:T(8,128)S(1)}, f32[256,256]{1,0:T(8,128)S(1)}, u32[]{:S(2)}, u32[]{:S(2)}) collective-permute-start(f32[256,256]{1,0:T(8,128)S(1)} %touch.21), channel_id=1, source_target_pairs={{0,28},{4,24},{8,20},{12,16},{16,12},{20,8},{24,4},{28,0},{1,29},{... | collective-permute-start | bytes 786440 | tf_op jit(solution)/shard_map/ppermute | solution.py:233
  128.3 20.1 %collective-permute-start.25 = (f32[256,256]{1,0:T(8,128)S(1)}, f32[256,256]{1,0:T(8,128)S(1)}, u32[]{:S(2)}, u32[]{:S(2)}) collective-permute-start(f32[256,256]{1,0:T(8,128)S(1)} %touch.25), channel_id=1, source_target_pairs={{0,16},{4,20},{8,24},{12,28},{16,0},{20,4},{24,8},{28,12},{1,17},{... | collective-permute-start | bytes 786440 | tf_op jit(solution)/shard_map/ppermute | solution.py:233
  139.8 14.7 %collective-permute-start.19 = (f32[256,256]{1,0:T(8,128)S(1)}, f32[256,256]{1,0:T(8,128)S(1)}, u32[]{:S(2)}, u32[]{:S(2)}) collective-permute-start(f32[256,256]{1,0:T(8,128)S(1)} %touch.22), channel_id=1, source_target_pairs={{0,20},{4,16},{8,28},{12,24},{16,4},{20,0},{24,12},{28,8},{1,21},{... | collective-permute-start | bytes 786440 | tf_op jit(solution)/shard_map/ppermute | solution.py:233
  139.9 20.5 %collective-permute-start.20 = (f32[256,256]{1,0:T(8,128)S(1)}, f32[256,256]{1,0:T(8,128)S(1)}, u32[]{:S(2)}, u32[]{:S(2)}) collective-permute-start(f32[256,256]{1,0:T(8,128)S(1)} %get-tuple-element.71), channel_id=1, source_target_pairs={{0,4},{4,0},{8,12},{12,8},{16,20},{20,16},{24,28},{28,24},{1,5},{5... | collective-permute-start | bytes 786440 | tf_op jit(solution)/shard_map/ppermute | solution.py:233
  140.9 19.5 %collective-permute-start.27 = (f32[256,256]{1,0:T(8,128)S(1)}, f32[256,256]{1,0:T(8,128)S(1)}, u32[]{:S(2)}, u32[]{:S(2)}) collective-permute-start(f32[256,256]{1,0:T(8,128)S(1)} %get-tuple-element.77), channel_id=1, source_target_pairs={{0,12},{4,8},{8,4},{12,0},{16,28},{20,24},{24,20},{28,16},{1,13},{... | collective-permute-start | bytes 786440 | tf_op jit(solution)/shard_map/ppermute | solution.py:233
  144.3 24.4 %collective-permute-start.30 = (f32[256,256]{1,0:T(8,128)S(1)}, f32[256,256]{1,0:T(8,128)S(1)}, u32[]{:S(2)}, u32[]{:S(2)}) collective-permute-start(f32[256,256]{1,0:T(8,128)S(1)} %get-tuple-element.80), channel_id=1, source_target_pairs={{0,8},{4,12},{8,0},{12,4},{16,24},{20,28},{24,16},{28,20},{1,9},{5... | collective-permute-start | bytes 786440 | tf_op jit(solution)/shard_map/ppermute | solution.py:233
  148.4 25.0 %collective-permute-start.29 = (f32[256,256]{1,0:T(8,128)S(1)}, f32[256,256]{1,0:T(8,128)S(1)}, u32[]{:S(2)}, u32[]{:S(2)}) collective-permute-start(f32[256,256]{1,0:T(8,128)S(1)} %touch.28), channel_id=1, source_target_pairs={{0,24},{4,28},{8,16},{12,20},{16,8},{20,12},{24,0},{28,4},{1,25},{... | collective-permute-start | bytes 786440 | tf_op jit(solution)/shard_map/ppermute | solution.py:233
  154.5 19.6 %collective-permute-start.22 = (f32[256,256]{1,0:T(8,128)S(1)}, f32[256,256]{1,0:T(8,128)S(1)}, u32[]{:S(2)}, u32[]{:S(2)}) collective-permute-start(f32[256,256]{1,0:T(8,128)S(1)} %get-tuple-element.72), channel_id=1, source_target_pairs={{0,4},{4,0},{8,12},{12,8},{16,20},{20,16},{24,28},{28,24},{1,5},{5... | collective-permute-start | bytes 786440 | tf_op jit(solution)/shard_map/ppermute | solution.py:233
  160.4 18.9 %collective-permute-start.23 = (f32[256,256]{1,0:T(8,128)S(1)}, f32[256,256]{1,0:T(8,128)S(1)}, u32[]{:S(2)}, u32[]{:S(2)}) collective-permute-start(f32[256,256]{1,0:T(8,128)S(1)} %get-tuple-element.73), channel_id=1, source_target_pairs={{0,8},{4,12},{8,0},{12,4},{16,24},{20,28},{24,16},{28,20},{1,9},{5... | collective-permute-start | bytes 786440 | tf_op jit(solution)/shard_map/ppermute | solution.py:233
  160.4 24.0 %collective-permute-start.26 = (f32[256,256]{1,0:T(8,128)S(1)}, f32[256,256]{1,0:T(8,128)S(1)}, u32[]{:S(2)}, u32[]{:S(2)}) collective-permute-start(f32[256,256]{1,0:T(8,128)S(1)} %touch.26), channel_id=1, source_target_pairs={{0,28},{4,24},{8,20},{12,16},{16,12},{20,8},{24,4},{28,0},{1,29},{... | collective-permute-start | bytes 786440 | tf_op jit(solution)/shard_map/ppermute | solution.py:233
  168.7 30.6 %collective-permute-start.21 = (f32[256,256]{1,0:T(8,128)S(1)}, f32[256,256]{1,0:T(8,128)S(1)}, u32[]{:S(2)}, u32[]{:S(2)}) collective-permute-start(f32[256,256]{1,0:T(8,128)S(1)} %touch.23), channel_id=1, source_target_pairs={{0,16},{4,20},{8,24},{12,28},{16,0},{20,4},{24,8},{28,12},{1,17},{... | collective-permute-start | bytes 786440 | tf_op jit(solution)/shard_map/ppermute | solution.py:233
  173.4 36.3 %collective-permute-start.32 = (f32[256,256]{1,0:T(8,128)S(1)}, f32[256,256]{1,0:T(8,128)S(1)}, u32[]{:S(2)}, u32[]{:S(2)}) collective-permute-start(f32[256,256]{1,0:T(8,128)S(1)} %get-tuple-element.83), channel_id=1, source_target_pairs={{0,12},{4,8},{8,4},{12,0},{16,28},{20,24},{24,20},{28,16},{1,13},{... | collective-permute-start | bytes 786440 | tf_op jit(solution)/shard_map/ppermute | solution.py:233
  174.1 40.6 %collective-permute-start.31 = (f32[256,256]{1,0:T(8,128)S(1)}, f32[256,256]{1,0:T(8,128)S(1)}, u32[]{:S(2)}, u32[]{:S(2)}) collective-permute-start(f32[256,256]{1,0:T(8,128)S(1)} %touch.29), channel_id=1, source_target_pairs={{0,20},{4,16},{8,28},{12,24},{16,4},{20,0},{24,12},{28,8},{1,21},{... | collective-permute-start | bytes 786440 | tf_op jit(solution)/shard_map/ppermute | solution.py:233
  184.4 33.6 %collective-permute-start.28 = (f32[256,256]{1,0:T(8,128)S(1)}, f32[256,256]{1,0:T(8,128)S(1)}, u32[]{:S(2)}, u32[]{:S(2)}) collective-permute-start(f32[256,256]{1,0:T(8,128)S(1)} %touch.27), channel_id=1, source_target_pairs={{0,24},{4,28},{8,16},{12,20},{16,8},{20,12},{24,0},{28,4},{1,25},{... | collective-permute-start | bytes 786440 | tf_op jit(solution)/shard_map/ppermute | solution.py:233
  199.4 24.6 %collective-permute-start.24 = (f32[256,256]{1,0:T(8,128)S(1)}, f32[256,256]{1,0:T(8,128)S(1)}, u32[]{:S(2)}, u32[]{:S(2)}) collective-permute-start(f32[256,256]{1,0:T(8,128)S(1)} %touch.24), channel_id=1, source_target_pairs={{0,28},{4,24},{8,20},{12,16},{16,12},{20,8},{24,4},{28,0},{1,29},{... | collective-permute-start | bytes 786440 | tf_op jit(solution)/shard_map/ppermute | solution.py:233
  199.5 4.7 %copy-start.6 = (f32[1,256,256]{2,1,0:T(8,128)S(1)}, f32[1,256,256]{2,1,0:T(8,128)}, u32[]{:S(2)}) copy-start(f32[1,256,256]{2,1,0:T(8,128)} %get-tuple-element.85.inner_ref) | copy-start | bytes 786436

commit v4 on v3

--- a/solution.py
+++ b/solution.py
@@ -104,7 +104,12 @@
         inner_ref[i] = inner
         message = mm3((send_ref[0], send_ref[1]), inner)
         piece[:width, :] = message[:width] + buffer[i, :width, :]
-        piece[width:, :] = message[width:]
+        piece[width : 2 * width, :] = message[width:]
+        extra = piece.shape[0] - 2 * width
+        for g in range(piece.shape[1] // width if extra else 0):
+            begin = place_ref[1] * (extra * piece.shape[1] // width) + g * extra
+            part = after_ref[pl.ds(pl.multiple_of(begin, 8), extra), :]
+            piece[2 * width :, g * width : (g + 1) * width] = part
 
 
 def nodes_kernel(place_ref, after_ref, pack_ref, pair_ref):
@@ -320,7 +325,7 @@
             name="touch",
         )(value, *after)
 
-    def leaf(chunk, ks, after):
+    def leaf(chunk, ks, after, rider):
         count = len(ks)
         out = pl.pallas_call(
             functools.partial(leaf_kernel, [part(chunk, k) for k in ks]),
@@ -328,13 +333,13 @@
             out_specs=(vmem(),) * (1 + count),
             scratch_shapes=[pltpu.VMEM((count, height, n), F32), pltpu.SemaphoreType.DMA((count,))],
             out_shape=(jax.ShapeDtypeStruct((count, 2 * width, n), F32),)
-            + (jax.ShapeDtypeStruct((2 * width, n), F32),) * count,
+            + (jax.ShapeDtypeStruct((2 * width + rider, n), F32),) * count,
             compiler_params=params(LARGE_LIMIT if chunk == 0 and ks[0] == far[0] else VMEM_LIMIT),
             cost_estimate=cost(
                 2 * 2 * width * (height + 2 * width) * n * count * 3, 4 * n * count * (height + 4 * width)
             ),
             name="leaf",
-        )(place, window, rows_m, send_m, corner(after))
+        )(place, window, rows_m, send_m, after if rider else corner(after))
         return out[0], list(out[1:])
 
     def nodes(pack, after):
@@ -402,8 +407,8 @@
 
     inners, sent = {}, [[None] * rows for _ in range(chunks)]
 
-    def leaves(chunk, ks, after):
-        inner, made = leaf(chunk, ks, after)
+    def leaves(chunk, ks, after, rider=0):
+        inner, made = leaf(chunk, ks, after, rider)
         for i, k in enumerate(ks):
             inners[chunk, k] = inner, i
             sent[chunk][k] = made[i]
@@ -413,9 +418,6 @@
     flat = share
     groups = max(1, n // width)
     extra = flat * width // n
-
-    def fold(pack):
-        return jnp.concatenate([pack[g * extra : (g + 1) * extra] for g in range(groups)], axis=1)
 
     def unfold(rider):
         return jnp.concatenate([rider[:, g * width : (g + 1) * width] for g in range(groups)], axis=0)
@@ -436,7 +438,7 @@
     own = other = None
     for chunk in range(chunks):
         if chunk == 0:
-            after = leaves(0, far[:1], send_m)
+            after = leaves(0, far[:1], dmat, extra)
             leaves(0, far[1:], steps[min(1, len(steps) - 1)])
         else:
             leaves(chunk, far, fars[1])
@@ -445,8 +447,8 @@
             near_trades(chunk, arrived[chunk], sent[chunk])
         for k in far:
             if (chunk, k) == (0, ride):
-                own = fold(lax.dynamic_slice_in_dim(dmat, core * share, share, axis=0))
-                got = far_swap(jnp.concatenate([sent[0][k], own]), k)
+                own = sent[0][k][2 * width :]
+                got = far_swap(sent[0][k], k)
                 arrived[0][k], other = got[: 2 * width], got[2 * width :]
                 nears["leaf"] = leaves(0, [0] + near, steps[-1])
                 arrived[0][0] = sent[0][0]

time: 228 us -> 226 us (level)
  waiting for transfers between devices: 92 us -> 82.5 us
  starting transfers between devices: 51.9 us -> 58.2 us
    ppermute x33, waiting for transfers between devices: 92 us -> 82.5 us  [swap(): lax.ppermute(value, axis, [(i, i ^ k) for i in range(lax.axis_size(axis))])]
    ppermute x33, starting transfers between devices: 51.9 us -> 58.2 us  [swap(): lax.ppermute(value, axis, [(i, i ^ k) for i in range(lax.axis_size(axis))])]
    unnamed x33 -> x32, local copies, waits for them, and re-layouts: 8.74 us -> 9 us
  transfers between devices with their start and end apart: 33 -> 33, of which waited for: 18 -> 15; matrix products, arithmetic and copies ran while one was open for 1% -> 1% of each run, Pallas kernels for 27% -> 27%
where the time goes in v4:
time: 226 us; the launch traced here: 223 us
  waiting for transfers between devices  82.5 us (37%)
  Pallas kernels  62.9 us (28%)
  starting transfers between devices  58.2 us (26%)
  local copies, waits for them, and re-layouts  10.8 us (5%)
  blocking collectives  7.4 us (3%)
    ppermute x33, waiting for transfers between devices, swap(): lax.ppermute(value, axis, [(i, i ^ k) for i in range(lax.axis_size(axis))])  82.5 us
    ppermute x33, starting transfers between devices, swap(): lax.ppermute(value, axis, [(i, i ^ k) for i in range(lax.axis_size(axis))])  58.2 us
    pallas_call x7, Pallas kernels, last(): pl.pallas_call(functools.partial(last_kernel, [part(chunk, k) for k in ks...  22 us
    pallas_call x5, Pallas kernels, leaf(): pl.pallas_call(functools.partial(leaf_kernel, [part(chunk, k) for k in ks...  20.4 us
    pallas_call x2, Pallas kernels, tree(): pl.pallas_call(functools.partial(tree_kernel, rows, order), out_shape=(ja...  9.37 us
    unnamed x32, local copies, waits for them, and re-layouts  9 us
    pallas_call x1, Pallas kernels, nodes(): pl.pallas_call(nodes_kernel, grid_spec=pltpu.PrefetchScalarGridSpec(num_s...  8.04 us
    all_gather x1, blocking collectives, local(): vecs = lax.all_gather(leaf_vecs, 'col', axis=1, tiled=True)  7.4 us
  transfers between devices with their start and end apart: 33, of which 15 were waited for; matrix products, arithmetic and copies ran while one was open for 1% of the time, Pallas kernels for 27%

profile of v4, /device:TPU:8, one launch (start us, length us, event | category | flops | bytes accessed | tf_op | source)
XLA Modules:
  0.0 223.1 jit_solution(14102772285719222308)
XLA Ops:
  0.1 0.9 copy-done.6
  1.0 0.9 copy-done.7
  2.4 2.7 %collective-permute-start = (f32[1,256,128]{2,1,0:T(8,128)S(1)}, f32[1,256,128]{2,1,0:T(8,128)S(1)}, u32[]{:S(2)}, u32[]{:S(2)}) collective-permute-start(f32[1,256,128]{2,1,0:T(8,128)S(1)} %pack.1), channel_id=1, source_target_pairs={{0,16},{4,20},{8,24},{12,28},{16,0},{20,4},{24,8},{28,12},{1,17},{... | collective-permute-start | bytes 393224 | tf_op jit(solution)/shard_map/ppermute | solution.py:238
  5.1 7.4 %all_gather.3.vecs_ref = f32[2,512,128]{2,1,0:T(8,128)S(1)} all-gather(f32[2,128,128]{2,1,0:T(8,128)} %param.6), channel_id=1, replica_groups=mesh['row'=8,'col'=4] {'col'}, dimensions={1}, use_global_device_ids=true | all-gather | bytes 655360 | tf_op jit(solution)/shard_map/all_gather | solution.py:279
  13.1 0.9 copy-done.12
  14.0 1.9 prep.1
  15.9 0.8 copy-done.1
  16.7 0.7 copy-done.3
  17.4 0.6 copy-done.11
  18.0 3.8 %leaf.7 = (f32[1,256,256]{2,1,0:T(8,128)}, f32[288,256]{1,0:T(8,128)}) custom-call(s32[2]{0:T(128)} %copy-done.8, f32[512,4096]{1,0:T(8,128)} %window_ref.23, bf16[2,256,512]{2,1,0:T(8,128)(2,1)} %copy-done.1, bf16[2,256,256]{2,1,0:T(8,128)(2,1)} %copy-done.3, f32[128,128]{1,0:T(8,128)} %copy-done.11), custom_call_target="tpu_custom_call" | custom-call | flops 301989888 | bytes 1048576 | tf_op jit(solution)/shard_map/leaf/pallas_call | solution.py:330
  21.8 1.1 collective-permute-start.5
  22.8 0.8 fusion.14
  23.7 1.6 collective-permute-start.4
  25.2 3.4 %copy-done = f32[512,4096]{1,0:T(8,128)S(1)} copy-done((f32[512,4096]{1,0:T(8,128)S(1)}, f32[512,4096]{1,0:T(8,128)}, u32[]{:S(2)}) %copy-start) | copy-done | bytes 8388632
  28.6 0.7 copy-done.9
  29.3 3.5 %leaf.5 = (f32[3,256,256]{2,1,0:T(8,128)S(1)}, f32[256,256]{1,0:T(8,128)S(1)}, f32[256,256]{1,0:T(8,128)S(1)}, f32[256,256]{1,0:T(8,128)S(1)}) custom-call(s32[2]{0:T(128)S(1)} %copy-done.9, f32[512,4096]{1,0:T(8,128)S(1)} %copy-done, bf16[2,256,512]{2,1,0:T(8,128)(2,1)S(1)} %copy-done.2, bf16[2,256,256]{2,1,0:T(8,128)(2,1)S(1)} %copy-done.4, ...), custom_call_target="tpu_custom_call" | custom-call | flops 905969664 | bytes 3145728 | tf_op jit(solution)/shard_map/leaf/pallas_call | solution.py:330
  32.8 2.0 collective-permute-start.2
  34.8 0.8 slice.196
  35.5 1.5 collective-permute-start.3
  37.1 11.0 %collective-permute-done.5 = f32[288,256]{1,0:T(8,128)S(1)} collective-permute-done((f32[288,256]{1,0:T(8,128)}, f32[288,256]{1,0:T(8,128)S(1)}, u32[]{:S(2)}, u32[]{:S(2)}) %collective-permute-start.5) | collective-permute-done | bytes 294944 | tf_op jit(solution)/shard_map/ppermute | solution.py:238
  48.1 5.5 %collective-permute-done.2.refs_1_ = f32[256,256]{1,0:T(8,128)S(1)} collective-permute-done((f32[256,256]{1,0:T(8,128)S(1)}, f32[256,256]{1,0:T(8,128)S(1)}, u32[]{:S(2)}, u32[]{:S(2)}) %collective-permute-start.2) | collective-permute-done | bytes 262176 | tf_op jit(solution)/shard_map/ppermute | solution.py:238
  53.6 4.4 %leaf.6 = (f32[4,256,256]{2,1,0:T(8,128)S(1)}, f32[256,256]{1,0:T(8,128)S(1)}, f32[256,256]{1,0:T(8,128)S(1)}, f32[256,256]{1,0:T(8,128)S(1)}, f32[256,256]{1,0:T(8,128)S(1)}) custom-call(s32[2]{0:T(128)S(1)} %copy-done.10, f32[512,4096]{1,0:T(8,128)S(1)} %copy-done, bf16[2,256,512]{2,1,0:T(8,128)(2,1)S(1)} %copy-done.2, bf16[2,256,256]{2,1,0:T(8,128)(2,1)S(1)} %copy-done.4, ...), custom_call_target="tpu_custom_call" | custom-call | flops 1207959552 | bytes 4194304 | tf_op jit(solution)/shard_map/leaf/pallas_call | solution.py:330
  58.1 4.4 %collective-permute-start.10 = (f32[256,256]{1,0:T(8,128)S(1)}, f32[256,256]{1,0:T(8,128)S(1)}, u32[]{:S(2)}, u32[]{:S(2)}) collective-permute-start(f32[256,256]{1,0:T(8,128)S(1)} %touch.16), channel_id=1, source_target_pairs={{0,16},{4,20},{8,24},{12,28},{16,0},{20,4},{24,8},{28,12},{1,17},{... | collective-permute-start | bytes 786440 | tf_op jit(solution)/shard_map/ppermute | solution.py:238
  62.4 4.4 %leaf.8 = (f32[4,256,256]{2,1,0:T(8,128)S(1)}, f32[256,256]{1,0:T(8,128)S(1)}, f32[256,256]{1,0:T(8,128)S(1)}, f32[256,256]{1,0:T(8,128)S(1)}, f32[256,256]{1,0:T(8,128)S(1)}) custom-call(s32[2]{0:T(128)S(1)} %copy-done.10, f32[512,4096]{1,0:T(8,128)S(1)} %copy-done, bf16[2,256,512]{2,1,0:T(8,128)(2,1)S(1)} %copy-done.2, bf16[2,256,256]{2,1,0:T(8,128)(2,1)S(1)} %copy-done.4, ...), custom_call_target="tpu_custom_call" | custom-call | flops 1207959552 | bytes 4194304 | tf_op jit(solution)/shard_map/leaf/pallas_call | solution.py:330
  67.5 5.5 %collective-permute-start.7 = (f32[320,256]{1,0:T(8,128)S(1)}, f32[320,256]{1,0:T(8,128)S(1)}, u32[]{:S(2)}, u32[]{:S(2)}) collective-permute-start(f32[320,256]{1,0:T(8,128)S(1)} %get-tuple-element.107), channel_id=1, source_target_pairs={{0,4},{4,0},{8,12},{12,8},{16,20},{20,16},{24,28},{28,24},{1,5},{5... | collective-permute-start | bytes 983048 | tf_op jit(solution)/shard_map/ppermute | solution.py:238
  73.1 1.5 collective-permute-start.8
  74.6 9.5 %collective-permute-done.9 = f32[320,256]{1,0:T(8,128)S(1)} collective-permute-done((f32[320,256]{1,0:T(8,128)S(1)}, f32[320,256]{1,0:T(8,128)S(1)}, u32[]{:S(2)}, u32[]{:S(2)}) %collective-permute-start.9) | collective-permute-done | bytes 327712 | tf_op jit(solution)/shard_map/ppermute | solution.py:238
  84.1 4.4 %leaf.9 = (f32[4,256,256]{2,1,0:T(8,128)S(1)}, f32[256,256]{1,0:T(8,128)S(1)}, f32[256,256]{1,0:T(8,128)S(1)}, f32[256,256]{1,0:T(8,128)S(1)}, f32[256,256]{1,0:T(8,128)S(1)}) custom-call(s32[2]{0:T(128)S(1)} %copy-done.10, f32[512,4096]{1,0:T(8,128)S(1)} %bitcast.56, bf16[2,256,512]{2,1,0:T(8,128)(2,1)S(1)} %copy-done.2, ...), custom_call_target="tpu_custom_call" | custom-call | flops 1207959552 | bytes 4194304 | tf_op jit(solution)/shard_map/leaf/pallas_call | solution.py:330
  88.6 2.2 collective-permute-start.15
  90.8 0.8 collective-permute-done.8
  91.7 2.6 %collective-permute-start.17 = (f32[256,256]{1,0:T(8,128)S(1)}, f32[256,256]{1,0:T(8,128)S(1)}, u32[]{:S(2)}, u32[]{:S(2)}) collective-permute-start(f32[256,256]{1,0:T(8,128)S(1)} %get-tuple-element.64), channel_id=1, source_target_pairs={{0,8},{4,12},{8,0},{12,4},{16,24},{20,28},{24,16},{28,20},{1,9},{5... | collective-permute-start | bytes 786440 | tf_op jit(solution)/shard_map/ppermute | solution.py:238
  94.8 1.6 collective-permute-done.15.refs_4_
  96.4 5.8 %collective-permute-start.18 = (f32[256,256]{1,0:T(8,128)S(1)}, f32[256,256]{1,0:T(8,128)S(1)}, u32[]{:S(2)}, u32[]{:S(2)}) collective-permute-start(f32[256,256]{1,0:T(8,128)S(1)} %get-tuple-element.65), channel_id=1, source_target_pairs={{0,12},{4,8},{8,4},{12,0},{16,28},{20,24},{24,20},{28,16},{1,13},{... | collective-permute-start | bytes 786440 | tf_op jit(solution)/shard_map/ppermute | solution.py:238
  102.3 1.6 collective-permute-done.17.refs_5_
  103.9 3.4 %collective-permute-start.14 = (f32[256,256]{1,0:T(8,128)S(1)}, f32[256,256]{1,0:T(8,128)S(1)}, u32[]{:S(2)}, u32[]{:S(2)}) collective-permute-start(f32[256,256]{1,0:T(8,128)S(1)} %touch.20), channel_id=1, source_target_pairs={{0,24},{4,28},{8,16},{12,20},{16,8},{20,12},{24,0},{28,4},{1,25},{... | collective-permute-start | bytes 786440 | tf_op jit(solution)/shard_map/ppermute | solution.py:238
  107.3 3.7 %collective-permute-start.16 = (f32[256,256]{1,0:T(8,128)S(1)}, f32[256,256]{1,0:T(8,128)S(1)}, u32[]{:S(2)}, u32[]{:S(2)}) collective-permute-start(f32[256,256]{1,0:T(8,128)S(1)} %touch.21), channel_id=1, source_target_pairs={{0,28},{4,24},{8,20},{12,16},{16,12},{20,8},{24,4},{28,0},{1,29},{... | collective-permute-start | bytes 786440 | tf_op jit(solution)/shard_map/ppermute | solution.py:238
  111.3 8.0 %nodes.1.pair_ref = bf16[2,2,8,256,256]{4,3,2,1,0:T(8,128)(2,1)S(1)} custom-call(s32[2]{0:T(128)S(1)} %copy-done.10, f32[8,128]{1,0:T(8,128)S(1)} %slice.241.after_ref.refs_1_, f32[2,8,256,128]{3,2,1,0:T(8,128)S(1)} %pad_maximum_fusion.pack_ref), custom_call_target="tpu_custom_call" | custom-call | flops 1207959552 | bytes 8388608 | tf_op jit(solution)/shard_map/nodes/pallas_call | solution.py:346
  119.4 4.7 %tree.3 = (f32[256,256]{1,0:T(8,128)S(1)}, f32[256,256]{1,0:T(8,128)S(1)}, f32[256,256]{1,0:T(8,128)S(1)}, f32[256,256]{1,0:T(8,128)S(1)}, f32[256,256]{1,0:T(8,...) custom-call(s32[2]{0:T(128)S(1)} %copy-done.10, ...), custom_call_target="tpu_custom_call" | custom-call | flops 3221225472 | bytes 8388608 | tf_op jit(solution)/shard_map/tree/pallas_call | solution.py:364
  124.1 3.1 %collective-permute-start.25 = (f32[256,256]{1,0:T(8,128)S(1)}, f32[256,256]{1,0:T(8,128)S(1)}, u32[]{:S(2)}, u32[]{:S(2)}) collective-permute-start(f32[256,256]{1,0:T(8,128)S(1)} %touch.25), channel_id=1, source_target_pairs={{0,16},{4,20},{8,24},{12,28},{16,0},{20,4},{24,8},{28,12},{1,17},{... | collective-permute-start | bytes 786440 | tf_op jit(solution)/shard_map/ppermute | solution.py:238
  127.3 10.4 %collective-permute-done.16.refs_3_ = f32[256,256]{1,0:T(8,128)S(1)} collective-permute-done((f32[256,256]{1,0:T(8,128)S(1)}, f32[256,256]{1,0:T(8,128)S(1)}, u32[]{:S(2)}, u32[]{:S(2)}) %collective-permute-start.16) | collective-permute-done | bytes 262176 | tf_op jit(solution)/shard_map/ppermute | solution.py:238
  137.8 1.3 collective-permute-start.20
  139.1 2.7 %collective-permute-start.27 = (f32[256,256]{1,0:T(8,128)S(1)}, f32[256,256]{1,0:T(8,128)S(1)}, u32[]{:S(2)}, u32[]{:S(2)}) collective-permute-start(f32[256,256]{1,0:T(8,128)S(1)} %get-tuple-element.77), channel_id=1, source_target_pairs={{0,12},{4,8},{8,4},{12,0},{16,28},{20,24},{24,20},{28,16},{1,13},{... | collective-permute-start | bytes 786440 | tf_op jit(solution)/shard_map/ppermute | solution.py:238
  141.9 4.0 %collective-permute-done.25.refs_0_ = f32[256,256]{1,0:T(8,128)S(1)} collective-permute-done((f32[256,256]{1,0:T(8,128)S(1)}, f32[256,256]{1,0:T(8,128)S(1)}, u32[]{:S(2)}, u32[]{:S(2)}) %collective-permute-start.25) | collective-permute-done | bytes 262176 | tf_op jit(solution)/shard_map/ppermute | solution.py:238
  145.9 0.6 collective-permute-start.29
  146.5 4.7 %tree.2 = (f32[256,256]{1,0:T(8,128)S(1)}, f32[256,256]{1,0:T(8,128)S(1)}, f32[256,256]{1,0:T(8,128)S(1)}, f32[256,256]{1,0:T(8,128)S(1)}, f32[256,256]{1,0:T(8,...) custom-call(s32[2]{0:T(128)S(1)} %copy-done.10, ...), custom_call_target="tpu_custom_call" | custom-call | flops 3221225472 | bytes 8388608 | tf_op jit(solution)/shard_map/tree/pallas_call | solution.py:364
  151.2 2.5 %collective-permute-done.19.refs_0_ = f32[256,256]{1,0:T(8,128)S(1)} collective-permute-done((f32[256,256]{1,0:T(8,128)S(1)}, f32[256,256]{1,0:T(8,128)S(1)}, u32[]{:S(2)}, u32[]{:S(2)}) %collective-permute-start.19) | collective-permute-done | bytes 262176 | tf_op jit(solution)/shard_map/ppermute | solution.py:238
  153.8 3.6 %collective-permute-done.20.refs_1_ = f32[256,256]{1,0:T(8,128)S(1)} collective-permute-done((f32[256,256]{1,0:T(8,128)S(1)}, f32[256,256]{1,0:T(8,128)S(1)}, u32[]{:S(2)}, u32[]{:S(2)}) %collective-permute-start.20) | collective-permute-done | bytes 262176 | tf_op jit(solution)/shard_map/ppermute | solution.py:238
  157.5 1.9 collective-permute-start.26
  159.4 6.8 %collective-permute-done.30.refs_2_ = f32[256,256]{1,0:T(8,128)S(1)} collective-permute-done((f32[256,256]{1,0:T(8,128)S(1)}, f32[256,256]{1,0:T(8,128)S(1)}, u32[]{:S(2)}, u32[]{:S(2)}) %collective-permute-start.30) | collective-permute-done | bytes 262176 | tf_op jit(solution)/shard_map/ppermute | solution.py:238
  166.2 5.8 %collective-permute-start.21 = (f32[256,256]{1,0:T(8,128)S(1)}, f32[256,256]{1,0:T(8,128)S(1)}, u32[]{:S(2)}, u32[]{:S(2)}) collective-permute-start(f32[256,256]{1,0:T(8,128)S(1)} %touch.23), channel_id=1, source_target_pairs={{0,16},{4,20},{8,24},{12,28},{16,0},{20,4},{24,8},{28,12},{1,17},{... | collective-permute-start | bytes 786440 | tf_op jit(solution)/shard_map/ppermute | solution.py:238
  172.1 1.1 collective-permute-start.31
  173.3 3.0 %collective-permute-done.23.refs_2_ = f32[256,256]{1,0:T(8,128)S(1)} collective-permute-done((f32[256,256]{1,0:T(8,128)S(1)}, f32[256,256]{1,0:T(8,128)S(1)}, u32[]{:S(2)}, u32[]{:S(2)}) %collective-permute-start.23) | collective-permute-done | bytes 262176 | tf_op jit(solution)/shard_map/ppermute | solution.py:238
  176.3 6.4 %collective-permute-done.26.refs_2_ = f32[256,256]{1,0:T(8,128)S(1)} collective-permute-done((f32[256,256]{1,0:T(8,128)S(1)}, f32[256,256]{1,0:T(8,128)S(1)}, u32[]{:S(2)}, u32[]{:S(2)}) %collective-permute-start.26) | collective-permute-done | bytes 262176 | tf_op jit(solution)/shard_map/ppermute | solution.py:238
  182.7 0.6 collective-permute-start.28
  183.3 13.9 %collective-permute-done.21.refs_0_ = f32[256,256]{1,0:T(8,128)S(1)} collective-permute-done((f32[256,256]{1,0:T(8,128)S(1)}, f32[256,256]{1,0:T(8,128)S(1)}, u32[]{:S(2)}, u32[]{:S(2)}) %collective-permute-start.21) | collective-permute-done | bytes 262176 | tf_op jit(solution)/shard_map/ppermute | solution.py:238
  197.3 1.9 collective-permute-start.24
  199.2 4.7 %last.7.refs_1_ = f32[512,4096]{1,0:T(8,128)} custom-call(s32[2]{0:T(128)S(1)} %copy-done.10, f32[512,4096]{1,0:T(8,128)S(1)} %bitcast.56, f32[4,256,256]{2,1,0:T(8,128)S(1)} %get-tuple-element.61.inner_ref, bf16[2,384,384]{2,1,0:T(8,128)(2,1)S(1)} %get-tuple-element.50.rest_ref, f32[256,256]{1,0:T(8,128)S(1)} %get-tuple-element.86.refs_0_, ...), custom_call_target="tpu_custom_call" | custom-call | flops 905969664 | bytes 6291456 | tf_op jit(solution)/shard_map/last/pallas_call | solution.py:385
  203.9 1.9 last.8.refs_3_
  205.8 3.6 %last.9.refs_4_ = f32[512,4096]{1,0:T(8,128)} custom-call(s32[2]{0:T(128)S(1)} %copy-done.10, f32[512,4096]{1,0:T(8,128)S(1)} %bitcast.56, f32[3,256,256]{2,1,0:T(8,128)S(1)} %get-tuple-element.84.inner_ref, bf16[2,384,384]{2,1,0:T(8,128)(2,1)S(1)} %get-tuple-element.50.rest_ref, ...), custom_call_target="tpu_custom_call", output_to_operand_aliasing={{}: (7, {})} | custom-call | flops 679477248 | bytes 4718592 | tf_op jit(solution)/shard_map/last/pallas_call | solution.py:385
  209.4 4.9 %last.10.refs_2_ = f32[512,4096]{1,0:T(8,128)} custom-call(s32[2]{0:T(128)S(1)} %copy-done.10, f32[512,4096]{1,0:T(8,128)S(1)} %bitcast.56, f32[4,256,256]{2,1,0:T(8,128)S(1)} %get-tuple-element.81.inner_ref, bf16[2,384,384]{2,1,0:T(8,128)(2,1)S(1)} %get-tuple-element.50.rest_ref, ...), custom_call_target="tpu_custom_call", output_to_operand_aliasing={{}: (8, {})} | custom-call | flops 905969664 | bytes 6291456 | tf_op jit(solution)/shard_map/last/pallas_call | solution.py:385
  214.4 3.1 %last.11.refs_1_ = f32[512,4096]{1,0:T(8,128)} custom-call(s32[2]{0:T(128)S(1)} %copy-done.10, f32[512,4096]{1,0:T(8,128)S(1)} %bitcast.56, f32[4,256,256]{2,1,0:T(8,128)S(1)} %get-tuple-element.49.inner_ref, bf16[2,384,384]{2,1,0:T(8,128)(2,1)S(1)} %get-tuple-element.50.rest_ref, ...), custom_call_target="tpu_custom_call", output_to_operand_aliasing={{}: (6, {})} | custom-call | flops 452984832 | bytes 3145728 | tf_op jit(solution)/shard_map/last/pallas_call | solution.py:385
  217.5 1.9 last.12.refs_1_
  219.4 1.7 collective-permute-done.24.refs_0_
  221.0 1.9 last.13
  (124 shorter events, 3.3 us)
Async XLA Ops:
  0.1 0.9 copy-start.6
  1.0 0.9 copy-start.7
  1.9 16.1 %copy-start.8 = (s32[2]{0:T(128)}, s32[2]{0:T(128)S(1)}, u32[]{:S(2)}) copy-start(s32[2]{0:T(128)S(1)} %pad_add_fusion.place_ref) | copy-start | bytes 28
  2.4 10.1 %collective-permute-start = (f32[1,256,128]{2,1,0:T(8,128)S(1)}, f32[1,256,128]{2,1,0:T(8,128)S(1)}, u32[]{:S(2)}, u32[]{:S(2)}) collective-permute-start(f32[1,256,128]{2,1,0:T(8,128)S(1)} %pack.1), channel_id=1, source_target_pairs={{0,16},{4,20},{8,24},{12,28},{16,0},{20,4},{24,8},{28,12},{1,17},{... | collective-permute-start | bytes 393224 | tf_op jit(solution)/shard_map/ppermute | solution.py:238
  12.5 11.1 %collective-permute-start.1 = (f32[2,256,128]{2,1,0:T(8,128)S(1)}, f32[2,256,128]{2,1,0:T(8,128)S(1)}, u32[]{:S(2)}, u32[]{:S(2)}) collective-permute-start(f32[2,256,128]{2,1,0:T(8,128)S(1)} %get-tuple-element.104), channel_id=1, source_target_pairs={{0,8},{4,12},{8,0},{12,4},{16,24},{20,28},{24,16},{28,20},{1,9},{5... | collective-permute-start | bytes 786440 | tf_op jit(solution)/shard_map/ppermute | solution.py:238
  13.1 0.9 copy-start.12
  15.9 0.8 copy-start.1
  16.7 0.7 copy-start.3
  17.4 0.6 copy-start.11
  18.0 7.2 %copy-start.2 = (bf16[2,256,512]{2,1,0:T(8,128)(2,1)S(1)}, bf16[2,256,512]{2,1,0:T(8,128)(2,1)}, u32[]{:S(2)}) copy-start(bf16[2,256,512]{2,1,0:T(8,128)(2,1)} %copy-done.1) | copy-start | bytes 1572868
  18.0 7.2 %copy-start.4 = (bf16[2,256,256]{2,1,0:T(8,128)(2,1)S(1)}, bf16[2,256,256]{2,1,0:T(8,128)(2,1)}, u32[]{:S(2)}) copy-start(bf16[2,256,256]{2,1,0:T(8,128)(2,1)} %copy-done.3) | copy-start | bytes 786436
  21.8 31.9 %copy-start.10 = (s32[2]{0:T(128)S(1)}, s32[2]{0:T(128)}, u32[]{:S(2)}) copy-start(s32[2]{0:T(128)} %copy-done.8) | copy-start | bytes 28
  21.8 26.3 %collective-permute-start.5 = (f32[288,256]{1,0:T(8,128)}, f32[288,256]{1,0:T(8,128)S(1)}, u32[]{:S(2)}, u32[]{:S(2)}) collective-permute-start(f32[288,256]{1,0:T(8,128)} %get-tuple-element.53), channel_id=1, source_target_pairs={{0,16},{4,20},{8,24},{12,28},{16,0},{20,4},{24,8},{28,12},{1,17},{... | collective-permute-start | bytes 884744 | tf_op jit(solution)/shard_map/ppermute | solution.py:238
  23.7 38.7 %collective-permute-start.4 = (f32[4,256,128]{2,1,0:T(8,128)S(1)}, f32[4,256,128]{2,1,0:T(8,128)S(1)}, u32[]{:S(2)}, u32[]{:S(2)}) collective-permute-start(f32[4,256,128]{2,1,0:T(8,128)S(1)} %bitcast.61), channel_id=1, source_target_pairs={{0,4},{4,0},{8,12},{12,8},{16,20},{20,16},{24,28},{28,24},{1,5},{5... | collective-permute-start | bytes 1572872 | tf_op jit(solution)/shard_map/ppermute | solution.py:238
  25.2 3.4 %copy-start = (f32[512,4096]{1,0:T(8,128)S(1)}, f32[512,4096]{1,0:T(8,128)}, u32[]{:S(2)}) copy-start(f32[512,4096]{1,0:T(8,128)} %window_ref.23) | copy-start | bytes 25165828
  28.6 0.7 copy-start.9
  32.8 20.8 %collective-permute-start.2 = (f32[256,256]{1,0:T(8,128)S(1)}, f32[256,256]{1,0:T(8,128)S(1)}, u32[]{:S(2)}, u32[]{:S(2)}) collective-permute-start(f32[256,256]{1,0:T(8,128)S(1)} %get-tuple-element.48), channel_id=1, source_target_pairs={{0,20},{4,16},{8,28},{12,24},{16,4},{20,0},{24,12},{28,8},{1,21},{... | collective-permute-start | bytes 786440 | tf_op jit(solution)/shard_map/ppermute | solution.py:238
  35.5 26.9 %collective-permute-start.3 = (f32[256,256]{1,0:T(8,128)S(1)}, f32[256,256]{1,0:T(8,128)S(1)}, u32[]{:S(2)}, u32[]{:S(2)}) collective-permute-start(f32[256,256]{1,0:T(8,128)S(1)} %get-tuple-element.51), channel_id=1, source_target_pairs={{0,24},{4,28},{8,16},{12,20},{16,8},{20,12},{24,0},{28,4},{1,25},{... | collective-permute-start | bytes 786440 | tf_op jit(solution)/shard_map/ppermute | solution.py:238
  58.1 15.1 %collective-permute-start.10 = (f32[256,256]{1,0:T(8,128)S(1)}, f32[256,256]{1,0:T(8,128)S(1)}, u32[]{:S(2)}, u32[]{:S(2)}) collective-permute-start(f32[256,256]{1,0:T(8,128)S(1)} %touch.16), channel_id=1, source_target_pairs={{0,16},{4,20},{8,24},{12,28},{16,0},{20,4},{24,8},{28,12},{1,17},{... | collective-permute-start | bytes 786440 | tf_op jit(solution)/shard_map/ppermute | solution.py:238
  62.4 21.7 %slice-start = ((s8[8388608]{0:T(1024)(128)(4,1)}), s8[4194304]{0:T(1024)(128)(4,1)S(1)}, s32[]{:S(2)}) async-start(s8[8388608]{0:T(1024)(128)(4,1)} %bitcast.55), calls=%async_computation | async-start | bytes 8388608
  66.8 17.3 %slice-start.1 = ((s8[8388608]{0:T(1024)(128)(4,1)}), s8[4194304]{0:T(1024)(128)(4,1)S(1)}, s32[]{:S(2)}) async-start(s8[8388608]{0:T(1024)(128)(4,1)} %bitcast.55), calls=%async_computation.1 | async-start | bytes 8388608
  66.9 17.2 %collective-permute-start.9 = (f32[320,256]{1,0:T(8,128)S(1)}, f32[320,256]{1,0:T(8,128)S(1)}, u32[]{:S(2)}, u32[]{:S(2)}) collective-permute-start(f32[320,256]{1,0:T(8,128)S(1)} %get-tuple-element.105), channel_id=1, source_target_pairs={{0,12},{4,8},{8,4},{12,0},{16,28},{20,24},{24,20},{28,16},{1,13},{... | collective-permute-start | bytes 983048 | tf_op jit(solution)/shard_map/ppermute | solution.py:238
  67.4 43.7 %collective-permute-start.6 = (f32[8,256,128]{2,1,0:T(8,128)S(1)}, f32[8,256,128]{2,1,0:T(8,128)S(1)}, u32[]{:S(2)}, u32[]{:S(2)}) collective-permute-start(f32[8,256,128]{2,1,0:T(8,128)S(1)} %touch.15), channel_id=1, source_target_pairs={{0,1},{1,0},{2,3},{3,2},{4,5},{5,4},{6,7},{7,6},{8,9},{9,8},{10,11... | collective-permute-start | bytes 3145736 | tf_op jit(solution)/shard_map/ppermute | solution.py:238
  67.5 23.3 %collective-permute-start.7 = (f32[320,256]{1,0:T(8,128)S(1)}, f32[320,256]{1,0:T(8,128)S(1)}, u32[]{:S(2)}, u32[]{:S(2)}) collective-permute-start(f32[320,256]{1,0:T(8,128)S(1)} %get-tuple-element.107), channel_id=1, source_target_pairs={{0,4},{4,0},{8,12},{12,8},{16,20},{20,16},{24,28},{28,24},{1,5},{5... | collective-permute-start | bytes 983048 | tf_op jit(solution)/shard_map/ppermute | solution.py:238
  73.0 21.5 %collective-permute-start.13 = (f32[256,256]{1,0:T(8,128)S(1)}, f32[256,256]{1,0:T(8,128)S(1)}, u32[]{:S(2)}, u32[]{:S(2)}) collective-permute-start(f32[256,256]{1,0:T(8,128)S(1)} %touch.19), channel_id=1, source_target_pairs={{0,28},{4,24},{8,20},{12,16},{16,12},{20,8},{24,4},{28,0},{1,29},{... | collective-permute-start | bytes 786440 | tf_op jit(solution)/shard_map/ppermute | solution.py:238
  73.1 18.4 %collective-permute-start.8 = (f32[320,256]{1,0:T(8,128)S(1)}, f32[320,256]{1,0:T(8,128)S(1)}, u32[]{:S(2)}, u32[]{:S(2)}) collective-permute-start(f32[320,256]{1,0:T(8,128)S(1)} %get-tuple-element.106), channel_id=1, source_target_pairs={{0,8},{4,12},{8,0},{12,4},{16,24},{20,28},{24,16},{28,20},{1,9},{5... | collective-permute-start | bytes 983048 | tf_op jit(solution)/shard_map/ppermute | solution.py:238
  88.6 7.8 %collective-permute-start.15 = (f32[256,256]{1,0:T(8,128)S(1)}, f32[256,256]{1,0:T(8,128)S(1)}, u32[]{:S(2)}, u32[]{:S(2)}) collective-permute-start(f32[256,256]{1,0:T(8,128)S(1)} %get-tuple-element.63), channel_id=1, source_target_pairs={{0,4},{4,0},{8,12},{12,8},{16,20},{20,16},{24,28},{28,24},{1,5},{5... | collective-permute-start | bytes 786440 | tf_op jit(solution)/shard_map/ppermute | solution.py:238
  91.7 12.3 %collective-permute-start.17 = (f32[256,256]{1,0:T(8,128)S(1)}, f32[256,256]{1,0:T(8,128)S(1)}, u32[]{:S(2)}, u32[]{:S(2)}) collective-permute-start(f32[256,256]{1,0:T(8,128)S(1)} %get-tuple-element.64), channel_id=1, source_target_pairs={{0,8},{4,12},{8,0},{12,4},{16,24},{20,28},{24,16},{28,20},{1,9},{5... | collective-permute-start | bytes 786440 | tf_op jit(solution)/shard_map/ppermute | solution.py:238
  94.3 13.0 %collective-permute-start.12 = (f32[256,256]{1,0:T(8,128)S(1)}, f32[256,256]{1,0:T(8,128)S(1)}, u32[]{:S(2)}, u32[]{:S(2)}) collective-permute-start(f32[256,256]{1,0:T(8,128)S(1)} %touch.18), channel_id=1, source_target_pairs={{0,20},{4,16},{8,28},{12,24},{16,4},{20,0},{24,12},{28,8},{1,21},{... | collective-permute-start | bytes 786440 | tf_op jit(solution)/shard_map/ppermute | solution.py:238
  94.5 16.5 %collective-permute-start.11 = (f32[8,64,128]{2,1,0:T(8,128)S(1)}, f32[8,64,128]{2,1,0:T(8,128)S(1)}, u32[]{:S(2)}, u32[]{:S(2)}) collective-permute-start(f32[8,64,128]{2,1,0:T(8,128)S(1)} %touch.17), channel_id=1, source_target_pairs={{0,1},{1,0},{2,3},{3,2},{4,5},{5,4},{6,7},{7,6},{8,9},{9,8},{10,11... | collective-permute-start | bytes 786440 | tf_op jit(solution)/shard_map/ppermute | solution.py:238
  96.4 30.8 %collective-permute-start.18 = (f32[256,256]{1,0:T(8,128)S(1)}, f32[256,256]{1,0:T(8,128)S(1)}, u32[]{:S(2)}, u32[]{:S(2)}) collective-permute-start(f32[256,256]{1,0:T(8,128)S(1)} %get-tuple-element.65), channel_id=1, source_target_pairs={{0,12},{4,8},{8,4},{12,0},{16,28},{20,24},{24,20},{28,16},{1,13},{... | collective-permute-start | bytes 786440 | tf_op jit(solution)/shard_map/ppermute | solution.py:238
  103.9 23.3 %collective-permute-start.14 = (f32[256,256]{1,0:T(8,128)S(1)}, f32[256,256]{1,0:T(8,128)S(1)}, u32[]{:S(2)}, u32[]{:S(2)}) collective-permute-start(f32[256,256]{1,0:T(8,128)S(1)} %touch.20), channel_id=1, source_target_pairs={{0,24},{4,28},{8,16},{12,20},{16,8},{20,12},{24,0},{28,4},{1,25},{... | collective-permute-start | bytes 786440 | tf_op jit(solution)/shard_map/ppermute | solution.py:238
  107.3 30.3 %collective-permute-start.16 = (f32[256,256]{1,0:T(8,128)S(1)}, f32[256,256]{1,0:T(8,128)S(1)}, u32[]{:S(2)}, u32[]{:S(2)}) collective-permute-start(f32[256,256]{1,0:T(8,128)S(1)} %touch.21), channel_id=1, source_target_pairs={{0,28},{4,24},{8,20},{12,16},{16,12},{20,8},{24,4},{28,0},{1,29},{... | collective-permute-start | bytes 786440 | tf_op jit(solution)/shard_map/ppermute | solution.py:238
  124.1 21.8 %collective-permute-start.25 = (f32[256,256]{1,0:T(8,128)S(1)}, f32[256,256]{1,0:T(8,128)S(1)}, u32[]{:S(2)}, u32[]{:S(2)}) collective-permute-start(f32[256,256]{1,0:T(8,128)S(1)} %touch.25), channel_id=1, source_target_pairs={{0,16},{4,20},{8,24},{12,28},{16,0},{20,4},{24,8},{28,12},{1,17},{... | collective-permute-start | bytes 786440 | tf_op jit(solution)/shard_map/ppermute | solution.py:238
  137.7 16.1 %collective-permute-start.19 = (f32[256,256]{1,0:T(8,128)S(1)}, f32[256,256]{1,0:T(8,128)S(1)}, u32[]{:S(2)}, u32[]{:S(2)}) collective-permute-start(f32[256,256]{1,0:T(8,128)S(1)} %touch.22), channel_id=1, source_target_pairs={{0,20},{4,16},{8,28},{12,24},{16,4},{20,0},{24,12},{28,8},{1,21},{... | collective-permute-start | bytes 786440 | tf_op jit(solution)/shard_map/ppermute | solution.py:238
  137.8 19.7 %collective-permute-start.20 = (f32[256,256]{1,0:T(8,128)S(1)}, f32[256,256]{1,0:T(8,128)S(1)}, u32[]{:S(2)}, u32[]{:S(2)}) collective-permute-start(f32[256,256]{1,0:T(8,128)S(1)} %get-tuple-element.71), channel_id=1, source_target_pairs={{0,4},{4,0},{8,12},{12,8},{16,20},{20,16},{24,28},{28,24},{1,5},{5... | collective-permute-start | bytes 786440 | tf_op jit(solution)/shard_map/ppermute | solution.py:238
  139.1 18.3 %collective-permute-start.27 = (f32[256,256]{1,0:T(8,128)S(1)}, f32[256,256]{1,0:T(8,128)S(1)}, u32[]{:S(2)}, u32[]{:S(2)}) collective-permute-start(f32[256,256]{1,0:T(8,128)S(1)} %get-tuple-element.77), channel_id=1, source_target_pairs={{0,12},{4,8},{8,4},{12,0},{16,28},{20,24},{24,20},{28,16},{1,13},{... | collective-permute-start | bytes 786440 | tf_op jit(solution)/shard_map/ppermute | solution.py:238
  141.9 24.3 %collective-permute-start.30 = (f32[256,256]{1,0:T(8,128)S(1)}, f32[256,256]{1,0:T(8,128)S(1)}, u32[]{:S(2)}, u32[]{:S(2)}) collective-permute-start(f32[256,256]{1,0:T(8,128)S(1)} %get-tuple-element.80), channel_id=1, source_target_pairs={{0,8},{4,12},{8,0},{12,4},{16,24},{20,28},{24,16},{28,20},{1,9},{5... | collective-permute-start | bytes 786440 | tf_op jit(solution)/shard_map/ppermute | solution.py:238
  145.9 26.1 %collective-permute-start.29 = (f32[256,256]{1,0:T(8,128)S(1)}, f32[256,256]{1,0:T(8,128)S(1)}, u32[]{:S(2)}, u32[]{:S(2)}) collective-permute-start(f32[256,256]{1,0:T(8,128)S(1)} %touch.28), channel_id=1, source_target_pairs={{0,24},{4,28},{8,16},{12,20},{16,8},{20,12},{24,0},{28,4},{1,25},{... | collective-permute-start | bytes 786440 | tf_op jit(solution)/shard_map/ppermute | solution.py:238
  153.8 18.4 %collective-permute-start.22 = (f32[256,256]{1,0:T(8,128)S(1)}, f32[256,256]{1,0:T(8,128)S(1)}, u32[]{:S(2)}, u32[]{:S(2)}) collective-permute-start(f32[256,256]{1,0:T(8,128)S(1)} %get-tuple-element.72), channel_id=1, source_target_pairs={{0,4},{4,0},{8,12},{12,8},{16,20},{20,16},{24,28},{28,24},{1,5},{5... | collective-permute-start | bytes 786440 | tf_op jit(solution)/shard_map/ppermute | solution.py:238
  157.5 18.8 %collective-permute-start.23 = (f32[256,256]{1,0:T(8,128)S(1)}, f32[256,256]{1,0:T(8,128)S(1)}, u32[]{:S(2)}, u32[]{:S(2)}) collective-permute-start(f32[256,256]{1,0:T(8,128)S(1)} %get-tuple-element.73), channel_id=1, source_target_pairs={{0,8},{4,12},{8,0},{12,4},{16,24},{20,28},{24,16},{28,20},{1,9},{5... | collective-permute-start | bytes 786440 | tf_op jit(solution)/shard_map/ppermute | solution.py:238
  157.5 25.2 %collective-permute-start.26 = (f32[256,256]{1,0:T(8,128)S(1)}, f32[256,256]{1,0:T(8,128)S(1)}, u32[]{:S(2)}, u32[]{:S(2)}) collective-permute-start(f32[256,256]{1,0:T(8,128)S(1)} %touch.26), channel_id=1, source_target_pairs={{0,28},{4,24},{8,20},{12,16},{16,12},{20,8},{24,4},{28,0},{1,29},{... | collective-permute-start | bytes 786440 | tf_op jit(solution)/shard_map/ppermute | solution.py:238
  166.2 31.1 %collective-permute-start.21 = (f32[256,256]{1,0:T(8,128)S(1)}, f32[256,256]{1,0:T(8,128)S(1)}, u32[]{:S(2)}, u32[]{:S(2)}) collective-permute-start(f32[256,256]{1,0:T(8,128)S(1)} %touch.23), channel_id=1, source_target_pairs={{0,16},{4,20},{8,24},{12,28},{16,0},{20,4},{24,8},{28,12},{1,17},{... | collective-permute-start | bytes 786440 | tf_op jit(solution)/shard_map/ppermute | solution.py:238
  172.0 37.4 %collective-permute-start.32 = (f32[256,256]{1,0:T(8,128)S(1)}, f32[256,256]{1,0:T(8,128)S(1)}, u32[]{:S(2)}, u32[]{:S(2)}) collective-permute-start(f32[256,256]{1,0:T(8,128)S(1)} %get-tuple-element.83), channel_id=1, source_target_pairs={{0,12},{4,8},{8,4},{12,0},{16,28},{20,24},{24,20},{28,16},{1,13},{... | collective-permute-start | bytes 786440 | tf_op jit(solution)/shard_map/ppermute | solution.py:238
  172.1 42.2 %collective-permute-start.31 = (f32[256,256]{1,0:T(8,128)S(1)}, f32[256,256]{1,0:T(8,128)S(1)}, u32[]{:S(2)}, u32[]{:S(2)}) collective-permute-start(f32[256,256]{1,0:T(8,128)S(1)} %touch.29), channel_id=1, source_target_pairs={{0,20},{4,16},{8,28},{12,24},{16,4},{20,0},{24,12},{28,8},{1,21},{... | collective-permute-start | bytes 786440 | tf_op jit(solution)/shard_map/ppermute | solution.py:238
  182.7 34.8 %collective-permute-start.28 = (f32[256,256]{1,0:T(8,128)S(1)}, f32[256,256]{1,0:T(8,128)S(1)}, u32[]{:S(2)}, u32[]{:S(2)}) collective-permute-start(f32[256,256]{1,0:T(8,128)S(1)} %touch.27), channel_id=1, source_target_pairs={{0,24},{4,28},{8,16},{12,20},{16,8},{20,12},{24,0},{28,4},{1,25},{... | collective-permute-start | bytes 786440 | tf_op jit(solution)/shard_map/ppermute | solution.py:238
  197.3 23.7 %collective-permute-start.24 = (f32[256,256]{1,0:T(8,128)S(1)}, f32[256,256]{1,0:T(8,128)S(1)}, u32[]{:S(2)}, u32[]{:S(2)}) collective-permute-start(f32[256,256]{1,0:T(8,128)S(1)} %touch.24), channel_id=1, source_target_pairs={{0,28},{4,24},{8,20},{12,16},{16,12},{20,8},{24,4},{28,0},{1,29},{... | collective-permute-start | bytes 786440 | tf_op jit(solution)/shard_map/ppermute | solution.py:238
  199.2 4.7 %copy-start.5 = (f32[1,256,256]{2,1,0:T(8,128)S(1)}, f32[1,256,256]{2,1,0:T(8,128)}, u32[]{:S(2)}) copy-start(f32[1,256,256]{2,1,0:T(8,128)} %get-tuple-element.85.inner_ref) | copy-start | bytes 786436

commit v5 on v4

--- a/solution.py
+++ b/solution.py
@@ -12,7 +12,7 @@
 F32 = jnp.float32
 BF16 = jnp.bfloat16
 FLIGHT = 3
-NEEDS = {3: ["leaf"], 5: [(0, 0)], 6: [(0, 1)], 7: [(0, 2), (1, 0)], 8: [(1, 1)], 9: [(1, 2)], 12: [(2, 0)], 13: [(2, 1)], 14: [(2, 2)], 15: [(3, 0), (3, 1)]}
+NEEDS = {3: ["leaf"], 5: [(0, 0)], 6: [(0, 1)], 7: [(0, 2), (1, 0)], 8: [(1, 1)], 9: [(1, 2)], 12: [(2, 0)], 13: [(2, 1)], 14: [(2, 2)], 15: [(3, 0), (3, 1), "last"]}
 RIDE = 0
 PACE = (0, 2, 4)
 CHUNKS = 2
@@ -193,7 +193,8 @@
 
 def last_kernel(parts, begin, place_ref, window_ref, inner_ref, rest_ref, *refs):
     count = len(parts)
-    pieces, (out_ref, buffer, both, sems) = refs[:count], refs[-4:]
+    pieces, (out_ref, token_ref, buffer, both, sems) = refs[:count], refs[-5:]
+    token_ref[...] = jnp.zeros(token_ref.shape, F32)
     width = inner_ref.shape[1] // 2
     loads, stores = [], []
     for i, part in enumerate(parts):
@@ -385,13 +386,13 @@
         return pl.pallas_call(
             functools.partial(last_kernel, [part(chunk, k) for k in ks], begin),
             in_specs=in_specs,
-            out_specs=hbm(),
+            out_specs=(hbm(), vmem()),
             scratch_shapes=[
                 pltpu.VMEM((count, height, n), F32),
                 pltpu.VMEM((3 * width, n), F32),
                 pltpu.SemaphoreType.DMA((2, count)),
             ],
-            out_shape=jax.ShapeDtypeStruct(window.shape, F32),
+            out_shape=(jax.ShapeDtypeStruct(window.shape, F32), jax.ShapeDtypeStruct((8, 128), F32)),
             input_output_aliases=aliases,
             compiler_params=params(),
             cost_estimate=cost(
@@ -473,7 +474,16 @@
     dmats = join(shares, [pace[2]])
     pack = join(pack, [pace[0]])
 
-    pairs = None
+    def finish(chunk, ks, out):
+        made = {}
+        for k in ks:
+            made.setdefault(id(inners[chunk, k][0]), []).append(k)
+        for some in made.values():
+            inner, begin = inners[chunk, some[0]]
+            out, nears["last"] = last(chunk, some, inner, begin, [returned[chunk][k] for k in some], out)
+        return out
+
+    pairs = out = None
     returned = []
     for chunk in range(chunks):
         if chunk == 0:
@@ -482,23 +492,14 @@
         returned.append([made[0]] + [None] * (rows - 1))
         near_trades(chunks + chunk, returned[chunk], made)
         for k in far:
+            if chunk and k == far[-1]:
+                out = finish(chunk - 1, [0] + near, out)
+                out = finish(chunk - 1, far, out)
             returned[chunk][k] = far_swap(made[k], k)
-
-    out = None
-    for chunk in range(chunks):
-        groups = [[0] + near, far]
-        if chunk == chunks - 1:
-            groups = [[0] + near, far[:cut]] + [[k] for k in far[cut:]]
-        for ks in groups:
-            ks = [k for k in ks if k < rows]
-            if not ks:
-                continue
-            held = {}
-            for k in ks:
-                held.setdefault(id(inners[chunk, k][0]), []).append(k)
-            for some in held.values():
-                inner, begin = inners[chunk, some[0]]
-                out = last(chunk, some, inner, begin, [returned[chunk][k] for k in some], out)
+    out = finish(chunks - 1, [0] + near, out)
+    out = finish(chunks - 1, far[:cut], out)
+    for k in far[cut:]:
+        out = finish(chunks - 1, [k], out)
     return out
 
 

time: 226 us -> 224 us (level); the launches traced: 223 us -> 224 us
  waiting for transfers between devices: 82.5 us -> 75.7 us
  starting transfers between devices: 58.2 us -> 62 us
  Pallas kernels: 62.9 us -> 66.4 us
    ppermute x33, waiting for transfers between devices: 82.5 us -> 75.7 us  [swap(): lax.ppermute(value, axis, [(i, i ^ k) for i in range(lax.axis_size(axis))])]
    ppermute x33, starting transfers between devices: 58.2 us -> 62 us  [swap(): lax.ppermute(value, axis, [(i, i ^ k) for i in range(lax.axis_size(axis))])]
    pallas_call x7, Pallas kernels: 22 us -> 25.5 us  [last(): pl.pallas_call(functools.partial(last_kernel, [part(chunk, k) for k in ks...]
  transfers between devices with their start and end apart: 33 -> 33, of which waited for: 15 -> 16; matrix products, arithmetic and copies ran while one was open for 1% -> 1% of each run, Pallas kernels for 27% -> 28%
where the time goes in v5:
time: 224 us
  waiting for transfers between devices  75.7 us (34%)
  Pallas kernels  66.4 us (30%)
  starting transfers between devices  62 us (28%)
  local copies, waits for them, and re-layouts  10.8 us (5%)
  blocking collectives  7.4 us (3%)
    ppermute x33, waiting for transfers between devices, swap(): lax.ppermute(value, axis, [(i, i ^ k) for i in range(lax.axis_size(axis))])  75.7 us
    ppermute x33, starting transfers between devices, swap(): lax.ppermute(value, axis, [(i, i ^ k) for i in range(lax.axis_size(axis))])  62 us
    pallas_call x7, Pallas kernels, last(): pl.pallas_call(functools.partial(last_kernel, [part(chunk, k) for k in ks...  25.5 us
    pallas_call x5, Pallas kernels, leaf(): pl.pallas_call(functools.partial(leaf_kernel, [part(chunk, k) for k in ks...  20.4 us
    pallas_call x2, Pallas kernels, tree(): pl.pallas_call(functools.partial(tree_kernel, rows, order), out_shape=(ja...  9.37 us
    unnamed x32, local copies, waits for them, and re-layouts  8.99 us
    pallas_call x1, Pallas kernels, nodes(): pl.pallas_call(nodes_kernel, grid_spec=pltpu.PrefetchScalarGridSpec(num_s...  8.04 us
    all_gather x1, blocking collectives, local(): vecs = lax.all_gather(leaf_vecs, 'col', axis=1, tiled=True)  7.4 us
  transfers between devices with their start and end apart: 33, of which 16 were waited for; matrix products, arithmetic and copies ran while one was open for 1% of the time, Pallas kernels for 28%

profile of v5, /device:TPU:8, one launch (start us, length us, event | category | flops | bytes accessed | tf_op | source)
XLA Modules:
  0.0 223.7 jit_solution(17580779998110745940)
XLA Ops:
  0.1 0.9 copy-done.6
  1.0 0.9 copy-done.7
  2.4 2.7 %collective-permute-start = (f32[1,256,128]{2,1,0:T(8,128)S(1)}, f32[1,256,128]{2,1,0:T(8,128)S(1)}, u32[]{:S(2)}, u32[]{:S(2)}) collective-permute-start(f32[1,256,128]{2,1,0:T(8,128)S(1)} %pack.1), channel_id=1, source_target_pairs={{0,16},{4,20},{8,24},{12,28},{16,0},{20,4},{24,8},{28,12},{1,17},{... | collective-permute-start | bytes 393224 | tf_op jit(solution)/shard_map/ppermute | solution.py:239
  5.1 7.4 %all_gather.3.vecs_ref = f32[2,512,128]{2,1,0:T(8,128)S(1)} all-gather(f32[2,128,128]{2,1,0:T(8,128)} %param.6), channel_id=1, replica_groups=mesh['row'=8,'col'=4] {'col'}, dimensions={1}, use_global_device_ids=true | all-gather | bytes 655360 | tf_op jit(solution)/shard_map/all_gather | solution.py:280
  13.1 0.9 copy-done.12
  14.0 1.9 prep.1
  15.9 0.8 copy-done.1
  18.0 3.8 %leaf.7 = (f32[1,256,256]{2,1,0:T(8,128)}, f32[288,256]{1,0:T(8,128)}) custom-call(s32[2]{0:T(128)} %copy-done.8, f32[512,4096]{1,0:T(8,128)} %window_ref.23, bf16[2,256,512]{2,1,0:T(8,128)(2,1)} %copy-done.1, bf16[2,256,256]{2,1,0:T(8,128)(2,1)} %copy-done.3, f32[128,128]{1,0:T(8,128)} %copy-done.11), custom_call_target="tpu_custom_call" | custom-call | flops 301989888 | bytes 1048576 | tf_op jit(solution)/shard_map/leaf/pallas_call | solution.py:331
  21.7 1.1 collective-permute-start.5
  22.8 0.8 fusion.14
  23.7 1.5 collective-permute-start.4
  25.2 3.4 %copy-done = f32[512,4096]{1,0:T(8,128)S(1)} copy-done((f32[512,4096]{1,0:T(8,128)S(1)}, f32[512,4096]{1,0:T(8,128)}, u32[]{:S(2)}) %copy-start) | copy-done | bytes 8388632
  29.3 3.5 %leaf.5 = (f32[3,256,256]{2,1,0:T(8,128)S(1)}, f32[256,256]{1,0:T(8,128)S(1)}, f32[256,256]{1,0:T(8,128)S(1)}, f32[256,256]{1,0:T(8,128)S(1)}) custom-call(s32[2]{0:T(128)S(1)} %copy-done.9, f32[512,4096]{1,0:T(8,128)S(1)} %copy-done, bf16[2,256,512]{2,1,0:T(8,128)(2,1)S(1)} %copy-done.2, bf16[2,256,256]{2,1,0:T(8,128)(2,1)S(1)} %copy-done.4, ...), custom_call_target="tpu_custom_call" | custom-call | flops 905969664 | bytes 3145728 | tf_op jit(solution)/shard_map/leaf/pallas_call | solution.py:331
  32.8 2.0 collective-permute-start.2
  34.8 0.8 slice.196
  35.5 1.5 collective-permute-start.3
  37.1 11.0 %collective-permute-done.5 = f32[288,256]{1,0:T(8,128)S(1)} collective-permute-done((f32[288,256]{1,0:T(8,128)}, f32[288,256]{1,0:T(8,128)S(1)}, u32[]{:S(2)}, u32[]{:S(2)}) %collective-permute-start.5) | collective-permute-done | bytes 294944 | tf_op jit(solution)/shard_map/ppermute | solution.py:239
  48.1 5.5 %collective-permute-done.2.refs_1_ = f32[256,256]{1,0:T(8,128)S(1)} collective-permute-done((f32[256,256]{1,0:T(8,128)S(1)}, f32[256,256]{1,0:T(8,128)S(1)}, u32[]{:S(2)}, u32[]{:S(2)}) %collective-permute-start.2) | collective-permute-done | bytes 262176 | tf_op jit(solution)/shard_map/ppermute | solution.py:239
  53.6 4.4 %leaf.6 = (f32[4,256,256]{2,1,0:T(8,128)S(1)}, f32[256,256]{1,0:T(8,128)S(1)}, f32[256,256]{1,0:T(8,128)S(1)}, f32[256,256]{1,0:T(8,128)S(1)}, f32[256,256]{1,0:T(8,128)S(1)}) custom-call(s32[2]{0:T(128)S(1)} %copy-done.10, f32[512,4096]{1,0:T(8,128)S(1)} %copy-done, bf16[2,256,512]{2,1,0:T(8,128)(2,1)S(1)} %copy-done.2, bf16[2,256,256]{2,1,0:T(8,128)(2,1)S(1)} %copy-done.4, ...), custom_call_target="tpu_custom_call" | custom-call | flops 1207959552 | bytes 4194304 | tf_op jit(solution)/shard_map/leaf/pallas_call | solution.py:331
  58.0 4.4 %collective-permute-start.10 = (f32[256,256]{1,0:T(8,128)S(1)}, f32[256,256]{1,0:T(8,128)S(1)}, u32[]{:S(2)}, u32[]{:S(2)}) collective-permute-start(f32[256,256]{1,0:T(8,128)S(1)} %touch.16), channel_id=1, source_target_pairs={{0,16},{4,20},{8,24},{12,28},{16,0},{20,4},{24,8},{28,12},{1,17},{... | collective-permute-start | bytes 786440 | tf_op jit(solution)/shard_map/ppermute | solution.py:239
  62.4 4.4 %leaf.8 = (f32[4,256,256]{2,1,0:T(8,128)S(1)}, f32[256,256]{1,0:T(8,128)S(1)}, f32[256,256]{1,0:T(8,128)S(1)}, f32[256,256]{1,0:T(8,128)S(1)}, f32[256,256]{1,0:T(8,128)S(1)}) custom-call(s32[2]{0:T(128)S(1)} %copy-done.10, f32[512,4096]{1,0:T(8,128)S(1)} %copy-done, bf16[2,256,512]{2,1,0:T(8,128)(2,1)S(1)} %copy-done.2, bf16[2,256,256]{2,1,0:T(8,128)(2,1)S(1)} %copy-done.4, ...), custom_call_target="tpu_custom_call" | custom-call | flops 1207959552 | bytes 4194304 | tf_op jit(solution)/shard_map/leaf/pallas_call | solution.py:331
  67.4 5.5 %collective-permute-start.7 = (f32[320,256]{1,0:T(8,128)S(1)}, f32[320,256]{1,0:T(8,128)S(1)}, u32[]{:S(2)}, u32[]{:S(2)}) collective-permute-start(f32[320,256]{1,0:T(8,128)S(1)} %get-tuple-element.123), channel_id=1, source_target_pairs={{0,4},{4,0},{8,12},{12,8},{16,20},{20,16},{24,28},{28,24},{1,5},{5... | collective-permute-start | bytes 983048 | tf_op jit(solution)/shard_map/ppermute | solution.py:239
  73.1 1.5 collective-permute-start.8
  74.6 9.5 %collective-permute-done.9 = f32[320,256]{1,0:T(8,128)S(1)} collective-permute-done((f32[320,256]{1,0:T(8,128)S(1)}, f32[320,256]{1,0:T(8,128)S(1)}, u32[]{:S(2)}, u32[]{:S(2)}) %collective-permute-start.9) | collective-permute-done | bytes 327712 | tf_op jit(solution)/shard_map/ppermute | solution.py:239
  84.1 4.4 %leaf.9 = (f32[4,256,256]{2,1,0:T(8,128)S(1)}, f32[256,256]{1,0:T(8,128)S(1)}, f32[256,256]{1,0:T(8,128)S(1)}, f32[256,256]{1,0:T(8,128)S(1)}, f32[256,256]{1,0:T(8,128)S(1)}) custom-call(s32[2]{0:T(128)S(1)} %copy-done.10, f32[512,4096]{1,0:T(8,128)S(1)} %bitcast.56, bf16[2,256,512]{2,1,0:T(8,128)(2,1)S(1)} %copy-done.2, ...), custom_call_target="tpu_custom_call" | custom-call | flops 1207959552 | bytes 4194304 | tf_op jit(solution)/shard_map/leaf/pallas_call | solution.py:331
  88.5 2.2 collective-permute-start.15
  90.8 0.8 collective-permute-done.8
  91.6 2.6 %collective-permute-start.17 = (f32[256,256]{1,0:T(8,128)S(1)}, f32[256,256]{1,0:T(8,128)S(1)}, u32[]{:S(2)}, u32[]{:S(2)}) collective-permute-start(f32[256,256]{1,0:T(8,128)S(1)} %get-tuple-element.72), channel_id=1, source_target_pairs={{0,8},{4,12},{8,0},{12,4},{16,24},{20,28},{24,16},{28,20},{1,9},{5... | collective-permute-start | bytes 786440 | tf_op jit(solution)/shard_map/ppermute | solution.py:239
  94.8 1.6 collective-permute-done.15.refs_4_
  96.4 5.8 %collective-permute-start.18 = (f32[256,256]{1,0:T(8,128)S(1)}, f32[256,256]{1,0:T(8,128)S(1)}, u32[]{:S(2)}, u32[]{:S(2)}) collective-permute-start(f32[256,256]{1,0:T(8,128)S(1)} %get-tuple-element.73), channel_id=1, source_target_pairs={{0,12},{4,8},{8,4},{12,0},{16,28},{20,24},{24,20},{28,16},{1,13},{... | collective-permute-start | bytes 786440 | tf_op jit(solution)/shard_map/ppermute | solution.py:239
  102.3 1.6 collective-permute-done.17.refs_5_
  103.9 3.4 %collective-permute-start.14 = (f32[256,256]{1,0:T(8,128)S(1)}, f32[256,256]{1,0:T(8,128)S(1)}, u32[]{:S(2)}, u32[]{:S(2)}) collective-permute-start(f32[256,256]{1,0:T(8,128)S(1)} %touch.20), channel_id=1, source_target_pairs={{0,24},{4,28},{8,16},{12,20},{16,8},{20,12},{24,0},{28,4},{1,25},{... | collective-permute-start | bytes 786440 | tf_op jit(solution)/shard_map/ppermute | solution.py:239
  107.3 3.7 %collective-permute-start.16 = (f32[256,256]{1,0:T(8,128)S(1)}, f32[256,256]{1,0:T(8,128)S(1)}, u32[]{:S(2)}, u32[]{:S(2)}) collective-permute-start(f32[256,256]{1,0:T(8,128)S(1)} %touch.21), channel_id=1, source_target_pairs={{0,28},{4,24},{8,20},{12,16},{16,12},{20,8},{24,4},{28,0},{1,29},{... | collective-permute-start | bytes 786440 | tf_op jit(solution)/shard_map/ppermute | solution.py:239
  111.3 8.0 %nodes.1.pair_ref = bf16[2,2,8,256,256]{4,3,2,1,0:T(8,128)(2,1)S(1)} custom-call(s32[2]{0:T(128)S(1)} %copy-done.10, f32[8,128]{1,0:T(8,128)S(1)} %slice.241.after_ref.refs_1_, f32[2,8,256,128]{3,2,1,0:T(8,128)S(1)} %pad_maximum_fusion.pack_ref), custom_call_target="tpu_custom_call" | custom-call | flops 1207959552 | bytes 8388608 | tf_op jit(solution)/shard_map/nodes/pallas_call | solution.py:347
  119.3 4.7 %tree.3 = (f32[256,256]{1,0:T(8,128)S(1)}, f32[256,256]{1,0:T(8,128)S(1)}, f32[256,256]{1,0:T(8,128)S(1)}, f32[256,256]{1,0:T(8,128)S(1)}, f32[256,256]{1,0:T(8,...) custom-call(s32[2]{0:T(128)S(1)} %copy-done.10, ...), custom_call_target="tpu_custom_call" | custom-call | flops 3221225472 | bytes 8388608 | tf_op jit(solution)/shard_map/tree/pallas_call | solution.py:365
  124.1 3.1 %collective-permute-start.25 = (f32[256,256]{1,0:T(8,128)S(1)}, f32[256,256]{1,0:T(8,128)S(1)}, u32[]{:S(2)}, u32[]{:S(2)}) collective-permute-start(f32[256,256]{1,0:T(8,128)S(1)} %touch.25), channel_id=1, source_target_pairs={{0,16},{4,20},{8,24},{12,28},{16,0},{20,4},{24,8},{28,12},{1,17},{... | collective-permute-start | bytes 786440 | tf_op jit(solution)/shard_map/ppermute | solution.py:239
  127.2 10.4 %collective-permute-done.16.refs_3_ = f32[256,256]{1,0:T(8,128)S(1)} collective-permute-done((f32[256,256]{1,0:T(8,128)S(1)}, f32[256,256]{1,0:T(8,128)S(1)}, u32[]{:S(2)}, u32[]{:S(2)}) %collective-permute-start.16) | collective-permute-done | bytes 262176 | tf_op jit(solution)/shard_map/ppermute | solution.py:239
  137.8 1.3 collective-permute-start.20
  139.1 2.0 collective-permute-start.27
  141.9 4.5 %collective-permute-done.25.refs_0_ = f32[256,256]{1,0:T(8,128)S(1)} collective-permute-done((f32[256,256]{1,0:T(8,128)S(1)}, f32[256,256]{1,0:T(8,128)S(1)}, u32[]{:S(2)}, u32[]{:S(2)}) %collective-permute-start.25) | collective-permute-done | bytes 262176 | tf_op jit(solution)/shard_map/ppermute | solution.py:239
  146.3 1.5 collective-permute-start.24
  147.8 4.7 %tree.2 = (f32[256,256]{1,0:T(8,128)S(1)}, f32[256,256]{1,0:T(8,128)S(1)}, f32[256,256]{1,0:T(8,128)S(1)}, f32[256,256]{1,0:T(8,128)S(1)}, f32[256,256]{1,0:T(8,...) custom-call(s32[2]{0:T(128)S(1)} %copy-done.10, ...), custom_call_target="tpu_custom_call" | custom-call | flops 3221225472 | bytes 8388608 | tf_op jit(solution)/shard_map/tree/pallas_call | solution.py:365
  152.5 1.9 collective-permute-done.19.refs_0_
  154.4 2.9 %collective-permute-start.23 = (f32[256,256]{1,0:T(8,128)S(1)}, f32[256,256]{1,0:T(8,128)S(1)}, u32[]{:S(2)}, u32[]{:S(2)}) collective-permute-start(f32[256,256]{1,0:T(8,128)S(1)} %get-tuple-element.81), channel_id=1, source_target_pairs={{0,8},{4,12},{8,0},{12,4},{16,24},{20,28},{24,16},{28,20},{1,9},{5... | collective-permute-start | bytes 786440 | tf_op jit(solution)/shard_map/ppermute | solution.py:239
  157.3 2.5 %collective-permute-start.26 = (f32[256,256]{1,0:T(8,128)S(1)}, f32[256,256]{1,0:T(8,128)S(1)}, u32[]{:S(2)}, u32[]{:S(2)}) collective-permute-start(f32[256,256]{1,0:T(8,128)S(1)} %touch.26), channel_id=1, source_target_pairs={{0,28},{4,24},{8,20},{12,16},{16,12},{20,8},{24,4},{28,0},{1,29},{... | collective-permute-start | bytes 786440 | tf_op jit(solution)/shard_map/ppermute | solution.py:239
  159.9 5.7 %collective-permute-done.24.refs_1_ = f32[256,256]{1,0:T(8,128)S(1)} collective-permute-done((f32[256,256]{1,0:T(8,128)S(1)}, f32[256,256]{1,0:T(8,128)S(1)}, u32[]{:S(2)}, u32[]{:S(2)}) %collective-permute-start.24) | collective-permute-done | bytes 262176 | tf_op jit(solution)/shard_map/ppermute | solution.py:239
  165.6 1.3 collective-permute-start.21
  167.0 0.8 collective-permute-done.28.refs_3_
  167.7 3.9 %collective-permute-start.32 = (f32[256,256]{1,0:T(8,128)S(1)}, f32[256,256]{1,0:T(8,128)S(1)}, u32[]{:S(2)}, u32[]{:S(2)}) collective-permute-start(f32[256,256]{1,0:T(8,128)S(1)} %get-tuple-element.97), channel_id=1, source_target_pairs={{0,12},{4,8},{8,4},{12,0},{16,28},{20,24},{24,20},{28,16},{1,13},{... | collective-permute-start | bytes 786440 | tf_op jit(solution)/shard_map/ppermute | solution.py:239
  171.6 1.1 collective-permute-start.31
  172.7 5.0 %collective-permute-done.23.refs_2_ = f32[256,256]{1,0:T(8,128)S(1)} collective-permute-done((f32[256,256]{1,0:T(8,128)S(1)}, f32[256,256]{1,0:T(8,128)S(1)}, u32[]{:S(2)}, u32[]{:S(2)}) %collective-permute-start.23) | collective-permute-done | bytes 262176 | tf_op jit(solution)/shard_map/ppermute | solution.py:239
  177.7 5.3 %last.7 = (f32[512,4096]{1,0:T(8,128)}, f32[8,128]{1,0:T(8,128)}) custom-call(s32[2]{0:T(128)S(1)} %copy-done.10, f32[512,4096]{1,0:T(8,128)S(1)} %bitcast.56, f32[4,256,256]{2,1,0:T(8,128)S(1)} %get-tuple-element.69.inner_ref, bf16[2,384,384]{2,1,0:T(8,128)(2,1)S(1)} %get-tuple-element.58.rest_ref, f32[256,256]{1,0:T(8,128)S(1)} %get-tuple-element.87.refs_0_, ...), custom_call_target="tpu_custom_call" | custom-call | flops 905969664 | bytes 6291456 | tf_op jit(solution)/shard_map/last/pallas_call | solution.py:386
  183.0 2.5 %last.8 = (f32[512,4096]{1,0:T(8,128)}, f32[8,128]{1,0:T(8,128)}) custom-call(s32[2]{0:T(128)S(1)} %copy-done.10, f32[512,4096]{1,0:T(8,128)S(1)} %bitcast.56, f32[1,256,256]{2,1,0:T(8,128)S(1)} %copy-done.5, bf16[2,384,384]{2,1,0:T(8,128)(2,1)S(1)} %get-tuple-element.58.rest_ref, ...), custom_call_target="tpu_custom_call", output_to_operand_aliasing={{0}: (5, {})} | custom-call | flops 226492416 | bytes 1572864 | tf_op jit(solution)/shard_map/last/pallas_call | solution.py:386
  185.6 1.2 collective-permute-start.30
  186.7 3.6 %last.9 = (f32[512,4096]{1,0:T(8,128)}, f32[8,128]{1,0:T(8,128)S(1)}) custom-call(s32[2]{0:T(128)S(1)} %copy-done.10, f32[512,4096]{1,0:T(8,128)S(1)} %bitcast.56, f32[3,256,256]{2,1,0:T(8,128)S(1)} %get-tuple-element.82.inner_ref, bf16[2,384,384]{2,1,0:T(8,128)(2,1)S(1)} %get-tuple-element.58.rest_ref, ...), custom_call_target="tpu_custom_call", output_to_operand_aliasing={{0}: (7, {})} | custom-call | flops 679477248 | bytes 4718592 | tf_op jit(solution)/shard_map/last/pallas_call | solution.py:386
  190.4 7.3 %collective-permute-done.21.refs_0_ = f32[256,256]{1,0:T(8,128)S(1)} collective-permute-done((f32[256,256]{1,0:T(8,128)S(1)}, f32[256,256]{1,0:T(8,128)S(1)}, u32[]{:S(2)}, u32[]{:S(2)}) %collective-permute-start.21) | collective-permute-done | bytes 262176 | tf_op jit(solution)/shard_map/ppermute | solution.py:239
  197.7 1.5 collective-permute-start.29
  199.1 5.5 %last.10 = (f32[512,4096]{1,0:T(8,128)}, f32[8,128]{1,0:T(8,128)}) custom-call(s32[2]{0:T(128)S(1)} %copy-done.10, f32[512,4096]{1,0:T(8,128)S(1)} %bitcast.56, f32[4,256,256]{2,1,0:T(8,128)S(1)} %get-tuple-element.95.inner_ref, bf16[2,384,384]{2,1,0:T(8,128)(2,1)S(1)} %get-tuple-element.58.rest_ref, ...), custom_call_target="tpu_custom_call", output_to_operand_aliasing={{0}: (8, {})} | custom-call | flops 905969664 | bytes 6291456 | tf_op jit(solution)/shard_map/last/pallas_call | solution.py:386
  204.7 4.2 %collective-permute-done.31.refs_1_ = f32[256,256]{1,0:T(8,128)S(1)} collective-permute-done((f32[256,256]{1,0:T(8,128)S(1)}, f32[256,256]{1,0:T(8,128)S(1)}, u32[]{:S(2)}, u32[]{:S(2)}) %collective-permute-start.31) | collective-permute-done | bytes 262176 | tf_op jit(solution)/shard_map/ppermute | solution.py:239
  208.9 3.7 %last.11 = (f32[512,4096]{1,0:T(8,128)}, f32[8,128]{1,0:T(8,128)}) custom-call(s32[2]{0:T(128)S(1)} %copy-done.10, f32[512,4096]{1,0:T(8,128)S(1)} %bitcast.56, f32[4,256,256]{2,1,0:T(8,128)S(1)} %get-tuple-element.57.inner_ref, bf16[2,384,384]{2,1,0:T(8,128)(2,1)S(1)} %get-tuple-element.58.rest_ref, ...), custom_call_target="tpu_custom_call", output_to_operand_aliasing={{0}: (6, {})} | custom-call | flops 452984832 | bytes 3145728 | tf_op jit(solution)/shard_map/last/pallas_call | solution.py:386
  212.5 3.6 %collective-permute-done.30.refs_0_ = f32[256,256]{1,0:T(8,128)S(1)} collective-permute-done((f32[256,256]{1,0:T(8,128)S(1)}, f32[256,256]{1,0:T(8,128)S(1)}, u32[]{:S(2)}, u32[]{:S(2)}) %collective-permute-start.30) | collective-permute-done | bytes 262176 | tf_op jit(solution)/shard_map/ppermute | solution.py:239
  216.1 2.5 %last.12 = (f32[512,4096]{1,0:T(8,128)}, f32[8,128]{1,0:T(8,128)}) custom-call(s32[2]{0:T(128)S(1)} %copy-done.10, f32[512,4096]{1,0:T(8,128)S(1)} %bitcast.56, f32[4,256,256]{2,1,0:T(8,128)S(1)} %get-tuple-element.57.inner_ref, bf16[2,384,384]{2,1,0:T(8,128)(2,1)S(1)} %get-tuple-element.58.rest_ref, ...), custom_call_target="tpu_custom_call", output_to_operand_aliasing={{0}: (5, {})} | custom-call | flops 226492416 | bytes 1572864 | tf_op jit(solution)/shard_map/last/pallas_call | solution.py:386
  218.6 2.4 %collective-permute-done.29.refs_0_ = f32[256,256]{1,0:T(8,128)S(1)} collective-permute-done((f32[256,256]{1,0:T(8,128)S(1)}, f32[256,256]{1,0:T(8,128)S(1)}, u32[]{:S(2)}, u32[]{:S(2)}) %collective-permute-start.29) | collective-permute-done | bytes 262176 | tf_op jit(solution)/shard_map/ppermute | solution.py:239
  221.0 2.5 %last.13 = (f32[512,4096]{1,0:T(8,128)}, f32[8,128]{1,0:T(8,128)}) custom-call(s32[2]{0:T(128)S(1)} %copy-done.10, f32[512,4096]{1,0:T(8,128)S(1)} %bitcast.56, f32[4,256,256]{2,1,0:T(8,128)S(1)} %get-tuple-element.57.inner_ref, bf16[2,384,384]{2,1,0:T(8,128)(2,1)S(1)} %get-tuple-element.58.rest_ref, ...), custom_call_target="tpu_custom_call", output_to_operand_aliasing={{0}: (5, {})} | custom-call | flops 226492416 | bytes 1572864 | tf_op jit(solution)/shard_map/last/pallas_call | solution.py:386
  (124 shorter events, 6.0 us)
Async XLA Ops:
  0.1 0.9 copy-start.6
  1.0 0.9 copy-start.7
  1.9 16.1 %copy-start.8 = (s32[2]{0:T(128)}, s32[2]{0:T(128)S(1)}, u32[]{:S(2)}) copy-start(s32[2]{0:T(128)S(1)} %pad_add_fusion.place_ref) | copy-start | bytes 28
  2.4 10.1 %collective-permute-start = (f32[1,256,128]{2,1,0:T(8,128)S(1)}, f32[1,256,128]{2,1,0:T(8,128)S(1)}, u32[]{:S(2)}, u32[]{:S(2)}) collective-permute-start(f32[1,256,128]{2,1,0:T(8,128)S(1)} %pack.1), channel_id=1, source_target_pairs={{0,16},{4,20},{8,24},{12,28},{16,0},{20,4},{24,8},{28,12},{1,17},{... | collective-permute-start | bytes 393224 | tf_op jit(solution)/shard_map/ppermute | solution.py:239
  12.5 11.0 %collective-permute-start.1 = (f32[2,256,128]{2,1,0:T(8,128)S(1)}, f32[2,256,128]{2,1,0:T(8,128)S(1)}, u32[]{:S(2)}, u32[]{:S(2)}) collective-permute-start(f32[2,256,128]{2,1,0:T(8,128)S(1)} %get-tuple-element.120), channel_id=1, source_target_pairs={{0,8},{4,12},{8,0},{12,4},{16,24},{20,28},{24,16},{28,20},{1,9},{5... | collective-permute-start | bytes 786440 | tf_op jit(solution)/shard_map/ppermute | solution.py:239
  13.1 0.9 copy-start.12
  15.9 0.8 copy-start.1
  16.7 0.7 copy-start.3
  17.3 0.6 copy-start.11
  18.0 7.2 %copy-start.2 = (bf16[2,256,512]{2,1,0:T(8,128)(2,1)S(1)}, bf16[2,256,512]{2,1,0:T(8,128)(2,1)}, u32[]{:S(2)}) copy-start(bf16[2,256,512]{2,1,0:T(8,128)(2,1)} %copy-done.1) | copy-start | bytes 1572868
  18.0 7.2 %copy-start.4 = (bf16[2,256,256]{2,1,0:T(8,128)(2,1)S(1)}, bf16[2,256,256]{2,1,0:T(8,128)(2,1)}, u32[]{:S(2)}) copy-start(bf16[2,256,256]{2,1,0:T(8,128)(2,1)} %copy-done.3) | copy-start | bytes 786436
  21.7 31.9 %copy-start.10 = (s32[2]{0:T(128)S(1)}, s32[2]{0:T(128)}, u32[]{:S(2)}) copy-start(s32[2]{0:T(128)} %copy-done.8) | copy-start | bytes 28
  21.7 26.3 %collective-permute-start.5 = (f32[288,256]{1,0:T(8,128)}, f32[288,256]{1,0:T(8,128)S(1)}, u32[]{:S(2)}, u32[]{:S(2)}) collective-permute-start(f32[288,256]{1,0:T(8,128)} %get-tuple-element.61), channel_id=1, source_target_pairs={{0,16},{4,20},{8,24},{12,28},{16,0},{20,4},{24,8},{28,12},{1,17},{... | collective-permute-start | bytes 884744 | tf_op jit(solution)/shard_map/ppermute | solution.py:239
  23.7 38.7 %collective-permute-start.4 = (f32[4,256,128]{2,1,0:T(8,128)S(1)}, f32[4,256,128]{2,1,0:T(8,128)S(1)}, u32[]{:S(2)}, u32[]{:S(2)}) collective-permute-start(f32[4,256,128]{2,1,0:T(8,128)S(1)} %bitcast.61), channel_id=1, source_target_pairs={{0,4},{4,0},{8,12},{12,8},{16,20},{20,16},{24,28},{28,24},{1,5},{5... | collective-permute-start | bytes 1572872 | tf_op jit(solution)/shard_map/ppermute | solution.py:239
  25.2 3.4 %copy-start = (f32[512,4096]{1,0:T(8,128)S(1)}, f32[512,4096]{1,0:T(8,128)}, u32[]{:S(2)}) copy-start(f32[512,4096]{1,0:T(8,128)} %window_ref.23) | copy-start | bytes 25165828
  28.6 0.7 copy-start.9
  32.8 20.8 %collective-permute-start.2 = (f32[256,256]{1,0:T(8,128)S(1)}, f32[256,256]{1,0:T(8,128)S(1)}, u32[]{:S(2)}, u32[]{:S(2)}) collective-permute-start(f32[256,256]{1,0:T(8,128)S(1)} %get-tuple-element.56), channel_id=1, source_target_pairs={{0,20},{4,16},{8,28},{12,24},{16,4},{20,0},{24,12},{28,8},{1,21},{... | collective-permute-start | bytes 786440 | tf_op jit(solution)/shard_map/ppermute | solution.py:239
  35.5 26.9 %collective-permute-start.3 = (f32[256,256]{1,0:T(8,128)S(1)}, f32[256,256]{1,0:T(8,128)S(1)}, u32[]{:S(2)}, u32[]{:S(2)}) collective-permute-start(f32[256,256]{1,0:T(8,128)S(1)} %get-tuple-element.59), channel_id=1, source_target_pairs={{0,24},{4,28},{8,16},{12,20},{16,8},{20,12},{24,0},{28,4},{1,25},{... | collective-permute-start | bytes 786440 | tf_op jit(solution)/shard_map/ppermute | solution.py:239
  58.0 15.0 %collective-permute-start.10 = (f32[256,256]{1,0:T(8,128)S(1)}, f32[256,256]{1,0:T(8,128)S(1)}, u32[]{:S(2)}, u32[]{:S(2)}) collective-permute-start(f32[256,256]{1,0:T(8,128)S(1)} %touch.16), channel_id=1, source_target_pairs={{0,16},{4,20},{8,24},{12,28},{16,0},{20,4},{24,8},{28,12},{1,17},{... | collective-permute-start | bytes 786440 | tf_op jit(solution)/shard_map/ppermute | solution.py:239
  62.4 21.7 %slice-start = ((s8[8388608]{0:T(1024)(128)(4,1)}), s8[4194304]{0:T(1024)(128)(4,1)S(1)}, s32[]{:S(2)}) async-start(s8[8388608]{0:T(1024)(128)(4,1)} %bitcast.55), calls=%async_computation | async-start | bytes 8388608
  66.8 17.3 %slice-start.1 = ((s8[8388608]{0:T(1024)(128)(4,1)}), s8[4194304]{0:T(1024)(128)(4,1)S(1)}, s32[]{:S(2)}) async-start(s8[8388608]{0:T(1024)(128)(4,1)} %bitcast.55), calls=%async_computation.1 | async-start | bytes 8388608
  66.9 17.2 %collective-permute-start.9 = (f32[320,256]{1,0:T(8,128)S(1)}, f32[320,256]{1,0:T(8,128)S(1)}, u32[]{:S(2)}, u32[]{:S(2)}) collective-permute-start(f32[320,256]{1,0:T(8,128)S(1)} %get-tuple-element.121), channel_id=1, source_target_pairs={{0,12},{4,8},{8,4},{12,0},{16,28},{20,24},{24,20},{28,16},{1,13},{... | collective-permute-start | bytes 983048 | tf_op jit(solution)/shard_map/ppermute | solution.py:239
  67.4 43.7 %collective-permute-start.6 = (f32[8,256,128]{2,1,0:T(8,128)S(1)}, f32[8,256,128]{2,1,0:T(8,128)S(1)}, u32[]{:S(2)}, u32[]{:S(2)}) collective-permute-start(f32[8,256,128]{2,1,0:T(8,128)S(1)} %touch.15), channel_id=1, source_target_pairs={{0,1},{1,0},{2,3},{3,2},{4,5},{5,4},{6,7},{7,6},{8,9},{9,8},{10,11... | collective-permute-start | bytes 3145736 | tf_op jit(solution)/shard_map/ppermute | solution.py:239
  67.4 23.3 %collective-permute-start.7 = (f32[320,256]{1,0:T(8,128)S(1)}, f32[320,256]{1,0:T(8,128)S(1)}, u32[]{:S(2)}, u32[]{:S(2)}) collective-permute-start(f32[320,256]{1,0:T(8,128)S(1)} %get-tuple-element.123), channel_id=1, source_target_pairs={{0,4},{4,0},{8,12},{12,8},{16,20},{20,16},{24,28},{28,24},{1,5},{5... | collective-permute-start | bytes 983048 | tf_op jit(solution)/shard_map/ppermute | solution.py:239
  73.0 21.5 %collective-permute-start.13 = (f32[256,256]{1,0:T(8,128)S(1)}, f32[256,256]{1,0:T(8,128)S(1)}, u32[]{:S(2)}, u32[]{:S(2)}) collective-permute-start(f32[256,256]{1,0:T(8,128)S(1)} %touch.19), channel_id=1, source_target_pairs={{0,28},{4,24},{8,20},{12,16},{16,12},{20,8},{24,4},{28,0},{1,29},{... | collective-permute-start | bytes 786440 | tf_op jit(solution)/shard_map/ppermute | solution.py:239
  73.1 18.4 %collective-permute-start.8 = (f32[320,256]{1,0:T(8,128)S(1)}, f32[320,256]{1,0:T(8,128)S(1)}, u32[]{:S(2)}, u32[]{:S(2)}) collective-permute-start(f32[320,256]{1,0:T(8,128)S(1)} %get-tuple-element.122), channel_id=1, source_target_pairs={{0,8},{4,12},{8,0},{12,4},{16,24},{20,28},{24,16},{28,20},{1,9},{5... | collective-permute-start | bytes 983048 | tf_op jit(solution)/shard_map/ppermute | solution.py:239
  88.5 7.8 %collective-permute-start.15 = (f32[256,256]{1,0:T(8,128)S(1)}, f32[256,256]{1,0:T(8,128)S(1)}, u32[]{:S(2)}, u32[]{:S(2)}) collective-permute-start(f32[256,256]{1,0:T(8,128)S(1)} %get-tuple-element.71), channel_id=1, source_target_pairs={{0,4},{4,0},{8,12},{12,8},{16,20},{20,16},{24,28},{28,24},{1,5},{5... | collective-permute-start | bytes 786440 | tf_op jit(solution)/shard_map/ppermute | solution.py:239
  91.6 12.3 %collective-permute-start.17 = (f32[256,256]{1,0:T(8,128)S(1)}, f32[256,256]{1,0:T(8,128)S(1)}, u32[]{:S(2)}, u32[]{:S(2)}) collective-permute-start(f32[256,256]{1,0:T(8,128)S(1)} %get-tuple-element.72), channel_id=1, source_target_pairs={{0,8},{4,12},{8,0},{12,4},{16,24},{20,28},{24,16},{28,20},{1,9},{5... | collective-permute-start | bytes 786440 | tf_op jit(solution)/shard_map/ppermute | solution.py:239
  94.3 13.0 %collective-permute-start.12 = (f32[256,256]{1,0:T(8,128)S(1)}, f32[256,256]{1,0:T(8,128)S(1)}, u32[]{:S(2)}, u32[]{:S(2)}) collective-permute-start(f32[256,256]{1,0:T(8,128)S(1)} %touch.18), channel_id=1, source_target_pairs={{0,20},{4,16},{8,28},{12,24},{16,4},{20,0},{24,12},{28,8},{1,21},{... | collective-permute-start | bytes 786440 | tf_op jit(solution)/shard_map/ppermute | solution.py:239
  94.5 16.5 %collective-permute-start.11 = (f32[8,64,128]{2,1,0:T(8,128)S(1)}, f32[8,64,128]{2,1,0:T(8,128)S(1)}, u32[]{:S(2)}, u32[]{:S(2)}) collective-permute-start(f32[8,64,128]{2,1,0:T(8,128)S(1)} %touch.17), channel_id=1, source_target_pairs={{0,1},{1,0},{2,3},{3,2},{4,5},{5,4},{6,7},{7,6},{8,9},{9,8},{10,11... | collective-permute-start | bytes 786440 | tf_op jit(solution)/shard_map/ppermute | solution.py:239
  96.4 30.8 %collective-permute-start.18 = (f32[256,256]{1,0:T(8,128)S(1)}, f32[256,256]{1,0:T(8,128)S(1)}, u32[]{:S(2)}, u32[]{:S(2)}) collective-permute-start(f32[256,256]{1,0:T(8,128)S(1)} %get-tuple-element.73), channel_id=1, source_target_pairs={{0,12},{4,8},{8,4},{12,0},{16,28},{20,24},{24,20},{28,16},{1,13},{... | collective-permute-start | bytes 786440 | tf_op jit(solution)/shard_map/ppermute | solution.py:239
  103.9 23.3 %collective-permute-start.14 = (f32[256,256]{1,0:T(8,128)S(1)}, f32[256,256]{1,0:T(8,128)S(1)}, u32[]{:S(2)}, u32[]{:S(2)}) collective-permute-start(f32[256,256]{1,0:T(8,128)S(1)} %touch.20), channel_id=1, source_target_pairs={{0,24},{4,28},{8,16},{12,20},{16,8},{20,12},{24,0},{28,4},{1,25},{... | collective-permute-start | bytes 786440 | tf_op jit(solution)/shard_map/ppermute | solution.py:239
  107.3 30.3 %collective-permute-start.16 = (f32[256,256]{1,0:T(8,128)S(1)}, f32[256,256]{1,0:T(8,128)S(1)}, u32[]{:S(2)}, u32[]{:S(2)}) collective-permute-start(f32[256,256]{1,0:T(8,128)S(1)} %touch.21), channel_id=1, source_target_pairs={{0,28},{4,24},{8,20},{12,16},{16,12},{20,8},{24,4},{28,0},{1,29},{... | collective-permute-start | bytes 786440 | tf_op jit(solution)/shard_map/ppermute | solution.py:239
  124.1 22.3 %collective-permute-start.25 = (f32[256,256]{1,0:T(8,128)S(1)}, f32[256,256]{1,0:T(8,128)S(1)}, u32[]{:S(2)}, u32[]{:S(2)}) collective-permute-start(f32[256,256]{1,0:T(8,128)S(1)} %touch.25), channel_id=1, source_target_pairs={{0,16},{4,20},{8,24},{12,28},{16,0},{20,4},{24,8},{28,12},{1,17},{... | collective-permute-start | bytes 786440 | tf_op jit(solution)/shard_map/ppermute | solution.py:239
  137.7 16.7 %collective-permute-start.19 = (f32[256,256]{1,0:T(8,128)S(1)}, f32[256,256]{1,0:T(8,128)S(1)}, u32[]{:S(2)}, u32[]{:S(2)}) collective-permute-start(f32[256,256]{1,0:T(8,128)S(1)} %touch.22), channel_id=1, source_target_pairs={{0,20},{4,16},{8,28},{12,24},{16,4},{20,0},{24,12},{28,8},{1,21},{... | collective-permute-start | bytes 786440 | tf_op jit(solution)/shard_map/ppermute | solution.py:239
  137.8 16.6 %collective-permute-start.20 = (f32[256,256]{1,0:T(8,128)S(1)}, f32[256,256]{1,0:T(8,128)S(1)}, u32[]{:S(2)}, u32[]{:S(2)}) collective-permute-start(f32[256,256]{1,0:T(8,128)S(1)} %get-tuple-element.79), channel_id=1, source_target_pairs={{0,4},{4,0},{8,12},{12,8},{16,20},{20,16},{24,28},{28,24},{1,5},{5... | collective-permute-start | bytes 786440 | tf_op jit(solution)/shard_map/ppermute | solution.py:239
  139.1 18.2 %collective-permute-start.27 = (f32[256,256]{1,0:T(8,128)S(1)}, f32[256,256]{1,0:T(8,128)S(1)}, u32[]{:S(2)}, u32[]{:S(2)}) collective-permute-start(f32[256,256]{1,0:T(8,128)S(1)} %get-tuple-element.88), channel_id=1, source_target_pairs={{0,8},{4,12},{8,0},{12,4},{16,24},{20,28},{24,16},{28,20},{1,9},{5... | collective-permute-start | bytes 786440 | tf_op jit(solution)/shard_map/ppermute | solution.py:239
  141.1 26.6 %collective-permute-start.28 = (f32[256,256]{1,0:T(8,128)S(1)}, f32[256,256]{1,0:T(8,128)S(1)}, u32[]{:S(2)}, u32[]{:S(2)}) collective-permute-start(f32[256,256]{1,0:T(8,128)S(1)} %get-tuple-element.89), channel_id=1, source_target_pairs={{0,12},{4,8},{8,4},{12,0},{16,28},{20,24},{24,20},{28,16},{1,13},{... | collective-permute-start | bytes 786440 | tf_op jit(solution)/shard_map/ppermute | solution.py:239
  146.3 19.2 %collective-permute-start.24 = (f32[256,256]{1,0:T(8,128)S(1)}, f32[256,256]{1,0:T(8,128)S(1)}, u32[]{:S(2)}, u32[]{:S(2)}) collective-permute-start(f32[256,256]{1,0:T(8,128)S(1)} %touch.24), channel_id=1, source_target_pairs={{0,24},{4,28},{8,16},{12,20},{16,8},{20,12},{24,0},{28,4},{1,25},{... | collective-permute-start | bytes 786440 | tf_op jit(solution)/shard_map/ppermute | solution.py:239
  152.5 30.5 %copy-start.5 = (f32[1,256,256]{2,1,0:T(8,128)S(1)}, f32[1,256,256]{2,1,0:T(8,128)}, u32[]{:S(2)}) copy-start(f32[1,256,256]{2,1,0:T(8,128)} %get-tuple-element.86.inner_ref) | copy-start | bytes 786436
  154.4 17.2 %collective-permute-start.22 = (f32[256,256]{1,0:T(8,128)S(1)}, f32[256,256]{1,0:T(8,128)S(1)}, u32[]{:S(2)}, u32[]{:S(2)}) collective-permute-start(f32[256,256]{1,0:T(8,128)S(1)} %get-tuple-element.80), channel_id=1, source_target_pairs={{0,4},{4,0},{8,12},{12,8},{16,20},{20,16},{24,28},{28,24},{1,5},{5... | collective-permute-start | bytes 786440 | tf_op jit(solution)/shard_map/ppermute | solution.py:239
  154.4 23.3 %collective-permute-start.23 = (f32[256,256]{1,0:T(8,128)S(1)}, f32[256,256]{1,0:T(8,128)S(1)}, u32[]{:S(2)}, u32[]{:S(2)}) collective-permute-start(f32[256,256]{1,0:T(8,128)S(1)} %get-tuple-element.81), channel_id=1, source_target_pairs={{0,8},{4,12},{8,0},{12,4},{16,24},{20,28},{24,16},{28,20},{1,9},{5... | collective-permute-start | bytes 786440 | tf_op jit(solution)/shard_map/ppermute | solution.py:239
  157.3 28.2 %collective-permute-start.26 = (f32[256,256]{1,0:T(8,128)S(1)}, f32[256,256]{1,0:T(8,128)S(1)}, u32[]{:S(2)}, u32[]{:S(2)}) collective-permute-start(f32[256,256]{1,0:T(8,128)S(1)} %touch.26), channel_id=1, source_target_pairs={{0,28},{4,24},{8,20},{12,16},{16,12},{20,8},{24,4},{28,0},{1,29},{... | collective-permute-start | bytes 786440 | tf_op jit(solution)/shard_map/ppermute | solution.py:239
  165.6 32.0 %collective-permute-start.21 = (f32[256,256]{1,0:T(8,128)S(1)}, f32[256,256]{1,0:T(8,128)S(1)}, u32[]{:S(2)}, u32[]{:S(2)}) collective-permute-start(f32[256,256]{1,0:T(8,128)S(1)} %touch.23), channel_id=1, source_target_pairs={{0,16},{4,20},{8,24},{12,28},{16,0},{20,4},{24,8},{28,12},{1,17},{... | collective-permute-start | bytes 786440 | tf_op jit(solution)/shard_map/ppermute | solution.py:239
  167.7 31.4 %collective-permute-start.32 = (f32[256,256]{1,0:T(8,128)S(1)}, f32[256,256]{1,0:T(8,128)S(1)}, u32[]{:S(2)}, u32[]{:S(2)}) collective-permute-start(f32[256,256]{1,0:T(8,128)S(1)} %get-tuple-element.97), channel_id=1, source_target_pairs={{0,12},{4,8},{8,4},{12,0},{16,28},{20,24},{24,20},{28,16},{1,13},{... | collective-permute-start | bytes 786440 | tf_op jit(solution)/shard_map/ppermute | solution.py:239
  171.6 37.3 %collective-permute-start.31 = (f32[256,256]{1,0:T(8,128)S(1)}, f32[256,256]{1,0:T(8,128)S(1)}, u32[]{:S(2)}, u32[]{:S(2)}) collective-permute-start(f32[256,256]{1,0:T(8,128)S(1)} %touch.29), channel_id=1, source_target_pairs={{0,20},{4,16},{8,28},{12,24},{16,4},{20,0},{24,12},{28,8},{1,21},{... | collective-permute-start | bytes 786440 | tf_op jit(solution)/shard_map/ppermute | solution.py:239
  185.6 30.6 %collective-permute-start.30 = (f32[256,256]{1,0:T(8,128)S(1)}, f32[256,256]{1,0:T(8,128)S(1)}, u32[]{:S(2)}, u32[]{:S(2)}) collective-permute-start(f32[256,256]{1,0:T(8,128)S(1)} %touch.28), channel_id=1, source_target_pairs={{0,24},{4,28},{8,16},{12,20},{16,8},{20,12},{24,0},{28,4},{1,25},{... | collective-permute-start | bytes 786440 | tf_op jit(solution)/shard_map/ppermute | solution.py:239
  197.7 23.4 %collective-permute-start.29 = (f32[256,256]{1,0:T(8,128)S(1)}, f32[256,256]{1,0:T(8,128)S(1)}, u32[]{:S(2)}, u32[]{:S(2)}) collective-permute-start(f32[256,256]{1,0:T(8,128)S(1)} %touch.27), channel_id=1, source_target_pairs={{0,28},{4,24},{8,20},{12,16},{16,12},{20,8},{24,4},{28,0},{1,29},{... | collective-permute-start | bytes 786440 | tf_op jit(solution)/shard_map/ppermute | solution.py:239
